TPU v7x, 32 devices: a whole 2x2x4 slice. The times are simulated.
32 devices in a mesh: fsdp: 4 (over y, x), context: 4 (over z), tensor: 2 (over core).
Axes of the slice: x: 2, y: 2, z: 4, core: 2. Of those that a mesh axis runs over, the one named last changes fastest.
Arguments:
- tokens: bfloat16 [4096, 1024], P(('fsdp', 'context')), may hold values from -6 to 6
- cotangent: bfloat16 [4096, 1024], P(('fsdp', 'context')), may hold values from -6 to 6
- ln1_gain: float32 [1024], replicated, may hold values from 0.25 to 1.75
- ln1_bias: float32 [1024], replicated, may hold values from -1.75 to 1.75
- ln2_gain: float32 [1024], replicated, may hold values from 0.25 to 1.75
- ln2_bias: float32 [1024], replicated, may hold values from -1.75 to 1.75
- w_qkv: bfloat16 [1024, 3, 1024], P('fsdp', None, 'tensor'), may hold values from -0.1875 to 0.1875
- b_qkv: float32 [3, 1024], P(None, 'tensor'), may hold values from -1.75 to 1.75
- w_out: bfloat16 [1024, 1024], P('fsdp', 'tensor'), may hold values from -3 to 3
- b_out: float32 [1024], replicated, may hold values from -1.75 to 1.75
- w_up: bfloat16 [1024, 4096], P('fsdp', 'tensor'), may hold values from -0.1875 to 0.1875
- b_up: float32 [4096], P('tensor'), may hold values from -1.75 to 1.75
- w_down: bfloat16 [1024, 4096], P('fsdp', 'tensor'), may hold values from -0.09375 to 0.09375
- b_down: float32 [1024], replicated, may hold values from -1.75 to 1.75
Outputs:
- output: bfloat16 [4096, 1024], P(('fsdp', 'context'))
- d_tokens: float32 [4096, 1024], P(('fsdp', 'context'))
- d_ln1_gain: float32 [1024], P(('fsdp', 'context'))
- d_ln1_bias: float32 [1024], P(('fsdp', 'context'))
- d_ln2_gain: float32 [1024], P(('fsdp', 'context'))
- d_ln2_bias: float32 [1024], P(('fsdp', 'context'))
- d_w_qkv: float32 [1024, 3, 1024], P(('fsdp', 'context'), None, 'tensor')
- d_b_qkv: float32 [3, 1024], P(None, 'tensor')
- d_w_out: float32 [1024, 1024], P(('fsdp', 'context'), 'tensor')
- d_b_out: float32 [1024], P(('fsdp', 'context'))
- d_w_up: float32 [1024, 4096], P(('fsdp', 'context'), 'tensor')
- d_b_up: float32 [4096], P('tensor')
- d_w_down: float32 [1024, 4096], P(('fsdp', 'context'), 'tensor')
- d_b_down: float32 [1024], P(('fsdp', 'context'))
All inputs are finite; a program needn't handle non-finite values.
Results may differ from a plain program's by a relative error of at most 0.014.
Values may be sent and summed in bfloat16 or wider, within the bound.
No kernel may reach another device: no remote copies, remote signals or barrier semaphores. Data moves between devices by JAX's collectives and lax.ppermute only.
A program may use at most 128 MiB of HBM per device.

v0:
```python
import math

import jax
import jax.numpy as jnp
from jax import lax
from jax.sharding import PartitionSpec as P

HEAD = 64
ROT = 16


EPSILON = 1e-05
NEGATIVE = -1e30


def layer_norm(values, gain, shift):
    center = values - jnp.mean(values, axis=-1, keepdims=True)
    spread = jnp.mean(center * center, axis=-1, keepdims=True)
    return center * lax.rsqrt(spread + EPSILON) * gain + shift


def rotary_tables(positions, rot):
    half = rot // 2
    inverse = 1.0 / 10000.0 ** (jnp.arange(half, dtype=jnp.float32) * 2.0 / rot)
    angles = positions.astype(jnp.float32)[:, None] * inverse[None, :]
    return (jnp.cos(angles), jnp.sin(angles))


def rotate(values, cosine, sine):
    half = cosine.shape[-1]
    first = values[..., :half]
    second = values[..., half : 2 * half]
    cos_b = cosine[:, None, :]
    sin_b = sine[:, None, :]
    return jnp.concatenate(
        [first * cos_b - second * sin_b, second * cos_b + first * sin_b, values[..., 2 * half :]],
        axis=-1,
    )


def gelu_exact(values):
    return jax.nn.gelu(values, approximate=False)


def on_device(
    tokens,
    cotangent,
    ln1_gain,
    ln1_bias,
    ln2_gain,
    ln2_bias,
    w_qkv,
    b_qkv,
    w_out,
    b_out,
    w_up,
    b_up,
    w_down,
    b_down,
):
    rows = tokens.shape[0]
    width = w_qkv.shape[2]
    local_heads = width // HEAD
    scale = 1.0 / math.sqrt(HEAD)
    seq_len = rows * lax.axis_size("context")
    whole = tokens.astype(jnp.float32)
    low_one = layer_norm(whole, ln1_gain, ln1_bias).astype(jnp.bfloat16)
    low_two = layer_norm(whole, ln2_gain, ln2_bias).astype(jnp.bfloat16)
    full_qkv, full_out, full_up, full_down = (
        lax.all_gather(w_qkv, "fsdp", axis=0, tiled=True),
        lax.all_gather(w_out, "fsdp", axis=0, tiled=True),
        lax.all_gather(w_up, "fsdp", axis=0, tiled=True),
        lax.all_gather(w_down, "fsdp", axis=0, tiled=True),
    )
    projected = (
        jnp.einsum("td,dke->tke", low_one, full_qkv, preferred_element_type=jnp.float32)
        + b_qkv[None]
    )
    positions = lax.axis_index("context") * rows + jnp.arange(rows, dtype=jnp.int32)
    last_query = positions[-1]
    cosine, sine = rotary_tables(positions, ROT)
    shaped = projected.reshape(rows, 3, local_heads, HEAD)
    query = rotate(shaped[:, 0], cosine, sine).astype(jnp.bfloat16)
    key = rotate(shaped[:, 1], cosine, sine).astype(jnp.bfloat16)
    value = shaped[:, 2].astype(jnp.bfloat16)
    pairs = jnp.stack([key.reshape(rows, width), value.reshape(rows, width)], axis=1)
    start_state = (
        jnp.full((local_heads, rows), NEGATIVE, jnp.float32),
        jnp.zeros((local_heads, rows), jnp.float32),
        jnp.zeros((local_heads, rows, HEAD), jnp.float32),
    )
    piece = lax.all_gather(pairs, "context", axis=0, tiled=True)
    size = piece.shape[0]
    block = math.gcd(size, math.lcm(512, rows))
    blocks = piece.reshape(size // block, block, 2, local_heads, HEAD)

    def forward_step(state, item):
        index, group = item
        first = index * block

        def forward_compute(inner):
            top, total, accum = inner
            key_pos = first + jnp.arange(block, dtype=jnp.int32)
            scores = (
                jnp.einsum("thd,rhd->htr", query, group[:, 0], preferred_element_type=jnp.float32)
                * scale
            )
            visible = key_pos[None, None, :] <= positions[None, :, None]
            scores = jnp.where(visible, scores, NEGATIVE)
            new_top = jnp.maximum(top, jnp.max(scores, axis=-1))
            weights = jnp.where(visible, jnp.exp(scores - new_top[..., None]), 0.0)
            factor = jnp.exp(top - new_top)
            total = total * factor + jnp.sum(weights, axis=-1)
            accum = accum * factor[..., None] + jnp.einsum(
                "htr,rhd->htd",
                weights.astype(jnp.bfloat16),
                group[:, 1],
                preferred_element_type=jnp.float32,
            )
            return (new_top, total, accum)

        return (lax.cond(first > last_query, lambda inner: inner, forward_compute, state), None)

    result, _ = lax.scan(
        forward_step, start_state, (jnp.arange(blocks.shape[0], dtype=jnp.int32), blocks)
    )
    top, total, accum = result
    attended = accum / total[..., None]
    log_total = top + jnp.log(total)
    mixed_low = attended.transpose(1, 0, 2).reshape(rows, width).astype(jnp.bfloat16)
    up_pre = jnp.dot(low_two, full_up, preferred_element_type=jnp.float32) + b_up
    active_low = gelu_exact(up_pre).astype(jnp.bfloat16)
    partial_sum = jnp.einsum(
        "te,de->td", mixed_low, full_out, preferred_element_type=jnp.float32
    ) + jnp.einsum("tf,df->td", active_low, full_down, preferred_element_type=jnp.float32)
    branches = lax.psum(partial_sum.astype(jnp.bfloat16), "tensor").astype(jnp.float32)
    result = (whole + branches + b_out + b_down).astype(jnp.bfloat16)
    grad_bias = jnp.sum(cotangent.astype(jnp.float32), axis=0)
    grad_w_out = jnp.einsum("td,te->de", cotangent, mixed_low, preferred_element_type=jnp.float32)
    grad_w_down = jnp.einsum("td,tf->df", cotangent, active_low, preferred_element_type=jnp.float32)
    grad_mixed = jnp.dot(cotangent, full_out, preferred_element_type=jnp.float32).astype(
        jnp.bfloat16
    )
    grad_active = jnp.dot(cotangent, full_down, preferred_element_type=jnp.float32)
    _, gelu_pull = jax.vjp(gelu_exact, up_pre)
    grad_up = gelu_pull(grad_active)[0].astype(jnp.bfloat16)
    grad_w_up = jnp.einsum("td,tf->df", low_two, grad_up, preferred_element_type=jnp.float32)
    grad_b_up = jnp.sum(grad_up.astype(jnp.float32), axis=0)
    grad_two = jnp.einsum("tf,df->td", grad_up, full_up, preferred_element_type=jnp.float32)
    grad_heads = grad_mixed.reshape(rows, local_heads, HEAD)
    delta = jnp.sum(grad_heads.astype(jnp.float32).transpose(1, 0, 2) * attended, axis=-1)
    query_start = jnp.zeros((local_heads, rows, HEAD), jnp.float32)
    back_state = (query_start, jnp.zeros((seq_len, 2, width), jnp.float32))
    piece = lax.all_gather(pairs, "context", axis=0, tiled=True)
    size = piece.shape[0]
    backward_block = math.gcd(size, math.lcm(512, rows))
    blocks = piece.reshape(size // backward_block, backward_block, 2, local_heads, HEAD)

    def backward_step(state, item):
        index, group = item
        first = index * backward_block

        def backward_compute(inner):
            grad_query = inner[0]
            key_pos = first + jnp.arange(backward_block, dtype=jnp.int32)
            scores = (
                jnp.einsum("thd,rhd->htr", query, group[:, 0], preferred_element_type=jnp.float32)
                * scale
            )
            visible = key_pos[None, None, :] <= positions[None, :, None]
            probs = jnp.where(visible, jnp.exp(scores - log_total[..., None]), 0.0)
            grad_probs = jnp.einsum(
                "thd,rhd->htr", grad_heads, group[:, 1], preferred_element_type=jnp.float32
            )
            grad_scores = (probs * (grad_probs - delta[..., None])).astype(jnp.bfloat16)
            grad_query = (
                grad_query
                + jnp.einsum(
                    "htr,rhd->htd", grad_scores, group[:, 0], preferred_element_type=jnp.float32
                )
                * scale
            )
            grad_value = jnp.einsum(
                "htr,thd->rhd",
                probs.astype(jnp.bfloat16),
                grad_heads,
                preferred_element_type=jnp.float32,
            )
            grad_key = (
                jnp.einsum("htr,thd->rhd", grad_scores, query, preferred_element_type=jnp.float32)
                * scale
            )
            update = jnp.stack(
                [
                    grad_key.reshape(backward_block, width),
                    grad_value.reshape(backward_block, width),
                ],
                axis=1,
            )
            return (grad_query, lax.dynamic_update_slice_in_dim(inner[1], update, first, 0))

        return (lax.cond(first > last_query, lambda inner: inner, backward_compute, state), None)

    result_state, _ = lax.scan(
        backward_step, back_state, (jnp.arange(blocks.shape[0], dtype=jnp.int32), blocks)
    )
    grad_query = result_state[0]
    grad_pairs = lax.psum_scatter(
        result_state[1].astype(jnp.bfloat16), "context", scatter_dimension=0, tiled=True
    ).astype(jnp.float32)
    _, turn_pull = jax.vjp(lambda values: rotate(values, cosine, sine), shaped[:, 0])
    grad_q_pre = turn_pull(grad_query.transpose(1, 0, 2))[0]
    grad_k_pre = turn_pull(grad_pairs[:, 0].reshape(rows, local_heads, HEAD))[0]
    grad_v_pre = grad_pairs[:, 1].reshape(rows, local_heads, HEAD)
    grad_proj = (
        jnp.stack([grad_q_pre, grad_k_pre, grad_v_pre], axis=1)
        .reshape(rows, 3, width)
        .astype(jnp.bfloat16)
    )
    grad_w_qkv = jnp.einsum("td,tke->dke", low_one, grad_proj, preferred_element_type=jnp.float32)
    grad_b_qkv = jnp.sum(grad_proj.astype(jnp.float32), axis=0)
    grad_one = jnp.einsum("tke,dke->td", grad_proj, full_qkv, preferred_element_type=jnp.float32)
    grad_one, grad_two = (
        lax.psum(grad_one.astype(jnp.bfloat16), "tensor").astype(jnp.float32),
        lax.psum(grad_two.astype(jnp.bfloat16), "tensor").astype(jnp.float32),
    )
    _, norm_pull_one = jax.vjp(layer_norm, whole, ln1_gain, ln1_bias)
    input_one, gain_one, shift_one = norm_pull_one(grad_one)
    _, norm_pull_two = jax.vjp(layer_norm, whole, ln2_gain, ln2_bias)
    input_two, gain_two, shift_two = norm_pull_two(grad_two)
    grad_tokens = cotangent.astype(jnp.float32) + input_one + input_two
    sum_qkv, sum_out, sum_up, sum_down, sum_g1, sum_c1, sum_g2, sum_c2, sum_bias = (
        lax.psum_scatter(grad_w_qkv, ("fsdp", "context"), scatter_dimension=0, tiled=True),
        lax.psum_scatter(grad_w_out, ("fsdp", "context"), scatter_dimension=0, tiled=True),
        lax.psum_scatter(grad_w_up, ("fsdp", "context"), scatter_dimension=0, tiled=True),
        lax.psum_scatter(grad_w_down, ("fsdp", "context"), scatter_dimension=0, tiled=True),
        lax.psum_scatter(gain_one, ("fsdp", "context"), scatter_dimension=0, tiled=True),
        lax.psum_scatter(shift_one, ("fsdp", "context"), scatter_dimension=0, tiled=True),
        lax.psum_scatter(gain_two, ("fsdp", "context"), scatter_dimension=0, tiled=True),
        lax.psum_scatter(shift_two, ("fsdp", "context"), scatter_dimension=0, tiled=True),
        lax.psum_scatter(grad_bias, ("fsdp", "context"), scatter_dimension=0, tiled=True),
    )
    bias_qkv, bias_up = lax.psum((grad_b_qkv, grad_b_up), ("fsdp", "context"))
    return (
        result,
        grad_tokens,
        sum_g1,
        sum_c1,
        sum_g2,
        sum_c2,
        sum_qkv,
        bias_qkv,
        sum_out,
        sum_bias,
        sum_up,
        bias_up,
        sum_down,
        sum_bias,
    )


def solution(mesh):
    in_specs = (
        P(("fsdp", "context"), None),
        P(("fsdp", "context"), None),
        P(),
        P(),
        P(),
        P(),
        P("fsdp", None, "tensor"),
        P(None, "tensor"),
        P("fsdp", "tensor"),
        P(),
        P("fsdp", "tensor"),
        P("tensor"),
        P("fsdp", "tensor"),
        P(),
    )
    out_specs = (
        P(("fsdp", "context"), None),
        P(("fsdp", "context"), None),
        P(("fsdp", "context")),
        P(("fsdp", "context")),
        P(("fsdp", "context")),
        P(("fsdp", "context")),
        P(("fsdp", "context"), None, "tensor"),
        P(None, "tensor"),
        P(("fsdp", "context"), "tensor"),
        P(("fsdp", "context")),
        P(("fsdp", "context"), "tensor"),
        P("tensor"),
        P(("fsdp", "context"), "tensor"),
        P(("fsdp", "context")),
    )
    return jax.shard_map(
        on_device, mesh=mesh, in_specs=in_specs, out_specs=out_specs, check_vma=False
    )
```

profile of v0, /device:TPU:0, one launch (start us, length us, event | category | flops | bytes accessed | tf_op | source)
XLA Modules:
  0.0 911.1 jit_solution(10422092635005952227)
XLA Ops:
  8.8 1.2 convert_reduce_fusion.4
  10.0 1.3 fusion.52
  11.4 45.2 %all-gather.6.cloned.1.call-done = bf16[1024,3,512]{2,0,1:T(8,128)(2,1)} async-done(((bf16[256,3,512]{2,0,1:T(8,128)(2,1)}), bf16[1024,3,512]{2,0,1:T(8,128)(2,1)}) %all-gather.6.cloned.1.call-update) | async-done | bytes 3145744 | tf_op jit(solution)/shard_map/all_gather | solution.py:70
  56.6 3.0 convolution_add_fusion.1
  63.0 22.1 %all-gather.10.cloned.1.call-done = bf16[1024,512]{1,0:T(8,128)(2,1)} async-done(((bf16[256,512]{1,0:T(8,128)(2,1)}), bf16[1024,512]{1,0:T(8,128)(2,1)}) %all-gather.10.cloned.1.call-update) | async-done | bytes 1048592 | tf_op jit(solution)/shard_map/all_gather | solution.py:71
  85.1 1.7 convolution_convert_fusion.1
  87.7 45.9 %all-gather.8.cloned.1.call-done = bf16[1024,2,512]{0,2,1:T(8,128)(2,1)} async-done(((bf16[256,2,512]{0,2,1:T(8,128)(2,1)}), bf16[1024,2,512]{0,2,1:T(8,128)(2,1)}) %all-gather.8.cloned.1.call-update) | async-done | bytes 2097168 | tf_op jit(solution)/shard_map/all_gather | solution.py:92
  133.5 3.3 reshape.273
  136.8 1.9 copy.66
  138.8 8.7 while.28
  140.7 4.8 conditional.6
  140.9 1.4 dynamic-slice_bitcast_fusion
  144.2 1.3 fusion.10
  147.5 1.7 fusion.63
  149.2 1.6 broadcast_in_dim.57
  151.7 25.0 %while.29 = (s32[]{:T(128)}, f32[8,256,64]{1,2,0:T(8,128)}, bf16[1024,2,512]{0,2,1:T(8,128)(2,1)}, s32[2]{0:T(128)S(1)}, s32[]{:T(128)}, /*index=5*/bf16[2,512,2...) while((s32[]{:T(128)}, f32[8,256,64]{1,2,0:T(8,128)}, ...), condition=%wide.region_13.14_spmd.clone, body=%wide.region_10.13_spmd.clone.sunk | while | flops 683016960 | bytes 30310740 | solution.py:204
  153.5 21.2 %conditional.7 = ((f32[8,256,64]{1,2,0:T(8,128)}, bf16[1024,2,512]{0,2,1:T(8,128)(2,1)})) conditional(s32[]{:T(128)} %convert_element_type.271, (s32[]{:T(128)}, s32[]{:T(128)}, bf16[2,512,2,8,64]{1,4,3,2,0:T(8,128)(2,1)}, s32[]{:T(128)}, bf16[256,8,64]{0,2,1:T(8,128)(2,1)S(1)}, /*index=5*/f32[8,256]{1,0:T(8,128)S(1)}, ...), branch_computations={%region_11.11_spmd, %region_12.12_spmd} | conditional | flops 683016960 | bytes 30309448 | solution.py:202
  153.6 1.3 dynamic-slice_bitcast_fusion.1
  155.8 2.4 fusion.17
  159.0 1.9 fusion.19
  162.0 10.5 %dynamic_update_slice.3 = bf16[1024,2,512]{0,2,1:T(8,128)(2,1)} dynamic-update-slice(bf16[1024,2,512]{0,2,1:T(8,128)(2,1)} %get-tuple-element.198, bf16[512,2,512]{0,2,1:T(8,128)(2,1)} %pad_maximum_fusion, s32[]{:T(128)S(6)} %select_n.16, s32[]{:T(128)} %constant.61.clone, s32[]{:T(128)} %constant.61.clone) | dynamic-update-slice | bytes 2097156 | tf_op jit(solution)/shard_map/while/body/eval_jaxpr/cond/branch_0_fun/dynamic_update_slice | solution.py:200
  172.4 2.3 fusion.25
  176.6 4.0 copy.69
  180.9 5.3 all-gather.12.cloned.1.call-done
  186.2 3.6 convolution_add_fusion
  189.8 50.9 %all-gather.14.cloned.1.call-done = bf16[1024,2048]{1,0:T(8,128)(2,1)} async-done(((bf16[256,2048]{1,0:T(8,128)(2,1)}), bf16[1024,2048]{1,0:T(8,128)(2,1)}) %all-gather.14.cloned.1.call-update) | async-done | bytes 4194320 | tf_op jit(solution)/shard_map/all_gather | solution.py:73
  240.6 7.4 convert_reduce_fusion
  248.4 2.3 copy-done.26
  250.7 1.3 fusion.74
  252.0 1.3 copy-done.25
  253.3 2.1 convolution_convert_fusion
  255.5 1.3 fusion.44
  256.8 29.9 %reduce-scatter.10.cloned.1.call-done = bf16[256,2,512]{2,0,1:T(8,128)(2,1)} async-done(((bf16[1024,2,512]{2,0,1:T(8,128)(2,1)}), bf16[256,2,512]{2,0,1:T(8,128)(2,1)}) %reduce-scatter.10.cloned.1.call-update) | async-done | bytes 524304 | tf_op jit(solution)/shard_map/reduce_scatter | solution.py:208
  288.4 3.8 fusion.43
  292.4 1.4 convolution_bitcast_fusion.1
  293.7 1.9 copy.82
  296.9 4.5 convolution_bitcast_fusion
  301.4 9.4 %copy.84 = f32[1024,2048]{1,0:T(8,128)} copy(f32[1024,2048]{0,1:T(8,128)} %convolution_bitcast_fusion) | data formatting | bytes 16777216
  310.9 1.2 copy-done.17
  312.1 4.7 fusion.70
  317.8 3.8 fusion.65
  323.7 1.9 fusion.53
  325.6 2.3 fusion.59
  327.9 2.0 convert_reduce_fusion.5
  329.9 76.2 %all-reduce.11 = (f32[1024]{0:T(1024)S(1)}, f32[1024]{0:T(1024)S(1)}, f32[1024]{0:T(1024)S(1)}, f32[1024]{0:T(1024)S(1)}, f32[3,512]{1,0:T(4,128)}, /*index=5*/f32[1024]{0:T(1024)S(1)}, f32[2048]{0:T(1024)}) all-reduce(f32[1024]{0:T(1024)S(1)} %get-tuple-element.392, ...), channel_id=3, replica_groups=mesh['fsdp'=4,'context'=4,'tensor'=2] {'fsdp','context'}, use_global_device_ids=true, to_apply=%region_22.23.clone | all-reduce | flops 8704 | bytes 69632
  408.5 174.3 %reduce-scatter.18.cloned.1.call-done = f32[64,2048]{1,0:T(8,128)} async-done(((f32[1024,2048]{1,0:T(8,128)}), f32[64,2048]{1,0:T(8,128)}) %reduce-scatter.18.cloned.1.call-update) | async-done | bytes 524304
  582.8 182.6 %reduce-scatter.14.cloned.1.call-done = f32[64,2048]{1,0:T(8,128)} async-done(((f32[1024,2048]{1,0:T(8,128)}), f32[64,2048]{1,0:T(8,128)}) %reduce-scatter.14.cloned.1.call-update) | async-done | bytes 524304 | tf_op jit(solution)/shard_map/reduce_scatter | solution.py:235
  765.4 138.7 %reduce-scatter.12.cloned.1.call-done = f32[64,3,512]{2,0,1:T(8,128)} async-done(((f32[1024,3,512]{2,0,1:T(8,128)}), f32[64,3,512]{2,0,1:T(8,128)}) %reduce-scatter.12.cloned.1.call-update) | async-done | bytes 393232 | tf_op jit(solution)/shard_map/reduce_scatter | solution.py:233
  (154 shorter events, 22.9 us)
Async XLA Ops:
  7.2 49.4 %copy-start.1 = (bf16[256,1024]{1,0:T(8,128)(2,1)S(1)}, bf16[256,1024]{1,0:T(8,128)(2,1)}, u32[]{:S(2)}) copy-start(bf16[256,1024]{1,0:T(8,128)(2,1)} %param.22) | copy-start | bytes 1572868
  7.2 49.4 %copy-start.21 = (f32[1024]{0:T(1024)S(1)}, f32[1024]{0:T(1024)}, u32[]{:S(2)}) copy-start(f32[1024]{0:T(1024)} %param.24) | copy-start | bytes 12292
  7.2 49.4 %copy-start.22 = (f32[1024]{0:T(1024)S(1)}, f32[1024]{0:T(1024)}, u32[]{:S(2)}) copy-start(f32[1024]{0:T(1024)} %param.25) | copy-start | bytes 12292
  7.2 49.4 %copy-start.27 = (f32[3,512]{1,0:T(4,128)S(1)}, f32[3,512]{1,0:T(4,128)}, u32[]{:S(2)}) copy-start(f32[3,512]{1,0:T(4,128)} %param.29) | copy-start | bytes 18436
  7.2 49.4 %all-gather.6.cloned.1.call-start = ((), (), s32[]{:S(2)}) async-start(), calls=%async_computation.5 | async-start | bytes 3932160 | tf_op jit(solution)/shard_map/all_gather | solution.py:70
  8.0 77.2 %all-gather.10.cloned.1.call-start = ((), (), s32[]{:S(2)}) async-start(), calls=%async_computation.7 | async-start | bytes 1310720 | tf_op jit(solution)/shard_map/all_gather | solution.py:71
  8.7 124.8 %all-gather.8.cloned.1.call-start = ((), (), s32[]{:S(2)}) async-start(), calls=%async_computation.6 | async-start | bytes 2621440 | tf_op jit(solution)/shard_map/all_gather | solution.py:92
  60.3 24.8 %copy-start.3 = (bf16[256,1024]{1,0:T(8,128)(2,1)S(1)}, bf16[256,1024]{1,0:T(8,128)(2,1)}, u32[]{:S(2)}) copy-start(bf16[256,1024]{1,0:T(8,128)(2,1)} %param.23) | copy-start | bytes 1572868
  61.2 125.0 %all-gather.12.cloned.1.call-start = ((), (), s32[]{:S(2)}) async-start(), calls=%async_computation.8 | async-start | bytes 5242880 | tf_op jit(solution)/shard_map/all_gather | solution.py:72
  61.8 178.8 %all-gather.14.cloned.1.call-start = ((), (), s32[]{:S(2)}) async-start(), calls=%async_computation.9 | async-start | bytes 5242880 | tf_op jit(solution)/shard_map/all_gather | solution.py:73
  62.4 224.3 %reduce-scatter.10.cloned.1.call-start = ((), (), s32[]{:S(2)}) async-start(), calls=%async_computation.10 | async-start | bytes 2621440 | tf_op jit(solution)/shard_map/reduce_scatter | solution.py:208
  180.6 5.6 copy-start.2
  180.6 5.6 copy-start.19
  180.6 5.6 copy-start.20
  180.6 5.6 copy-start.28
  180.6 60.0 %copy-start.4 = (bf16[256,1024]{1,0:T(8,128)(2,1)S(1)}, bf16[256,1024]{1,0:T(8,128)(2,1)}, u32[]{:S(2)}) copy-start(bf16[256,1024]{1,0:T(8,128)(2,1)} %param.23) | copy-start | bytes 1572868
  180.7 143.0 %all-reduce.15.cloned.1.call-start = ((), (), s32[]{:S(2)}) async-start(), calls=%async_computation.15 | async-start | bytes 3145728 | tf_op jit(solution)/shard_map/psum | solution.py:136
  248.0 4.0 copy-start.16
  248.0 2.7 copy-start.26
  250.7 1.3 copy-start.6
  250.7 2.6 copy-start.25
  253.3 2.2 copy-start
  253.3 2.2 copy-start.10
  253.3 2.2 copy-start.15
  288.2 4.0 copy-start.11
  288.4 3.9 copy-start.13
  288.4 3.9 copy-start.5
  292.3 116.2 %reduce-scatter.16.cloned.1.call-start = ((), (), s32[]{:S(2)}) async-start(), calls=%async_computation.13 | async-start | bytes 2228224
  295.6 1.2 copy-start.7
  295.7 287.1 %reduce-scatter.18.cloned.1.call-start = ((), (), s32[]{:S(2)}) async-start(), calls=%async_computation.14 | async-start | bytes 8912896
  310.8 1.3 copy-start.17
  310.8 454.6 %reduce-scatter.14.cloned.1.call-start = ((), (), s32[]{:S(2)}) async-start(), calls=%async_computation.12 | async-start | bytes 8912896 | tf_op jit(solution)/shard_map/reduce_scatter | solution.py:235
  316.7 0.9 copy-start.12
  316.7 1.0 copy-start.14
  316.8 587.3 %reduce-scatter.12.cloned.1.call-start = ((), (), s32[]{:S(2)}) async-start(), calls=%async_computation.11 | async-start | bytes 6684672 | tf_op jit(solution)/shard_map/reduce_scatter | solution.py:233
  321.6 0.7 copy-start.29
  321.6 6.3 copy-start.23
  321.6 6.3 copy-start.24
  323.6 4.3 copy-start.8
  323.7 4.3 copy-start.9
  323.7 4.3 copy-start.18
  406.2 498.4 %copy-start.30 = (f32[64]{0:T(128)}, f32[64]{0:T(128)S(1)}, u32[]{:S(2)}) copy-start(f32[64]{0:T(128)S(1)} %dynamic-slice.9) | copy-start | bytes 772
Sparse Core Ops, SparseCore 0:
  9.9 46.6 all-gather.5
  58.5 26.6 all-gather.9
  87.3 46.2 all-gather.7
  135.2 50.9 all-gather.11
  187.9 52.6 all-gather.13
  242.8 43.8 reduce-scatter.9
  292.4 19.8 all-reduce.14
  315.2 85.9 reduce-scatter.15
  404.0 178.7 reduce-scatter.17
  585.5 179.8 reduce-scatter.13
  768.3 135.7 reduce-scatter.11
where the time goes:
time: 913 us; the launch traced here: 911 us
  waiting for transfers between devices  697 us (76%)
  blocking collectives  76.2 us (8%)
  local copies, waits for them, and re-layouts  51.9 us (6%)
  matrix products  48.7 us (5%)
  other arithmetic  15.5 us (2%)
  between operations  15.1 us (2%)
    reduce_scatter x1, waiting for transfers between devices, on_device(): lax.psum_scatter(grad_w_up, ('fsdp', 'context'), scatter_dimension=0, til...  183 us
    unnamed x13, waiting for transfers between devices  177 us
    reduce_scatter x1, waiting for transfers between devices, on_device(): lax.psum_scatter(grad_w_qkv, ('fsdp', 'context'), scatter_dimension=0, ti...  139 us
    unnamed x1, blocking collectives  76.2 us
    all_gather x1, waiting for transfers between devices, on_device(): lax.all_gather(w_down, 'fsdp', axis=0, tiled=True)  50.9 us
    all_gather x1, waiting for transfers between devices, on_device(): piece = lax.all_gather(pairs, 'context', axis=0, tiled=True)  45.9 us
    all_gather x1, waiting for transfers between devices, on_device(): lax.all_gather(w_qkv, 'fsdp', axis=0, tiled=True)  45.2 us
    reduce_scatter x1, waiting for transfers between devices, on_device(): lax.psum_scatter(result_state[1].astype(jnp.bfloat16), 'context', scatter...  29.9 us
  transfers between devices with their start and end apart: 11, of which 9 were waited for; matrix products, arithmetic and copies ran while one was open for 11% of the time, Pallas kernels for 0%

commit v1 on v0

--- a/solution.py
+++ b/solution.py
@@ -3,6 +3,8 @@
 import jax
 import jax.numpy as jnp
 from jax import lax
+from jax.experimental import pallas as pl
+from jax.experimental.pallas import tpu as pltpu
 from jax.sharding import PartitionSpec as P
 
 HEAD = 64
@@ -42,7 +44,7 @@
     return jax.nn.gelu(values, approximate=False)
 
 
-def on_device(
+def gathered_weights(
     tokens,
     cotangent,
     ln1_gain,
@@ -259,6 +261,585 @@
     )
 
 
+VMEM_BYTES = 60 * 1024 * 1024
+
+
+def send(values, axis, step):
+    size = lax.axis_size(axis)
+    return lax.ppermute(values, axis, [(index, index ^ step) for index in range(size)])
+
+
+def take(values, start, size, axis=0):
+    return lax.dynamic_slice_in_dim(values, start, size, axis)
+
+
+def both_halves(values):
+    core = lax.axis_index("tensor")
+    other = send(values, "tensor", 1)
+    return jnp.concatenate(
+        [jnp.where(core == 0, values, other), jnp.where(core == 0, other, values)], axis=0
+    )
+
+
+def call(body, outs, place, *arrays, scratch=()):
+    return pl.pallas_call(
+        body,
+        out_shape=[jax.ShapeDtypeStruct(shape, kind) for shape, kind in outs],
+        in_specs=[pl.BlockSpec(memory_space=pltpu.SMEM)]
+        + [pl.BlockSpec(memory_space=pltpu.VMEM)] * len(arrays),
+        out_specs=[pl.BlockSpec(memory_space=pltpu.VMEM)] * len(outs),
+        scratch_shapes=[pltpu.VMEM(shape, kind) for shape, kind in scratch],
+        compiler_params=pltpu.CompilerParams(vmem_limit_bytes=VMEM_BYTES),
+    )(place, *arrays)
+
+
+def span(index, size, offset=0):
+    return pl.ds(pl.multiple_of(index * size + offset, size), size)
+
+
+def dot(first, second, contract=(1, 0)):
+    return lax.dot_general(
+        first, second, ((contract[:1], contract[1:]), ((), ())), preferred_element_type=jnp.float32
+    )
+
+
+def high_low(values):
+    high = values.astype(jnp.bfloat16)
+    return high, (values - high.astype(jnp.float32)).astype(jnp.bfloat16)
+
+
+def small_rows(lines, width):
+    rows = []
+    for line in lines:
+        rest = width - line.shape[1]
+        if rest:
+            line = jnp.concatenate([line, jnp.zeros((1, rest), jnp.float32)], axis=1)
+        rows.extend(high_low(line))
+    rows.append(jnp.zeros((16 - len(rows), width), jnp.bfloat16))
+    return jnp.concatenate([row.astype(jnp.float32) for row in rows], axis=0).astype(jnp.bfloat16)
+
+
+def turn(values, table, sign):
+    wide = values.shape[1]
+    half = ROT // 2
+    ahead = pltpu.roll(values, wide - half, 1)
+    behind = pltpu.roll(values, half, 1)
+    return values * table[0] + sign * (ahead * table[1] + behind * table[2])
+
+
+def turn_tables(seq_len, width):
+    cosine, sine = rotary_tables(jnp.arange(seq_len, dtype=jnp.int32), ROT)
+    rest = jnp.zeros((seq_len, HEAD - ROT), jnp.float32)
+    none = jnp.zeros_like(sine)
+    one = jnp.concatenate([cosine, cosine, rest + 1.0], axis=1)
+    ahead = jnp.concatenate([-sine, none, rest], axis=1)
+    behind = jnp.concatenate([none, sine, rest], axis=1)
+    heads = width // HEAD
+    return jnp.stack([jnp.tile(part, (1, heads)) for part in (one, ahead, behind)])
+
+
+def pack_kernel(place, tokens, cotangent, qkv, out, up, down, half_tokens, half_grad, first, second):
+    here, core = place[1], place[2]
+    rows = half_tokens.shape[0]
+    half_tokens[...] = tokens[span(core, rows), :]
+    half_grad[...] = cotangent[span(core, rows), :]
+    width = (first.shape[1] - second.shape[1]) // 2
+    units = second.shape[1] - width
+    for part in range(3):
+        first[:, part * width : (part + 1) * width] = qkv[:, part, span(here, width)]
+    first[:, 3 * width :] = up[:, span(here, units)]
+    second[:, :width] = out[:, span(here, width)]
+    second[:, width:] = down[:, span(here, units)]
+
+
+def assemble_rows(place, whole, own, got, other):
+    here, core = place[1], place[2]
+    rows, half = own.shape[0], own.shape[0] // 2
+    whole[span(here, rows), :] = own[...]
+    for step in range(1, len(got) + 1):
+        start = (here ^ step) * rows
+        whole[pl.ds(pl.multiple_of(start + core * half, half), half), :] = got[step - 1][...]
+        whole[pl.ds(pl.multiple_of(start + (1 - core) * half, half), half), :] = other[step - 1][...]
+
+
+def assemble_width(place, whole, parts):
+    rows = parts[0].shape[0]
+    for step, part in enumerate(parts):
+        whole[span(place[0] ^ step, rows), :] = part[...]
+
+
+def head_mask(width, head):
+    lane = lax.broadcasted_iota(jnp.int32, (1, width), 1)
+    return (lane >= head * HEAD) & (lane < (head + 1) * HEAD)
+
+
+def only_head(values, head):
+    return jnp.where(head_mask(values.shape[1], head), values, jnp.zeros_like(values))
+
+
+def causal(block, keys):
+    row = lax.broadcasted_iota(jnp.int32, (block, keys), 0) + (keys - block)
+    return lax.broadcasted_iota(jnp.int32, (block, keys), 1) <= row
+
+
+def forward_kernel(members, quarters, place, *refs):
+    own, refs = refs[0], refs[1:]
+    got, refs = refs[: members - 1], refs[members - 1 :]
+    other, refs = refs[: members - 1], refs[members - 1 :]
+    parts, refs = refs[:quarters], refs[quarters:]
+    gain_one, shift_one, gain_two, shift_two, bias_qkv, bias_up, table = refs[:7]
+    hat, qkv, mixed, log_total, joined, slope, weights, seq = refs[7:]
+    assemble_rows(place, seq, own, got, other)
+    assemble_width(place, weights, parts)
+    seq_len = seq.shape[0]
+    width = mixed.shape[1]
+    block = own.shape[0]
+    for start in range(0, seq_len, block):
+        rows = slice(start, start + block)
+        values = seq[rows, :].astype(jnp.float32)
+        center = values - jnp.mean(values, axis=-1, keepdims=True)
+        spread = jnp.mean(center * center, axis=-1, keepdims=True)
+        normed = center * lax.rsqrt(spread + EPSILON)
+        hat[rows, :] = normed.astype(jnp.bfloat16)
+        low_one = (normed * gain_one[...] + shift_one[...]).astype(jnp.bfloat16)
+        projected = dot(low_one, weights[:, : 3 * width]) + bias_qkv[...]
+        turning = [table[part, rows, :] for part in range(3)]
+        query = turn(projected[:, :width], turning, 1.0).astype(jnp.bfloat16)
+        qkv[rows, :width] = query * (1.0 / math.sqrt(HEAD))
+        qkv[rows, width : 2 * width] = turn(
+            projected[:, width : 2 * width], turning, 1.0
+        ).astype(jnp.bfloat16)
+        qkv[rows, 2 * width :] = projected[:, 2 * width :].astype(jnp.bfloat16)
+        low_two = (normed * gain_two[...] + shift_two[...]).astype(jnp.bfloat16)
+        pre = dot(low_two, weights[:, 3 * width :]) + bias_up[...]
+        phi = 0.5 * (1.0 + lax.erf(pre * (1.0 / math.sqrt(2.0))))
+        density = jnp.exp(-0.5 * pre * pre) * (1.0 / math.sqrt(2.0 * math.pi))
+        joined[rows, width:] = (pre * phi).astype(jnp.bfloat16)
+        slope[rows, :] = phi + pre * density
+    for start in range(0, seq_len, block):
+        rows = slice(start, start + block)
+        keys = start + block
+        visible = causal(block, keys)
+        result = jnp.zeros((block, width), jnp.float32)
+        logs = jnp.zeros((block, width), jnp.float32)
+        for head in range(width // HEAD):
+            scores = dot(only_head(qkv[rows, :width], head), qkv[:keys, width : 2 * width], (1, 1))
+            scores = jnp.where(visible, scores, NEGATIVE)
+            top = jnp.max(scores, axis=-1, keepdims=True)
+            expo = jnp.where(visible, jnp.exp(scores - top), 0.0)
+            total = jnp.sum(expo, axis=-1, keepdims=True)
+            attended = dot(expo.astype(jnp.bfloat16), qkv[:keys, 2 * width :]) / total
+            mask = head_mask(width, head)
+            result = jnp.where(mask, attended, result)
+            logs = jnp.where(mask, top + jnp.log(total), logs)
+        mixed[rows, :] = result
+        log_total[rows, :] = logs
+        joined[rows, :width] = result.astype(jnp.bfloat16)
+
+
+def branch_kernel(members, place, joined, *refs):
+    parts, (weights, kept, other) = refs[:-3], refs[-3:]
+    assemble_width(place, weights, parts)
+    here, core = place[1], place[2]
+    half = kept.shape[1]
+    for step in range(members):
+        start = (here ^ step) * (2 * half)
+        mine = joined[pl.ds(pl.multiple_of(start + core * half, half), half), :]
+        kept[step] = dot(mine, weights[...], (1, 1))
+        twin = joined[pl.ds(pl.multiple_of(start + (1 - core) * half, half), half), :]
+        other[step] = dot(twin, weights[...], (1, 1)).astype(jnp.bfloat16)
+
+
+def gradient_kernel(members, quarters, place, own, *refs):
+    got, refs = refs[: members - 1], refs[members - 1 :]
+    other, refs = refs[: members - 1], refs[members - 1 :]
+    hat, joined, slope, weights = refs[:4]
+    messages, (grad_heads, grad_up, grad) = refs[4 : 4 + quarters], refs[4 + quarters :]
+    assemble_rows(place, grad, own, got, other)
+    seq_len, depth = grad.shape
+    width = grad_heads.shape[1]
+    units = grad_up.shape[1]
+    block = own.shape[0]
+    biases = jnp.zeros((1, units), jnp.float32)
+    for start in range(0, seq_len, block):
+        rows = slice(start, start + block)
+        back = dot(grad[rows, :], weights[...])
+        grad_heads[rows, :] = back[:, :width].astype(jnp.bfloat16)
+        low = (back[:, width:] * slope[rows, :]).astype(jnp.bfloat16)
+        grad_up[rows, :] = low
+        biases = biases + jnp.sum(low.astype(jnp.float32), axis=0, keepdims=True)
+    part = depth // quarters
+    for step in range(quarters):
+        columns = span(place[0] ^ step, part)
+        message = messages[step]
+        message[:part, :units] = dot(hat[:, columns], grad_up[...], (0, 0)).astype(jnp.bfloat16)
+        values = grad[:, columns]
+        message[:part, units:] = dot(values, joined[...], (0, 0)).astype(jnp.bfloat16)
+        sums = jnp.sum(values.astype(jnp.float32), axis=0, keepdims=True)
+        message[part:, :] = small_rows([biases, sums], message.shape[1])
+
+
+def backward_kernel(members, quarters, place, *refs):
+    qkv, mixed, log_total, grad_heads, grad_up, hat, weights, table, gain_one, gain_two = refs[:10]
+    kept, other = refs[10:12]
+    messages, (grad_proj, sum_key, sum_value) = refs[12 : 12 + quarters], refs[12 + quarters :]
+    here, core = place[1], place[2]
+    seq_len, width = mixed.shape
+    half = kept.shape[1]
+    block = 2 * half
+    scale = 1.0 / math.sqrt(HEAD)
+    sum_key[...] = jnp.zeros_like(sum_key)
+    sum_value[...] = jnp.zeros_like(sum_value)
+    for start in range(0, seq_len, block):
+        rows = slice(start, start + block)
+        keys = start + block
+        visible = causal(block, keys)
+        key, value = qkv[:keys, width : 2 * width], qkv[:keys, 2 * width :]
+        grad_query = jnp.zeros((block, width), jnp.float32)
+        grad_key = jnp.zeros((keys, width), jnp.float32)
+        grad_value = jnp.zeros((keys, width), jnp.float32)
+        product = grad_heads[rows, :].astype(jnp.float32) * mixed[rows, :]
+        for head in range(width // HEAD):
+            query = only_head(qkv[rows, :width], head)
+            heads = only_head(grad_heads[rows, :], head)
+            delta = jnp.sum(only_head(product, head), axis=-1, keepdims=True)
+            logs = log_total[rows, head * HEAD : head * HEAD + 1]
+            scores = dot(query, key, (1, 1))
+            probs = jnp.where(visible, jnp.exp(scores - logs), 0.0)
+            grad_scores = (probs * (dot(heads, value, (1, 1)) - delta)).astype(jnp.bfloat16)
+            grad_query = jnp.where(
+                head_mask(width, head), dot(grad_scores, key) * scale, grad_query
+            )
+            grad_key = grad_key + dot(grad_scores, query, (0, 0))
+            grad_value = grad_value + dot(probs.astype(jnp.bfloat16), heads, (0, 0))
+        turning = [table[part, rows, :] for part in range(3)]
+        grad_proj[rows, :width] = turn(grad_query, turning, -1.0).astype(jnp.bfloat16)
+        sum_key[:keys, :] += grad_key
+        sum_value[:keys, :] += grad_value
+    for start in range(0, seq_len, block):
+        rows = slice(start, start + block)
+        turning = [table[part, rows, :] for part in range(3)]
+        grad_proj[rows, width : 2 * width] = turn(sum_key[rows, :], turning, -1.0).astype(
+            jnp.bfloat16
+        )
+        grad_proj[rows, 2 * width :] = sum_value[rows, :].astype(jnp.bfloat16)
+
+    def norm_gradient(rows):
+        return (
+            dot(grad_proj[rows, :], weights[:, : 3 * width], (1, 1)) * gain_one[...]
+            + dot(grad_up[rows, :], weights[:, 3 * width :], (1, 1)) * gain_two[...]
+        )
+
+    for step in range(members):
+        start = (here ^ step) * block
+        kept[step] = norm_gradient(pl.ds(pl.multiple_of(start + core * half, half), half))
+        twin = norm_gradient(pl.ds(pl.multiple_of(start + (1 - core) * half, half), half))
+        other[step] = twin.astype(jnp.bfloat16)
+    depth = hat.shape[1]
+    part = depth // quarters
+    biases = jnp.sum(grad_proj[...].astype(jnp.float32), axis=0, keepdims=True)
+    for step in range(quarters):
+        message = messages[step]
+        message[:part, :] = dot(
+            hat[:, span(place[0] ^ step, part)], grad_proj[...], (0, 0)
+        ).astype(jnp.bfloat16)
+        message[part:, :] = small_rows([biases], message.shape[1])
+
+
+def share_kernel(members, quarters, place, *refs):
+    parts, messages, line = refs[:quarters], refs[quarters : quarters + members], refs[-1]
+    rows = messages[0].shape[0] - 16
+    whole = rows * members
+    for step in range(members):
+        chosen = span(place[1] ^ step, rows)
+        total = parts[0][chosen, :].astype(jnp.float32)
+        for part in parts[1:]:
+            total = total + part[chosen, :].astype(jnp.float32)
+        messages[step][:rows, :] = total.astype(jnp.bfloat16)
+    total = parts[0][whole:, :].astype(jnp.float32)
+    for part in parts[1:]:
+        total = total + part[whole:, :].astype(jnp.float32)
+    lines = [total[2 * index : 2 * index + 1] + total[2 * index + 1 : 2 * index + 2] for index in (0, 1)]
+    line[...] = lines[1]
+    small = small_rows(lines[:1], total.shape[1])
+    for step in range(members):
+        messages[step][rows:, :] = small
+
+
+def owner_kernel(members, place, *refs):
+    first, refs = refs[:members], refs[members:]
+    second, refs = refs[:members], refs[members:]
+    w_qkv, w_up, gain_one, shift_one, gain_two, shift_two = refs[:6]
+    grad_qkv, bias_qkv, grad_out, grad_up, bias_up, grad_down, norms = refs[6:]
+    here = place[1]
+    rows = grad_up.shape[0]
+    width = grad_out.shape[1] // members
+    units = grad_up.shape[1] // members
+    sums = [jnp.zeros((rows, 1), jnp.float32)] * 4
+    for step in range(members):
+        place_of = here ^ step
+        message = first[step]
+        line = message[rows : rows + 16, :].astype(jnp.float32)
+        line = line[0:1, :units] + line[1:2, :units]
+        values = message[:rows, :units].astype(jnp.float32)
+        there = span(place_of, units)
+        grad_up[:, there] = values * gain_two[...] + shift_two[...] * line
+        bias_up[:, there] = line
+        weight = w_up[:, there].astype(jnp.float32)
+        sums[2] = sums[2] + jnp.sum(weight * values, axis=1, keepdims=True)
+        sums[3] = sums[3] + jnp.sum(weight * line, axis=1, keepdims=True)
+        grad_out[:, span(place_of, width)] = message[:rows, units : units + width].astype(
+            jnp.float32
+        )
+        grad_down[:, there] = message[:rows, units + width :].astype(jnp.float32)
+        message = second[step]
+        whole_line = message[rows : rows + 16, :].astype(jnp.float32)
+        for index in range(3):
+            cut = slice(index * width, (index + 1) * width)
+            line = whole_line[0:1, cut] + whole_line[1:2, cut]
+            values = message[:rows, cut].astype(jnp.float32)
+            there = span(place_of, width)
+            grad_qkv[index, :, there] = values * gain_one[...] + shift_one[...] * line
+            bias_qkv[index : index + 1, there] = line
+            weight = w_qkv[:, index, there].astype(jnp.float32)
+            sums[0] = sums[0] + jnp.sum(weight * values, axis=1, keepdims=True)
+            sums[1] = sums[1] + jnp.sum(weight * line, axis=1, keepdims=True)
+    lane = lax.broadcasted_iota(jnp.int32, (rows, 128), 1)
+    result = jnp.zeros((rows, 128), jnp.float32)
+    for index, total in enumerate(sums):
+        result = jnp.where(lane == index, total, result)
+    norms[...] = result
+
+
+def sum_rows(kept, other):
+    got = send(other, "tensor", 1)
+    total = kept[0] + got[0].astype(jnp.float32)
+    for step in range(1, kept.shape[0]):
+        piece = (kept[step] + got[step].astype(jnp.float32)).astype(jnp.bfloat16)
+        total = total + send(piece, "context", step).astype(jnp.float32)
+    return total
+
+
+def whole_sequences(
+    tokens,
+    cotangent,
+    ln1_gain,
+    ln1_bias,
+    ln2_gain,
+    ln2_bias,
+    w_qkv,
+    b_qkv,
+    w_out,
+    b_out,
+    w_up,
+    b_up,
+    w_down,
+    b_down,
+):
+    members, quarters = lax.axis_size("context"), lax.axis_size("fsdp")
+    here, core = lax.axis_index("context"), lax.axis_index("tensor")
+    rows, depth = tokens.shape
+    half = rows // 2
+    part = depth // quarters
+    width = w_qkv.shape[2] // members
+    units = w_up.shape[1] // members
+    seq_len = rows * members
+    low, wide = jnp.bfloat16, jnp.float32
+    place = jnp.stack([lax.axis_index("fsdp"), here, core]).astype(jnp.int32)
+    others = range(1, members)
+
+    half_tokens, half_grad, own_first, own_second = call(
+        pack_kernel,
+        [
+            ((half, depth), low),
+            ((half, depth), low),
+            ((part, 3 * width + units), low),
+            ((part, width + units), low),
+        ],
+        place,
+        tokens,
+        cotangent,
+        w_qkv,
+        w_out,
+        w_up,
+        w_down,
+    )
+    seq_got = [send(half_tokens, "context", step) for step in others]
+    seq_other = [send(values, "tensor", 1) for values in seq_got]
+    first = [own_first] + [send(own_first, "fsdp", step) for step in range(1, quarters)]
+    second = [own_second] + [send(own_second, "fsdp", step) for step in range(1, quarters)]
+    grad_got = [send(half_grad, "context", step) for step in others]
+    grad_other = [send(values, "tensor", 1) for values in grad_got]
+
+    table = turn_tables(seq_len, width)
+    line = lambda values: values.reshape(1, -1)
+    hat, qkv, mixed, log_total, joined, slope, weights_one = call(
+        lambda *refs: forward_kernel(members, quarters, *refs),
+        [
+            ((seq_len, depth), low),
+            ((seq_len, 3 * width), low),
+            ((seq_len, width), wide),
+            ((seq_len, width), wide),
+            ((seq_len, width + units), low),
+            ((seq_len, units), wide),
+            ((depth, 3 * width + units), low),
+        ],
+        place,
+        tokens,
+        *seq_got,
+        *seq_other,
+        *first,
+        line(ln1_gain),
+        line(ln1_bias),
+        line(ln2_gain),
+        line(ln2_bias),
+        line(take(b_qkv, here * width, width, 1)),
+        line(take(b_up, here * units, units)),
+        table,
+        scratch=[((seq_len, depth), low)],
+    )
+    weights_two, kept, other = call(
+        lambda *refs: branch_kernel(members, *refs),
+        [
+            ((depth, width + units), low),
+            ((members, half, depth), wide),
+            ((members, half, depth), low),
+        ],
+        place,
+        joined,
+        *second,
+    )
+    branches = sum_rows(kept, other)
+    own = take(tokens, core * half, half).astype(wide)
+    result = both_halves((own + branches + b_out + b_down).astype(low))
+
+    *messages, grad_heads, grad_up = call(
+        lambda *refs: gradient_kernel(members, quarters, *refs),
+        [((part + 16, width + 2 * units), low)] * quarters
+        + [((seq_len, width), low), ((seq_len, units), low)],
+        place,
+        cotangent,
+        *grad_got,
+        *grad_other,
+        hat,
+        joined,
+        slope,
+        weights_two,
+        scratch=[((seq_len, depth), low)],
+    )
+    early = messages[:1] + [send(messages[step], "fsdp", step) for step in range(1, quarters)]
+    kept, other, *messages = call(
+        lambda *refs: backward_kernel(members, quarters, *refs),
+        [((members, half, depth), wide), ((members, half, depth), low)]
+        + [((part + 16, 3 * width), low)] * quarters,
+        place,
+        qkv,
+        mixed,
+        log_total,
+        grad_heads,
+        grad_up,
+        hat,
+        weights_one,
+        table,
+        line(ln1_gain),
+        line(ln2_gain),
+        scratch=[
+            ((seq_len, 3 * width), low),
+            ((seq_len, width), wide),
+            ((seq_len, width), wide),
+        ],
+    )
+    late = messages[:1] + [send(messages[step], "fsdp", step) for step in range(1, quarters)]
+    grad_norm = sum_rows(kept, other)
+
+    lines = part // members
+
+    def share(parts):
+        total = parts[0].shape[1]
+        *pieces, sums = call(
+            lambda *refs: share_kernel(members, quarters, *refs),
+            [((lines + 16, total), low)] * members + [((1, total), wide)],
+            place,
+            *parts,
+        )
+        return pieces[:1] + [send(pieces[step], "context", step) for step in others], sums
+
+    early, sums = share(early)
+    late, _ = share(late)
+
+    center = own - jnp.mean(own, axis=-1, keepdims=True)
+    factor = lax.rsqrt(jnp.mean(center * center, axis=-1, keepdims=True) + EPSILON)
+    normed = center * factor
+    grad_input = factor * (
+        grad_norm
+        - jnp.mean(grad_norm, axis=-1, keepdims=True)
+        - normed * jnp.mean(grad_norm * normed, axis=-1, keepdims=True)
+    )
+    own_grad = take(cotangent, core * half, half).astype(wide)
+    grad_tokens = both_halves(own_grad + grad_input)
+
+    begin = lax.axis_index("fsdp") * part + here * lines
+    column = lambda values: take(values, begin, lines).reshape(-1, 1)
+    grad_w_qkv, bias_qkv, grad_w_out, grad_w_up, bias_up, grad_w_down, norms = call(
+        lambda *refs: owner_kernel(members, *refs),
+        [
+            ((3, lines, members * width), wide),
+            ((3, members * width), wide),
+            ((lines, members * width), wide),
+            ((lines, members * units), wide),
+            ((1, members * units), wide),
+            ((lines, members * units), wide),
+            ((lines, 128), wide),
+        ],
+        place,
+        *early,
+        *late,
+        take(w_qkv, here * lines, lines),
+        take(w_up, here * lines, lines),
+        column(ln1_gain),
+        column(ln1_bias),
+        column(ln2_gain),
+        column(ln2_bias),
+    )
+    norms = norms[:, :4].T
+    norms = norms + send(norms, "tensor", 1)
+    columns = take(sums[0], here * lines, lines)
+    return (
+        result,
+        grad_tokens,
+        norms[0],
+        norms[1],
+        norms[2],
+        norms[3],
+        grad_w_qkv.transpose(1, 0, 2),
+        bias_qkv,
+        grad_w_out,
+        columns,
+        grad_w_up,
+        bias_up[0],
+        grad_w_down,
+        columns,
+    )
+
+
+def power_of_two(number):
+    return number & (number - 1) == 0
+
+
+def on_device(*arrays):
+    members = lax.axis_size("context")
+    local_heads = arrays[6].shape[2] // HEAD
+    units = arrays[10].shape[1]
+    fits = (
+        local_heads % members == 0
+        and units % members == 0
+        and lax.axis_size("tensor") == 2
+        and power_of_two(members)
+        and power_of_two(lax.axis_size("fsdp"))
+    )
+    return whole_sequences(*arrays) if fits else gathered_weights(*arrays)
+
+
 def solution(mesh):
     in_specs = (
         P(("fsdp", "context"), None),

time: 913 us -> 251 us (0.27)
  waiting for transfers between devices: 697 us -> 114 us
  blocking collectives: 76.2 us -> 0 us
  Pallas kernels: 0 us -> 54.7 us
  starting transfers between devices: 0.84 us -> 52.8 us
  matrix products: 48.7 us -> 0 us
  local copies, waits for them, and re-layouts: 51.9 us -> 17.7 us
  between operations: 15.1 us -> 1.16 us
    reduce_scatter x3 -> x0, waiting for transfers between devices: 351 us -> none  [the longest x1 183 us: on_device(): lax.psum_scatter(grad_w_up, ('fsdp', 'context'), scatter_dimension=0, til...]
    unnamed x13 -> x0, waiting for transfers between devices: 177 us -> none
    all_gather x5 -> x0, waiting for transfers between devices: 169 us -> none  [the longest x1 50.9 us: on_device(): lax.all_gather(w_down, 'fsdp', axis=0, tiled=True)]
    ppermute x0 -> x41, waiting for transfers between devices: none -> 114 us  [send(): lax.ppermute(values, axis, [(index, index ^ step) for index in range(size)])]
    unnamed x1 -> x0, blocking collectives: 76.2 us -> none
    pallas_call x0 -> x8, Pallas kernels: none -> 54.7 us  [call(): pl.pallas_call(body, out_shape=[jax.ShapeDtypeStruct(shape, kind) for sha...]
    ppermute x0 -> x41, starting transfers between devices: none -> 52.8 us  [send(): lax.ppermute(values, axis, [(index, index ^ step) for index in range(size)])]
    dot_general x19 -> x0, matrix products: 48.7 us -> none  [the longest x1 7.39 us: on_device(): jnp.dot(cotangent, full_down, preferred_element_type=jnp.float32)]
  transfers between devices with their start and end apart: 11 -> 41, of which waited for: 9 -> 16; matrix products, arithmetic and copies ran while one was open for 11% -> 8% of each run, Pallas kernels for 0% -> 11%
where the time goes in v1:
time: 251 us
  waiting for transfers between devices  114 us (45%)
  Pallas kernels  54.7 us (22%)
  starting transfers between devices  52.8 us (21%)
  local copies, waits for them, and re-layouts  17.7 us (7%)
  other arithmetic  10 us (4%)
    ppermute x41, waiting for transfers between devices, send(): lax.ppermute(values, axis, [(index, index ^ step) for index in range(size)])  114 us
    pallas_call x8, Pallas kernels, call(): pl.pallas_call(body, out_shape=[jax.ShapeDtypeStruct(shape, kind) for sha...  54.7 us
    ppermute x41, starting transfers between devices, send(): lax.ppermute(values, axis, [(index, index ^ step) for index in range(size)])  52.8 us
    dynamic_slice x4, local copies, waits for them, and re-layouts, take(): return lax.dynamic_slice_in_dim(values, start, size, axis)  5.49 us
    unnamed x64, local copies, waits for them, and re-layouts  5.33 us
  transfers between devices with their start and end apart: 41, of which 16 were waited for; matrix products, arithmetic and copies ran while one was open for 8% of the time, Pallas kernels for 11%

profile of v1, /device:TPU:0, one launch (start us, length us, event | category | flops | bytes accessed | tf_op | source)
XLA Modules:
  0.0 250.8 jit_solution(18208863057372206779)
XLA Ops:
  0.7 2.8 %copy.34.qkv = bf16[256,3,512]{2,1,0:T(4,128)(2,1)} copy(bf16[256,3,512]{2,0,1:T(8,128)(2,1)} %param.20) | data formatting | bytes 1572864 | tf_op args[6]
  4.0 3.7 %shard_map.245 = (bf16[128,1024]{1,0:T(8,128)(2,1)}, bf16[128,1024]{1,0:T(8,128)(2,1)}, bf16[256,896]{1,0:T(8,128)(2,1)}, bf16[256,640]{1,0:T(8,128)(2,1)}) custom-call(s32[3]{0:T(128)} %pad_add_fusion.place.refs_0_, bf16[256,1024]{1,0:T(8,128)(2,1)} %refs_1_.2, bf16[256,1024]{1,0:T(8,128)(2,1)} %refs_1_.3, bf16[256,3,512]{2,1,0:T(4,128)(2,1)} %copy.34.qkv, ...), custom_call_target="tpu_custom_call" | custom-call | tf_op jit(solution)/shard_map/pallas_call | solution.py:285
  7.7 5.1 %collective-permute-start.2 = (bf16[128,1024]{1,0:T(8,128)(2,1)}, bf16[128,1024]{1,0:T(8,128)(2,1)S(1)}, u32[]{:S(2)}, u32[]{:S(2)}) collective-permute-start(bf16[128,1024]{1,0:T(8,128)(2,1)} %get-tuple-element.56), channel_id=1, source_target_pairs={{0,6},{2,4},{4,2},{6,0},{1,7},{3,5},{5,3},{7,1},{8,14},{10,12},{12... | collective-permute-start | bytes 786440 | tf_op jit(solution)/shard_map/ppermute | solution.py:269
  13.3 3.8 %collective-permute-start.19 = (bf16[128,1024]{1,0:T(8,128)(2,1)}, bf16[128,1024]{1,0:T(8,128)(2,1)}, u32[]{:S(2)}, u32[]{:S(2)}) collective-permute-start(bf16[128,1024]{1,0:T(8,128)(2,1)} %get-tuple-element.65), channel_id=1, source_target_pairs={{0,6},{2,4},{4,2},{6,0},{1,7},{3,5},{5,3},{7,1},{8,14},{10,12},{12... | collective-permute-start | bytes 786440 | tf_op jit(solution)/shard_map/ppermute | solution.py:269
  17.1 3.1 %collective-permute-done.2.refs_4_ = bf16[128,1024]{1,0:T(8,128)(2,1)S(1)} collective-permute-done((bf16[128,1024]{1,0:T(8,128)(2,1)}, bf16[128,1024]{1,0:T(8,128)(2,1)S(1)}, u32[]{:S(2)}, u32[]{:S(2)}) %collective-permute-start.2) | collective-permute-done | bytes 262176 | tf_op jit(solution)/shard_map/ppermute | solution.py:269
  20.2 2.6 %collective-permute-start.8 = (bf16[256,896]{1,0:T(8,128)(2,1)}, bf16[256,896]{1,0:T(8,128)(2,1)S(1)}, u32[]{:S(2)}, u32[]{:S(2)}) collective-permute-start(bf16[256,896]{1,0:T(8,128)(2,1)} %get-tuple-element.57.refs_8_), channel_id=1, source_target_pairs={{0,24},{8,16},{16,8},{24,0},{1,25},{9,17},{17,9},{25,1},{2,26},{10... | collective-permute-start | bytes 1376264 | tf_op jit(solution)/shard_map/ppermute | solution.py:269
  22.9 24.6 %collective-permute-done.1.refs_3_ = bf16[128,1024]{1,0:T(8,128)(2,1)S(1)} collective-permute-done((bf16[128,1024]{1,0:T(8,128)(2,1)}, bf16[128,1024]{1,0:T(8,128)(2,1)S(1)}, u32[]{:S(2)}, u32[]{:S(2)}) %collective-permute-start.1) | collective-permute-done | bytes 262176 | tf_op jit(solution)/shard_map/ppermute | solution.py:269
  47.5 2.4 collective-permute-start.11
  50.5 7.4 %collective-permute-done.18.refs_3_ = bf16[128,1024]{1,0:T(8,128)(2,1)} collective-permute-done((bf16[128,1024]{1,0:T(8,128)(2,1)}, bf16[128,1024]{1,0:T(8,128)(2,1)}, u32[]{:S(2)}, u32[]{:S(2)}) %collective-permute-start.18) | collective-permute-done | bytes 262176 | tf_op jit(solution)/shard_map/ppermute | solution.py:269
  58.0 1.5 collective-permute-start.6
  59.5 2.5 %collective-permute-done.17.refs_2_ = bf16[128,1024]{1,0:T(8,128)(2,1)} collective-permute-done((bf16[128,1024]{1,0:T(8,128)(2,1)}, bf16[128,1024]{1,0:T(8,128)(2,1)}, u32[]{:S(2)}, u32[]{:S(2)}) %collective-permute-start.17) | collective-permute-done | bytes 262176 | tf_op jit(solution)/shard_map/ppermute | solution.py:269
  63.0 3.3 %collective-permute-done.7.refs_10_ = bf16[256,896]{1,0:T(8,128)(2,1)S(1)} collective-permute-done((bf16[256,896]{1,0:T(8,128)(2,1)}, bf16[256,896]{1,0:T(8,128)(2,1)S(1)}, u32[]{:S(2)}, u32[]{:S(2)}) %collective-permute-start.7) | collective-permute-done | bytes 458784 | tf_op jit(solution)/shard_map/ppermute | solution.py:269
  66.2 1.5 collective-permute-start.10
  67.7 1.9 collective-permute-done.6.refs_9_
  69.7 1.5 collective-permute-start.9
  76.1 11.7 %shard_map.246 = (bf16[1024,1024]{1,0:T(8,128)(2,1)}, bf16[1024,384]{1,0:T(8,128)(2,1)}, f32[1024,128]{1,0:T(8,128)}, f32[1024,128]{1,0:T(8,128)}, bf16[1024,640...) custom-call(s32[3]{0:T(128)} %pad_add_fusion.place.refs_0_, bf16[256,1024]{1,0:T(8,128)(2,1)} %refs_1_.2, ...), custom_call_target="tpu_custom_call" | custom-call | tf_op jit(solution)/shard_map/pallas_call | solution.py:285
  87.8 6.6 %shard_map.247 = (bf16[1024,640]{1,0:T(8,128)(2,1)}, f32[4,128,1024]{2,1,0:T(8,128)}, bf16[4,128,1024]{2,1,0:T(8,128)(2,1)}) custom-call(s32[3]{0:T(128)} %pad_add_fusion.place.refs_0_, bf16[1024,640]{1,0:T(8,128)(2,1)} %get-tuple-element.58.refs_1_.refs_9_, bf16[256,640]{1,0:T(8,128)(2,1)} %get-tuple-element.59.refs_2_, ...), custom_call_target="tpu_custom_call" | custom-call | tf_op jit(solution)/shard_map/pallas_call | solution.py:285
  94.5 9.4 %shard_map.248 = (bf16[272,1152]{1,0:T(8,128)(2,1)}, bf16[272,1152]{1,0:T(8,128)(2,1)}, bf16[272,1152]{1,0:T(8,128)(2,1)}, bf16[272,1152]{1,0:T(8,128)(2,1)}, bf...) custom-call(s32[3]{0:T(128)} %pad_add_fusion.place.refs_0_, bf16[256,1024]{1,0:T(8,128)(2,1)} %refs_1_.3, ...), custom_call_target="tpu_custom_call" | custom-call | tf_op jit(solution)/shard_map/pallas_call | solution.py:285
  103.8 15.1 %shard_map.249 = (f32[4,128,1024]{2,1,0:T(8,128)}, bf16[4,128,1024]{2,1,0:T(8,128)(2,1)}, bf16[272,384]{1,0:T(8,128)(2,1)}, bf16[272,384]{1,0:T(8,128)(2,1)}, bf...) custom-call(s32[3]{0:T(128)} %pad_add_fusion.place.refs_0_, bf16[1024,384]{1,0:T(8,128)(2,1)} %get-tuple-element.62.refs_1_, ...), custom_call_target="tpu_custom_call" | custom-call | tf_op jit(solution)/shard_map/pallas_call | solution.py:285
  119.5 1.5 collective-permute-start.35
  121.0 1.5 collective-permute-start.28
  123.0 1.5 collective-permute-start.30
  124.7 2.4 collective-permute-done.34.refs_2_
  128.7 1.5 collective-permute-start.36
  130.2 1.7 constant_dynamic-slice_fusion.1.refs_10_
  131.8 27.1 %collective-permute-done.36.refs_4_ = bf16[272,384]{1,0:T(8,128)(2,1)S(1)} collective-permute-done((bf16[272,384]{1,0:T(8,128)(2,1)}, bf16[272,384]{1,0:T(8,128)(2,1)S(1)}, u32[]{:S(2)}, u32[]{:S(2)}) %collective-permute-start.36) | collective-permute-done | bytes 208928 | tf_op jit(solution)/shard_map/ppermute | solution.py:269
  159.6 2.0 shard_map.251
  161.8 2.8 %collective-permute-start.38 = (bf16[80,384]{1,0:T(8,128)(2,1)}, bf16[80,384]{1,0:T(8,128)(2,1)S(1)}, u32[]{:S(2)}, u32[]{:S(2)}) collective-permute-start(bf16[80,384]{1,0:T(8,128)(2,1)} %get-tuple-element.88), channel_id=1, source_target_pairs={{0,4},{2,6},{4,0},{6,2},{1,5},{3,7},{5,1},{7,3},{8,12},{10,14},{12... | collective-permute-start | bytes 184328 | tf_op jit(solution)/shard_map/ppermute | solution.py:269
  164.6 1.6 collective-permute-start.39
  169.0 2.8 %shard_map.250 = (bf16[80,1152]{1,0:T(8,128)(2,1)}, bf16[80,1152]{1,0:T(8,128)(2,1)}, bf16[80,1152]{1,0:T(8,128)(2,1)}, bf16[80,1152]{1,0:T(8,128)(2,1)}, f32[1,1152]{1,0:T(1,128)}) custom-call(s32[3]{0:T(128)} %pad_add_fusion.place.refs_0_, bf16[272,1152]{1,0:T(8,128)(2,1)} %get-tuple-element.74.refs_1_, bf16[272,1152]{1,0:T(8,128)(2,1)} %copy-done.6, ...), custom_call_target="tpu_custom_call" | custom-call | tf_op jit(solution)/shard_map/pallas_call | solution.py:285
  172.0 2.8 %collective-permute-start.32 = (bf16[80,1152]{1,0:T(8,128)(2,1)}, bf16[80,1152]{1,0:T(8,128)(2,1)S(1)}, u32[]{:S(2)}, u32[]{:S(2)}) collective-permute-start(bf16[80,1152]{1,0:T(8,128)(2,1)} %get-tuple-element.80), channel_id=1, source_target_pairs={{0,4},{2,6},{4,0},{6,2},{1,5},{3,7},{5,1},{7,3},{8,12},{10,14},{12... | collective-permute-start | bytes 552968 | tf_op jit(solution)/shard_map/ppermute | solution.py:269
  174.8 1.6 collective-permute-start.33
  176.3 1.7 constant_dynamic-slice_fusion.2.refs_9_
  178.8 1.7 collective-permute-done.31.refs_2_
  180.5 8.0 %collective-permute-done.32.refs_3_ = bf16[80,1152]{1,0:T(8,128)(2,1)S(1)} collective-permute-done((bf16[80,1152]{1,0:T(8,128)(2,1)}, bf16[80,1152]{1,0:T(8,128)(2,1)S(1)}, u32[]{:S(2)}, u32[]{:S(2)}) %collective-permute-start.32) | collective-permute-done | bytes 184352 | tf_op jit(solution)/shard_map/ppermute | solution.py:269
  189.3 3.4 %shard_map.252 = (f32[3,64,512]{2,1,0:T(8,128)}, f32[3,512]{1,0:T(4,128)}, f32[64,512]{1,0:T(8,128)}, f32[64,2048]{1,0:T(8,128)}, f32[1,2048]{1,0:T(1,128)}, /*index=5*/f32[64,2048]{1,0:T(8,128)}, f32[64,128]{1,0:T(8,128)}) custom-call(s32[3]{0:T(128)} %pad_add_fusion.place.refs_0_, bf16[80,1152]{1,0:T(8,128)(2,1)} %get-tuple-element.78.refs_1_, ...), custom_call_target="tpu_custom_call" | custom-call | tf_op jit(solution)/shard_map/pallas_call | solution.py:285
  193.6 1.4 fusion.19
  195.0 2.6 %collective-permute-start.24 = (bf16[128,1024]{1,0:T(8,128)(2,1)S(1)}, bf16[128,1024]{1,0:T(8,128)(2,1)S(1)}, u32[]{:S(2)}, u32[]{:S(2)}) collective-permute-start(bf16[128,1024]{1,0:T(8,128)(2,1)S(1)} %get-tuple-element.105), channel_id=1, source_target_pairs={{0,2},{2,0},{4,6},{6,4},{1,3},{3,1},{5,7},{7,5},{8,10},{10,8},{12,... | collective-permute-start | bytes 786440 | tf_op jit(solution)/shard_map/ppermute | solution.py:269
  197.7 2.3 collective-permute-start.26
  200.0 1.4 fusion.16
  201.4 2.2 collective-permute-start.13
  204.8 2.3 collective-permute-start.15
  207.1 5.6 %collective-permute-done.26 = bf16[128,1024]{1,0:T(8,128)(2,1)S(1)} collective-permute-done((bf16[128,1024]{1,0:T(8,128)(2,1)S(1)}, bf16[128,1024]{1,0:T(8,128)(2,1)S(1)}, u32[]{:S(2)}, u32[]{:S(2)}) %collective-permute-start.26) | collective-permute-done | bytes 262176 | tf_op jit(solution)/shard_map/ppermute | solution.py:269
  212.8 6.1 %collective-permute-start.14 = (bf16[128,1024]{1,0:T(8,128)(2,1)S(1)}, bf16[128,1024]{1,0:T(8,128)(2,1)S(1)}, u32[]{:S(2)}, u32[]{:S(2)}) collective-permute-start(bf16[128,1024]{1,0:T(8,128)(2,1)S(1)} %get-tuple-element.110), channel_id=1, source_target_pairs={{0,4},{2,6},{4,0},{6,2},{1,5},{3,7},{5,1},{7,3},{8,12},{10,14},{12... | collective-permute-start | bytes 786440 | tf_op jit(solution)/shard_map/ppermute | solution.py:269
  218.8 4.3 %collective-permute-done.25 = bf16[128,1024]{1,0:T(8,128)(2,1)S(1)} collective-permute-done((bf16[128,1024]{1,0:T(8,128)(2,1)S(1)}, bf16[128,1024]{1,0:T(8,128)(2,1)S(1)}, u32[]{:S(2)}, u32[]{:S(2)}) %collective-permute-start.25) | collective-permute-done | bytes 262176 | tf_op jit(solution)/shard_map/ppermute | solution.py:269
  224.5 5.1 %collective-permute-done.15 = bf16[128,1024]{1,0:T(8,128)(2,1)S(1)} collective-permute-done((bf16[128,1024]{1,0:T(8,128)(2,1)S(1)}, bf16[128,1024]{1,0:T(8,128)(2,1)S(1)}, u32[]{:S(2)}, u32[]{:S(2)}) %collective-permute-start.15) | collective-permute-done | bytes 262176 | tf_op jit(solution)/shard_map/ppermute | solution.py:269
  229.6 15.6 %collective-permute-done.14 = bf16[128,1024]{1,0:T(8,128)(2,1)S(1)} collective-permute-done((bf16[128,1024]{1,0:T(8,128)(2,1)S(1)}, bf16[128,1024]{1,0:T(8,128)(2,1)S(1)}, u32[]{:S(2)}, u32[]{:S(2)}) %collective-permute-start.14) | collective-permute-done | bytes 262176 | tf_op jit(solution)/shard_map/ppermute | solution.py:269
  245.2 1.4 fusion.7
  (150 shorter events, 23.1 us)
Async XLA Ops:
  0.6 71.4 %copy-start = (f32[3,512]{1,0:T(4,128)S(1)}, f32[3,512]{1,0:T(4,128)}, u32[]{:S(2)}) copy-start(f32[3,512]{1,0:T(4,128)} %param.21) | copy-start | bytes 18436
  7.7 12.5 %collective-permute-start.2 = (bf16[128,1024]{1,0:T(8,128)(2,1)}, bf16[128,1024]{1,0:T(8,128)(2,1)S(1)}, u32[]{:S(2)}, u32[]{:S(2)}) collective-permute-start(bf16[128,1024]{1,0:T(8,128)(2,1)} %get-tuple-element.56), channel_id=1, source_target_pairs={{0,6},{2,4},{4,2},{6,0},{1,7},{3,5},{5,3},{7,1},{8,14},{10,12},{12... | collective-permute-start | bytes 786440 | tf_op jit(solution)/shard_map/ppermute | solution.py:269
  12.8 34.7 %collective-permute-start.1 = (bf16[128,1024]{1,0:T(8,128)(2,1)}, bf16[128,1024]{1,0:T(8,128)(2,1)S(1)}, u32[]{:S(2)}, u32[]{:S(2)}) collective-permute-start(bf16[128,1024]{1,0:T(8,128)(2,1)} %get-tuple-element.56), channel_id=1, source_target_pairs={{0,4},{2,6},{4,0},{6,2},{1,5},{3,7},{5,1},{7,3},{8,12},{10,14},{12... | collective-permute-start | bytes 786440 | tf_op jit(solution)/shard_map/ppermute | solution.py:269
  12.8 37.2 %collective-permute-start = (bf16[128,1024]{1,0:T(8,128)(2,1)}, bf16[128,1024]{1,0:T(8,128)(2,1)S(1)}, u32[]{:S(2)}, u32[]{:S(2)}) collective-permute-start(bf16[128,1024]{1,0:T(8,128)(2,1)} %get-tuple-element.56), channel_id=1, source_target_pairs={{0,2},{2,0},{4,6},{6,4},{1,3},{3,1},{5,7},{7,5},{8,10},{10,8},{12,... | collective-permute-start | bytes 786440 | tf_op jit(solution)/shard_map/ppermute | solution.py:269
  13.3 36.6 %collective-permute-start.19 = (bf16[128,1024]{1,0:T(8,128)(2,1)}, bf16[128,1024]{1,0:T(8,128)(2,1)}, u32[]{:S(2)}, u32[]{:S(2)}) collective-permute-start(bf16[128,1024]{1,0:T(8,128)(2,1)} %get-tuple-element.65), channel_id=1, source_target_pairs={{0,6},{2,4},{4,2},{6,0},{1,7},{3,5},{5,3},{7,1},{8,14},{10,12},{12... | collective-permute-start | bytes 786440 | tf_op jit(solution)/shard_map/ppermute | solution.py:269
  17.1 40.8 %collective-permute-start.18 = (bf16[128,1024]{1,0:T(8,128)(2,1)}, bf16[128,1024]{1,0:T(8,128)(2,1)}, u32[]{:S(2)}, u32[]{:S(2)}) collective-permute-start(bf16[128,1024]{1,0:T(8,128)(2,1)} %get-tuple-element.65), channel_id=1, source_target_pairs={{0,4},{2,6},{4,0},{6,2},{1,5},{3,7},{5,1},{7,3},{8,12},{10,14},{12... | collective-permute-start | bytes 786440 | tf_op jit(solution)/shard_map/ppermute | solution.py:269
  20.2 53.0 %copy-start.13 = (bf16[128,1024]{1,0:T(8,128)(2,1)}, bf16[128,1024]{1,0:T(8,128)(2,1)S(1)}, u32[]{:S(2)}) copy-start(bf16[128,1024]{1,0:T(8,128)(2,1)S(1)} %collective-permute-done.2.refs_4_) | copy-start | bytes 786436
  20.2 42.3 %collective-permute-start.8 = (bf16[256,896]{1,0:T(8,128)(2,1)}, bf16[256,896]{1,0:T(8,128)(2,1)S(1)}, u32[]{:S(2)}, u32[]{:S(2)}) collective-permute-start(bf16[256,896]{1,0:T(8,128)(2,1)} %get-tuple-element.57.refs_8_), channel_id=1, source_target_pairs={{0,24},{8,16},{16,8},{24,0},{1,25},{9,17},{17,9},{25,1},{2,26},{10... | collective-permute-start | bytes 1376264 | tf_op jit(solution)/shard_map/ppermute | solution.py:269
  47.5 14.5 %collective-permute-start.11 = (bf16[256,640]{1,0:T(8,128)(2,1)}, bf16[256,640]{1,0:T(8,128)(2,1)S(1)}, u32[]{:S(2)}, u32[]{:S(2)}) collective-permute-start(bf16[256,640]{1,0:T(8,128)(2,1)} %get-tuple-element.59.refs_2_), channel_id=1, source_target_pairs={{0,24},{8,16},{16,8},{24,0},{1,25},{9,17},{17,9},{25,1},{2,26},{10... | collective-permute-start | bytes 983048 | tf_op jit(solution)/shard_map/ppermute | solution.py:269
  49.9 12.1 %collective-permute-start.17 = (bf16[128,1024]{1,0:T(8,128)(2,1)}, bf16[128,1024]{1,0:T(8,128)(2,1)}, u32[]{:S(2)}, u32[]{:S(2)}) collective-permute-start(bf16[128,1024]{1,0:T(8,128)(2,1)} %get-tuple-element.65), channel_id=1, source_target_pairs={{0,2},{2,0},{4,6},{6,4},{1,3},{3,1},{5,7},{7,5},{8,10},{10,8},{12,... | collective-permute-start | bytes 786440 | tf_op jit(solution)/shard_map/ppermute | solution.py:269
  49.9 16.3 %collective-permute-start.7 = (bf16[256,896]{1,0:T(8,128)(2,1)}, bf16[256,896]{1,0:T(8,128)(2,1)S(1)}, u32[]{:S(2)}, u32[]{:S(2)}) collective-permute-start(bf16[256,896]{1,0:T(8,128)(2,1)} %get-tuple-element.57.refs_8_), channel_id=1, source_target_pairs={{0,16},{8,24},{16,0},{24,8},{1,17},{9,25},{17,1},{25,9},{2,18},{10... | collective-permute-start | bytes 1376264 | tf_op jit(solution)/shard_map/ppermute | solution.py:269
  58.0 11.7 %collective-permute-start.6 = (bf16[256,896]{1,0:T(8,128)(2,1)}, bf16[256,896]{1,0:T(8,128)(2,1)S(1)}, u32[]{:S(2)}, u32[]{:S(2)}) collective-permute-start(bf16[256,896]{1,0:T(8,128)(2,1)} %get-tuple-element.57.refs_8_), channel_id=1, source_target_pairs={{0,8},{8,0},{16,24},{24,16},{1,9},{9,1},{17,25},{25,17},{2,10},{10... | collective-permute-start | bytes 1376264 | tf_op jit(solution)/shard_map/ppermute | solution.py:269
  62.0 9.3 %collective-permute-start.5 = (bf16[128,1024]{1,0:T(8,128)(2,1)S(1)}, bf16[128,1024]{1,0:T(8,128)(2,1)S(1)}, u32[]{:S(2)}, u32[]{:S(2)}) collective-permute-start(bf16[128,1024]{1,0:T(8,128)(2,1)S(1)} %collective-permute-done.2.refs_4_), channel_id=1, source_target_pairs={{0,1},{1,0},{2,3},{3,2},{4,5},{5,4},{6,7},{7,6},{8,9},{9,8},{10,11... | collective-permute-start | bytes 786440 | tf_op jit(solution)/shard_map/ppermute | solution.py:269
  62.0 9.4 %collective-permute-start.4 = (bf16[128,1024]{1,0:T(8,128)(2,1)S(1)}, bf16[128,1024]{1,0:T(8,128)(2,1)}, u32[]{:S(2)}, u32[]{:S(2)}) collective-permute-start(bf16[128,1024]{1,0:T(8,128)(2,1)S(1)} %collective-permute-done.1.refs_3_), channel_id=1, source_target_pairs={{0,1},{1,0},{2,3},{3,2},{4,5},{5,4},{6,7},{7,6},{8,9},{9,8},{10,11... | collective-permute-start | bytes 786440 | tf_op jit(solution)/shard_map/ppermute | solution.py:269
  62.5 9.4 %collective-permute-start.3 = (bf16[128,1024]{1,0:T(8,128)(2,1)S(1)}, bf16[128,1024]{1,0:T(8,128)(2,1)}, u32[]{:S(2)}, u32[]{:S(2)}) collective-permute-start(bf16[128,1024]{1,0:T(8,128)(2,1)S(1)} %collective-permute-done.refs_2_), channel_id=1, source_target_pairs={{0,1},{1,0},{2,3},{3,2},{4,5},{5,4},{6,7},{7,6},{8,9},{9,8},{10,11... | collective-permute-start | bytes 786440 | tf_op jit(solution)/shard_map/ppermute | solution.py:269
  66.2 21.6 %collective-permute-start.10 = (bf16[256,640]{1,0:T(8,128)(2,1)}, bf16[256,640]{1,0:T(8,128)(2,1)}, u32[]{:S(2)}, u32[]{:S(2)}) collective-permute-start(bf16[256,640]{1,0:T(8,128)(2,1)} %get-tuple-element.59.refs_2_), channel_id=1, source_target_pairs={{0,16},{8,24},{16,0},{24,8},{1,17},{9,25},{17,1},{25,9},{2,18},{10... | collective-permute-start | bytes 983048 | tf_op jit(solution)/shard_map/ppermute | solution.py:269
  69.7 18.1 %collective-permute-start.9 = (bf16[256,640]{1,0:T(8,128)(2,1)}, bf16[256,640]{1,0:T(8,128)(2,1)}, u32[]{:S(2)}, u32[]{:S(2)}) collective-permute-start(bf16[256,640]{1,0:T(8,128)(2,1)} %get-tuple-element.59.refs_2_), channel_id=1, source_target_pairs={{0,8},{8,0},{16,24},{24,16},{1,9},{9,1},{17,25},{25,17},{2,10},{10... | collective-permute-start | bytes 983048 | tf_op jit(solution)/shard_map/ppermute | solution.py:269
  71.3 23.1 %collective-permute-start.22 = (bf16[128,1024]{1,0:T(8,128)(2,1)}, bf16[128,1024]{1,0:T(8,128)(2,1)}, u32[]{:S(2)}, u32[]{:S(2)}) collective-permute-start(bf16[128,1024]{1,0:T(8,128)(2,1)} %collective-permute-done.19.refs_4_), channel_id=1, source_target_pairs={{0,1},{1,0},{2,3},{3,2},{4,5},{5,4},{6,7},{7,6},{8,9},{9,8},{10,11... | collective-permute-start | bytes 786440 | tf_op jit(solution)/shard_map/ppermute | solution.py:269
  71.4 23.0 %collective-permute-start.21 = (bf16[128,1024]{1,0:T(8,128)(2,1)}, bf16[128,1024]{1,0:T(8,128)(2,1)}, u32[]{:S(2)}, u32[]{:S(2)}) collective-permute-start(bf16[128,1024]{1,0:T(8,128)(2,1)} %collective-permute-done.18.refs_3_), channel_id=1, source_target_pairs={{0,1},{1,0},{2,3},{3,2},{4,5},{5,4},{6,7},{7,6},{8,9},{9,8},{10,11... | collective-permute-start | bytes 786440 | tf_op jit(solution)/shard_map/ppermute | solution.py:269
  71.9 22.5 %collective-permute-start.20 = (bf16[128,1024]{1,0:T(8,128)(2,1)}, bf16[128,1024]{1,0:T(8,128)(2,1)}, u32[]{:S(2)}, u32[]{:S(2)}) collective-permute-start(bf16[128,1024]{1,0:T(8,128)(2,1)} %collective-permute-done.17.refs_2_), channel_id=1, source_target_pairs={{0,1},{1,0},{2,3},{3,2},{4,5},{5,4},{6,7},{7,6},{8,9},{9,8},{10,11... | collective-permute-start | bytes 786440 | tf_op jit(solution)/shard_map/ppermute | solution.py:269
  118.9 8.2 %collective-permute-start.34 = (bf16[272,384]{1,0:T(8,128)(2,1)}, bf16[272,384]{1,0:T(8,128)(2,1)S(1)}, u32[]{:S(2)}, u32[]{:S(2)}) collective-permute-start(bf16[272,384]{1,0:T(8,128)(2,1)} %get-tuple-element.83), channel_id=1, source_target_pairs={{0,8},{8,0},{16,24},{24,16},{1,9},{9,1},{17,25},{25,17},{2,10},{10... | collective-permute-start | bytes 626696 | tf_op jit(solution)/shard_map/ppermute | solution.py:269
  119.5 9.2 %collective-permute-start.35 = (bf16[272,384]{1,0:T(8,128)(2,1)}, bf16[272,384]{1,0:T(8,128)(2,1)S(1)}, u32[]{:S(2)}, u32[]{:S(2)}) collective-permute-start(bf16[272,384]{1,0:T(8,128)(2,1)} %get-tuple-element.84), channel_id=1, source_target_pairs={{0,16},{8,24},{16,0},{24,8},{1,17},{9,25},{17,1},{25,9},{2,18},{10... | collective-permute-start | bytes 626696 | tf_op jit(solution)/shard_map/ppermute | solution.py:269
  121.0 40.6 %collective-permute-start.28 = (bf16[272,1152]{1,0:T(8,128)(2,1)}, bf16[272,1152]{1,0:T(8,128)(2,1)S(1)}, u32[]{:S(2)}, u32[]{:S(2)}) collective-permute-start(bf16[272,1152]{1,0:T(8,128)(2,1)} %get-tuple-element.75), channel_id=1, source_target_pairs={{0,8},{8,0},{16,24},{24,16},{1,9},{9,1},{17,25},{25,17},{2,10},{10... | collective-permute-start | bytes 1880072 | tf_op jit(solution)/shard_map/ppermute | solution.py:269
  122.5 39.2 %collective-permute-start.29 = (bf16[272,1152]{1,0:T(8,128)(2,1)}, bf16[272,1152]{1,0:T(8,128)(2,1)S(1)}, u32[]{:S(2)}, u32[]{:S(2)}) collective-permute-start(bf16[272,1152]{1,0:T(8,128)(2,1)} %get-tuple-element.76), channel_id=1, source_target_pairs={{0,16},{8,24},{16,0},{24,8},{1,17},{9,25},{17,1},{25,9},{2,18},{10... | collective-permute-start | bytes 1880072 | tf_op jit(solution)/shard_map/ppermute | solution.py:269
  123.0 41.6 %collective-permute-start.30 = (bf16[272,1152]{1,0:T(8,128)(2,1)}, bf16[272,1152]{1,0:T(8,128)(2,1)S(1)}, u32[]{:S(2)}, u32[]{:S(2)}) collective-permute-start(bf16[272,1152]{1,0:T(8,128)(2,1)} %get-tuple-element.77), channel_id=1, source_target_pairs={{0,24},{8,16},{16,8},{24,0},{1,25},{9,17},{17,9},{25,1},{2,26},{10... | collective-permute-start | bytes 1880072 | tf_op jit(solution)/shard_map/ppermute | solution.py:269
  127.1 31.9 %copy-start.17 = (bf16[272,384]{1,0:T(8,128)(2,1)}, bf16[272,384]{1,0:T(8,128)(2,1)S(1)}, u32[]{:S(2)}) copy-start(bf16[272,384]{1,0:T(8,128)(2,1)S(1)} %collective-permute-done.34.refs_2_) | copy-start | bytes 626692
  127.1 66.5 %collective-permute-start.23 = (bf16[4,128,1024]{2,1,0:T(8,128)(2,1)}, bf16[4,128,1024]{2,1,0:T(8,128)(2,1)}, u32[]{:S(2)}, u32[]{:S(2)}) collective-permute-start(bf16[4,128,1024]{2,1,0:T(8,128)(2,1)} %get-tuple-element.73), channel_id=1, source_target_pairs={{0,1},{1,0},{2,3},{3,2},{4,5},{5,4},{6,7},{7,6},{8,9},{9,8},{10,11... | collective-permute-start | bytes 3145736 | tf_op jit(solution)/shard_map/ppermute | solution.py:269
  128.7 30.3 %collective-permute-start.36 = (bf16[272,384]{1,0:T(8,128)(2,1)}, bf16[272,384]{1,0:T(8,128)(2,1)S(1)}, u32[]{:S(2)}, u32[]{:S(2)}) collective-permute-start(bf16[272,384]{1,0:T(8,128)(2,1)} %get-tuple-element.85), channel_id=1, source_target_pairs={{0,24},{8,16},{16,8},{24,0},{1,25},{9,17},{17,9},{25,1},{2,26},{10... | collective-permute-start | bytes 626696 | tf_op jit(solution)/shard_map/ppermute | solution.py:269
  159.0 41.0 %collective-permute-start.12 = (bf16[4,128,1024]{2,1,0:T(8,128)(2,1)}, bf16[4,128,1024]{2,1,0:T(8,128)(2,1)}, u32[]{:S(2)}, u32[]{:S(2)}) collective-permute-start(bf16[4,128,1024]{2,1,0:T(8,128)(2,1)} %get-tuple-element.61), channel_id=1, source_target_pairs={{0,1},{1,0},{2,3},{3,2},{4,5},{5,4},{6,7},{7,6},{8,9},{9,8},{10,11... | collective-permute-start | bytes 3145736 | tf_op jit(solution)/shard_map/ppermute | solution.py:269
  161.7 10.2 %collective-permute-start.37 = (bf16[80,384]{1,0:T(8,128)(2,1)}, bf16[80,384]{1,0:T(8,128)(2,1)S(1)}, u32[]{:S(2)}, u32[]{:S(2)}) collective-permute-start(bf16[80,384]{1,0:T(8,128)(2,1)} %get-tuple-element.87), channel_id=1, source_target_pairs={{0,2},{2,0},{4,6},{6,4},{1,3},{3,1},{5,7},{7,5},{8,10},{10,8},{12,... | collective-permute-start | bytes 184328 | tf_op jit(solution)/shard_map/ppermute | solution.py:269
  161.8 10.2 %collective-permute-start.38 = (bf16[80,384]{1,0:T(8,128)(2,1)}, bf16[80,384]{1,0:T(8,128)(2,1)S(1)}, u32[]{:S(2)}, u32[]{:S(2)}) collective-permute-start(bf16[80,384]{1,0:T(8,128)(2,1)} %get-tuple-element.88), channel_id=1, source_target_pairs={{0,4},{2,6},{4,0},{6,2},{1,5},{3,7},{5,1},{7,3},{8,12},{10,14},{12... | collective-permute-start | bytes 184328 | tf_op jit(solution)/shard_map/ppermute | solution.py:269
  164.6 10.2 %collective-permute-start.39 = (bf16[80,384]{1,0:T(8,128)(2,1)}, bf16[80,384]{1,0:T(8,128)(2,1)S(1)}, u32[]{:S(2)}, u32[]{:S(2)}) collective-permute-start(bf16[80,384]{1,0:T(8,128)(2,1)} %get-tuple-element.89), channel_id=1, source_target_pairs={{0,6},{2,4},{4,2},{6,0},{1,7},{3,5},{5,3},{7,1},{8,14},{10,12},{12... | collective-permute-start | bytes 184328 | tf_op jit(solution)/shard_map/ppermute | solution.py:269
  171.9 8.6 %collective-permute-start.31 = (bf16[80,1152]{1,0:T(8,128)(2,1)}, bf16[80,1152]{1,0:T(8,128)(2,1)S(1)}, u32[]{:S(2)}, u32[]{:S(2)}) collective-permute-start(bf16[80,1152]{1,0:T(8,128)(2,1)} %get-tuple-element.79), channel_id=1, source_target_pairs={{0,2},{2,0},{4,6},{6,4},{1,3},{3,1},{5,7},{7,5},{8,10},{10,8},{12,... | collective-permute-start | bytes 552968 | tf_op jit(solution)/shard_map/ppermute | solution.py:269
  172.0 16.5 %collective-permute-start.32 = (bf16[80,1152]{1,0:T(8,128)(2,1)}, bf16[80,1152]{1,0:T(8,128)(2,1)S(1)}, u32[]{:S(2)}, u32[]{:S(2)}) collective-permute-start(bf16[80,1152]{1,0:T(8,128)(2,1)} %get-tuple-element.80), channel_id=1, source_target_pairs={{0,4},{2,6},{4,0},{6,2},{1,5},{3,7},{5,1},{7,3},{8,12},{10,14},{12... | collective-permute-start | bytes 552968 | tf_op jit(solution)/shard_map/ppermute | solution.py:269
  174.8 13.7 %collective-permute-start.33 = (bf16[80,1152]{1,0:T(8,128)(2,1)}, bf16[80,1152]{1,0:T(8,128)(2,1)S(1)}, u32[]{:S(2)}, u32[]{:S(2)}) collective-permute-start(bf16[80,1152]{1,0:T(8,128)(2,1)} %get-tuple-element.81), channel_id=1, source_target_pairs={{0,6},{2,4},{4,2},{6,0},{1,7},{3,5},{5,3},{7,1},{8,14},{10,12},{12... | collective-permute-start | bytes 552968 | tf_op jit(solution)/shard_map/ppermute | solution.py:269
  178.8 71.5 %copy-start.29 = (f32[64]{0:T(128)}, f32[64]{0:T(128)S(1)}, u32[]{:S(2)}) copy-start(f32[64]{0:T(128)S(1)} %fusion.23) | copy-start | bytes 772
  193.6 53.6 %collective-permute-start.40 = (f32[4,64]{0,1:T(8,128)S(1)}, f32[4,64]{0,1:T(8,128)S(1)}, u32[]{:S(2)}, u32[]{:S(2)}) collective-permute-start(f32[4,64]{0,1:T(8,128)S(1)} %slice_bitcast_fusion), channel_id=1, source_target_pairs={{0,1},{1,0},{2,3},{3,2},{4,5},{5,4},{6,7},{7,6},{8,9},{9,8},{10,11... | collective-permute-start | bytes 3080 | tf_op jit(solution)/shard_map/ppermute | solution.py:269
  195.0 9.8 %collective-permute-start.24 = (bf16[128,1024]{1,0:T(8,128)(2,1)S(1)}, bf16[128,1024]{1,0:T(8,128)(2,1)S(1)}, u32[]{:S(2)}, u32[]{:S(2)}) collective-permute-start(bf16[128,1024]{1,0:T(8,128)(2,1)S(1)} %get-tuple-element.105), channel_id=1, source_target_pairs={{0,2},{2,0},{4,6},{6,4},{1,3},{3,1},{5,7},{7,5},{8,10},{10,8},{12,... | collective-permute-start | bytes 786440 | tf_op jit(solution)/shard_map/ppermute | solution.py:269
  197.7 15.1 %collective-permute-start.26 = (bf16[128,1024]{1,0:T(8,128)(2,1)S(1)}, bf16[128,1024]{1,0:T(8,128)(2,1)S(1)}, u32[]{:S(2)}, u32[]{:S(2)}) collective-permute-start(bf16[128,1024]{1,0:T(8,128)(2,1)S(1)} %get-tuple-element.106), channel_id=1, source_target_pairs={{0,6},{2,4},{4,2},{6,0},{1,7},{3,5},{5,3},{7,1},{8,14},{10,12},{12... | collective-permute-start | bytes 786440 | tf_op jit(solution)/shard_map/ppermute | solution.py:269
  199.9 23.2 %collective-permute-start.25 = (bf16[128,1024]{1,0:T(8,128)(2,1)S(1)}, bf16[128,1024]{1,0:T(8,128)(2,1)S(1)}, u32[]{:S(2)}, u32[]{:S(2)}) collective-permute-start(bf16[128,1024]{1,0:T(8,128)(2,1)S(1)} %get-tuple-element.107), channel_id=1, source_target_pairs={{0,4},{2,6},{4,0},{6,2},{1,5},{3,7},{5,1},{7,3},{8,12},{10,14},{12... | collective-permute-start | bytes 786440 | tf_op jit(solution)/shard_map/ppermute | solution.py:269
  201.4 43.9 %copy-start.3 = (bf16[256,1024]{1,0:T(8,128)(2,1)S(1)}, bf16[256,1024]{1,0:T(8,128)(2,1)}, u32[]{:S(2)}) copy-start(bf16[256,1024]{1,0:T(8,128)(2,1)} %refs_1_.3) | copy-start | bytes 1572868
  201.4 43.9 %copy-start.27 = (f32[1024]{0:T(1024)S(1)}, f32[1024]{0:T(1024)}, u32[]{:S(2)}) copy-start(f32[1024]{0:T(1024)} %param.27) | copy-start | bytes 12292
  201.4 43.9 %copy-start.28 = (f32[1024]{0:T(1024)S(1)}, f32[1024]{0:T(1024)}, u32[]{:S(2)}) copy-start(f32[1024]{0:T(1024)} %param.23) | copy-start | bytes 12292
  201.4 23.1 %collective-permute-start.13 = (bf16[128,1024]{1,0:T(8,128)(2,1)S(1)}, bf16[128,1024]{1,0:T(8,128)(2,1)S(1)}, u32[]{:S(2)}, u32[]{:S(2)}) collective-permute-start(bf16[128,1024]{1,0:T(8,128)(2,1)S(1)} %get-tuple-element.108), channel_id=1, source_target_pairs={{0,2},{2,0},{4,6},{6,4},{1,3},{3,1},{5,7},{7,5},{8,10},{10,8},{12,... | collective-permute-start | bytes 786440 | tf_op jit(solution)/shard_map/ppermute | solution.py:269
  204.8 24.8 %collective-permute-start.15 = (bf16[128,1024]{1,0:T(8,128)(2,1)S(1)}, bf16[128,1024]{1,0:T(8,128)(2,1)S(1)}, u32[]{:S(2)}, u32[]{:S(2)}) collective-permute-start(bf16[128,1024]{1,0:T(8,128)(2,1)S(1)} %get-tuple-element.109), channel_id=1, source_target_pairs={{0,6},{2,4},{4,2},{6,0},{1,7},{3,5},{5,3},{7,1},{8,14},{10,12},{12... | collective-permute-start | bytes 786440 | tf_op jit(solution)/shard_map/ppermute | solution.py:269
  212.8 32.5 %collective-permute-start.14 = (bf16[128,1024]{1,0:T(8,128)(2,1)S(1)}, bf16[128,1024]{1,0:T(8,128)(2,1)S(1)}, u32[]{:S(2)}, u32[]{:S(2)}) collective-permute-start(bf16[128,1024]{1,0:T(8,128)(2,1)S(1)} %get-tuple-element.110), channel_id=1, source_target_pairs={{0,4},{2,6},{4,0},{6,2},{1,5},{3,7},{5,1},{7,3},{8,12},{10,14},{12... | collective-permute-start | bytes 786440 | tf_op jit(solution)/shard_map/ppermute | solution.py:269
  246.6 1.6 collective-permute-start.16
  246.7 2.4 collective-permute-start.27
  (23 other events, 263.9 us)

commit v2 on v1

--- a/solution.py
+++ b/solution.py
@@ -261,7 +261,7 @@
     )
 
 
-VMEM_BYTES = 60 * 1024 * 1024
+MEBIBYTE = 1024 * 1024
 
 
 def send(values, axis, step):
@@ -281,16 +281,49 @@
     )
 
 
-def call(body, outs, place, *arrays, scratch=()):
+def call(body, outs, place, *arrays, scratch=(), after=(), flops=10**9, memory=16):
+    skipped = len(after)
+
+    def kernel(place_ref, *refs):
+        body(place_ref, *refs[skipped:])
+
     return pl.pallas_call(
-        body,
+        kernel,
         out_shape=[jax.ShapeDtypeStruct(shape, kind) for shape, kind in outs],
         in_specs=[pl.BlockSpec(memory_space=pltpu.SMEM)]
+        + [pl.BlockSpec(memory_space=pl.ANY)] * skipped
         + [pl.BlockSpec(memory_space=pltpu.VMEM)] * len(arrays),
         out_specs=[pl.BlockSpec(memory_space=pltpu.VMEM)] * len(outs),
         scratch_shapes=[pltpu.VMEM(shape, kind) for shape, kind in scratch],
-        compiler_params=pltpu.CompilerParams(vmem_limit_bytes=VMEM_BYTES),
-    )(place, *arrays)
+        cost_estimate=pl.CostEstimate(flops=flops, bytes_accessed=0, transcendentals=0),
+        compiler_params=pltpu.CompilerParams(vmem_limit_bytes=memory * MEBIBYTE),
+    )(place, *after, *arrays)
+
+
+def cut_call(body, outs, place, blocks, after=()):
+    skipped = len(after)
+
+    def kernel(place_ref, *refs):
+        body(place_ref, *refs[skipped:])
+
+    def whole(count):
+        return lambda step, place_ref: (0,) * count
+
+    return pl.pallas_call(
+        kernel,
+        grid_spec=pltpu.PrefetchScalarGridSpec(
+            num_scalar_prefetch=1,
+            grid=(1,),
+            in_specs=[pl.BlockSpec(memory_space=pl.ANY)] * skipped
+            + [
+                pl.BlockSpec(shape, lambda step, place_ref, where=where: where(place_ref))
+                for _, shape, where in blocks
+            ],
+            out_specs=[pl.BlockSpec(shape, whole(len(shape))) for shape, _ in outs],
+        ),
+        out_shape=[jax.ShapeDtypeStruct(shape, kind) for shape, kind in outs],
+        compiler_params=pltpu.CompilerParams(vmem_limit_bytes=60 * MEBIBYTE),
+    )(place, *after, *[array for array, _, _ in blocks])
 
 
 def span(index, size, offset=0):
@@ -338,18 +371,20 @@
     return jnp.stack([jnp.tile(part, (1, heads)) for part in (one, ahead, behind)])
 
 
-def pack_kernel(place, tokens, cotangent, qkv, out, up, down, half_tokens, half_grad, first, second):
-    here, core = place[1], place[2]
-    rows = half_tokens.shape[0]
-    half_tokens[...] = tokens[span(core, rows), :]
-    half_grad[...] = cotangent[span(core, rows), :]
-    width = (first.shape[1] - second.shape[1]) // 2
-    units = second.shape[1] - width
+def pack_kernel(
+    place, tokens, cotangent, qkv, up, out, down, qkv_rows, up_rows, first, second, weights, own_qkv, own_up
+):
+    width, units = qkv.shape[2], up.shape[1]
+    first[...] = tokens[...]
+    second[...] = cotangent[...]
     for part in range(3):
-        first[:, part * width : (part + 1) * width] = qkv[:, part, span(here, width)]
-    first[:, 3 * width :] = up[:, span(here, units)]
-    second[:, :width] = out[:, span(here, width)]
-    second[:, width:] = down[:, span(here, units)]
+        weights[:, part * width : (part + 1) * width] = qkv[part]
+    cut = 3 * width + units
+    weights[:, 3 * width : cut] = up[...]
+    weights[:, cut : cut + width] = out[...]
+    weights[:, cut + width :] = down[...]
+    own_qkv[...] = qkv_rows[...]
+    own_up[...] = up_rows[...]
 
 
 def assemble_rows(place, whole, own, got, other):
@@ -358,14 +393,20 @@
     whole[span(here, rows), :] = own[...]
     for step in range(1, len(got) + 1):
         start = (here ^ step) * rows
-        whole[pl.ds(pl.multiple_of(start + core * half, half), half), :] = got[step - 1][...]
-        whole[pl.ds(pl.multiple_of(start + (1 - core) * half, half), half), :] = other[step - 1][...]
-
-
-def assemble_width(place, whole, parts):
+        mine = pl.ds(pl.multiple_of(start + core * half, half), half)
+        whole[mine, :] = got[step - 1][...]
+        twins = pl.ds(pl.multiple_of(start + (1 - core) * half, half), half)
+        whole[twins, :] = other[step - 1][...]
+
+
+def assemble_width(place, whole, parts, columns):
     rows = parts[0].shape[0]
     for step, part in enumerate(parts):
-        whole[span(place[0] ^ step, rows), :] = part[...]
+        whole[span(place[0] ^ step, rows), :] = part[:, columns]
+
+
+def column_sums(values):
+    return dot(jnp.ones((16, values.shape[0]), jnp.bfloat16), values)[0:1, :]
 
 
 def head_mask(width, head):
@@ -377,9 +418,9 @@
     return jnp.where(head_mask(values.shape[1], head), values, jnp.zeros_like(values))
 
 
-def causal(block, keys):
-    row = lax.broadcasted_iota(jnp.int32, (block, keys), 0) + (keys - block)
-    return lax.broadcasted_iota(jnp.int32, (block, keys), 1) <= row
+def causal(rows, first, keys):
+    row = lax.broadcasted_iota(jnp.int32, (rows, keys), 0) + first
+    return lax.broadcasted_iota(jnp.int32, (rows, keys), 1) <= row
 
 
 def forward_kernel(members, quarters, place, *refs):
@@ -388,9 +429,12 @@
     other, refs = refs[: members - 1], refs[members - 1 :]
     parts, refs = refs[:quarters], refs[quarters:]
     gain_one, shift_one, gain_two, shift_two, bias_qkv, bias_up, table = refs[:7]
-    hat, qkv, mixed, log_total, joined, slope, weights, seq = refs[7:]
+    hat_turned, qkv, mixed, log_total, joined, slope, weights, weights_two = refs[7:15]
+    seq, low_one, low_two = refs[15:]
     assemble_rows(place, seq, own, got, other)
-    assemble_width(place, weights, parts)
+    cut = weights.shape[1]
+    assemble_width(place, weights, parts, slice(0, cut))
+    assemble_width(place, weights_two, parts, slice(cut, cut + weights_two.shape[1]))
     seq_len = seq.shape[0]
     width = mixed.shape[1]
     block = own.shape[0]
@@ -400,33 +444,33 @@
         center = values - jnp.mean(values, axis=-1, keepdims=True)
         spread = jnp.mean(center * center, axis=-1, keepdims=True)
         normed = center * lax.rsqrt(spread + EPSILON)
-        hat[rows, :] = normed.astype(jnp.bfloat16)
-        low_one = (normed * gain_one[...] + shift_one[...]).astype(jnp.bfloat16)
-        projected = dot(low_one, weights[:, : 3 * width]) + bias_qkv[...]
-        turning = [table[part, rows, :] for part in range(3)]
-        query = turn(projected[:, :width], turning, 1.0).astype(jnp.bfloat16)
-        qkv[rows, :width] = query * (1.0 / math.sqrt(HEAD))
-        qkv[rows, width : 2 * width] = turn(
-            projected[:, width : 2 * width], turning, 1.0
-        ).astype(jnp.bfloat16)
-        qkv[rows, 2 * width :] = projected[:, 2 * width :].astype(jnp.bfloat16)
-        low_two = (normed * gain_two[...] + shift_two[...]).astype(jnp.bfloat16)
-        pre = dot(low_two, weights[:, 3 * width :]) + bias_up[...]
-        phi = 0.5 * (1.0 + lax.erf(pre * (1.0 / math.sqrt(2.0))))
-        density = jnp.exp(-0.5 * pre * pre) * (1.0 / math.sqrt(2.0 * math.pi))
-        joined[rows, width:] = (pre * phi).astype(jnp.bfloat16)
-        slope[rows, :] = phi + pre * density
+        hat_turned[:, rows] = normed.astype(jnp.bfloat16).T
+        low_one[rows, :] = (normed * gain_one[...] + shift_one[...]).astype(jnp.bfloat16)
+        low_two[rows, :] = (normed * gain_two[...] + shift_two[...]).astype(jnp.bfloat16)
+    turning = [table[part] for part in range(3)]
+    query = dot(low_one[...], weights[:, :width]) + bias_qkv[:, :width]
+    query = turn(query, turning, 1.0).astype(jnp.bfloat16)
+    qkv[:, :width] = query * (1.0 / math.sqrt(HEAD))
+    key = dot(low_one[...], weights[:, width : 2 * width]) + bias_qkv[:, width : 2 * width]
+    qkv[:, width : 2 * width] = turn(key, turning, 1.0).astype(jnp.bfloat16)
+    value = dot(low_one[...], weights[:, 2 * width : 3 * width]) + bias_qkv[:, 2 * width :]
+    qkv[:, 2 * width :] = value.astype(jnp.bfloat16)
+    pre = dot(low_two[...], weights[:, 3 * width :]) + bias_up[...]
+    phi = 0.5 * (1.0 + lax.erf(pre * (1.0 / math.sqrt(2.0))))
+    density = jnp.exp(-0.5 * pre * pre) * (1.0 / math.sqrt(2.0 * math.pi))
+    joined[:, width:] = (pre * phi).astype(jnp.bfloat16)
+    slope[...] = phi + pre * density
     for start in range(0, seq_len, block):
         rows = slice(start, start + block)
         keys = start + block
-        visible = causal(block, keys)
+        visible = causal(block, start, keys)
         result = jnp.zeros((block, width), jnp.float32)
         logs = jnp.zeros((block, width), jnp.float32)
         for head in range(width // HEAD):
             scores = dot(only_head(qkv[rows, :width], head), qkv[:keys, width : 2 * width], (1, 1))
             scores = jnp.where(visible, scores, NEGATIVE)
             top = jnp.max(scores, axis=-1, keepdims=True)
-            expo = jnp.where(visible, jnp.exp(scores - top), 0.0)
+            expo = jnp.exp(scores - top)
             total = jnp.sum(expo, axis=-1, keepdims=True)
             attended = dot(expo.astype(jnp.bfloat16), qkv[:keys, 2 * width :]) / total
             mask = head_mask(width, head)
@@ -437,63 +481,60 @@
         joined[rows, :width] = result.astype(jnp.bfloat16)
 
 
-def branch_kernel(members, place, joined, *refs):
-    parts, (weights, kept, other) = refs[:-3], refs[-3:]
-    assemble_width(place, weights, parts)
+def gather_halves(place, values, mine, twins):
     here, core = place[1], place[2]
-    half = kept.shape[1]
+    members, half = mine.shape[:2]
     for step in range(members):
         start = (here ^ step) * (2 * half)
-        mine = joined[pl.ds(pl.multiple_of(start + core * half, half), half), :]
-        kept[step] = dot(mine, weights[...], (1, 1))
-        twin = joined[pl.ds(pl.multiple_of(start + (1 - core) * half, half), half), :]
-        other[step] = dot(twin, weights[...], (1, 1)).astype(jnp.bfloat16)
+        mine[step] = values[pl.ds(pl.multiple_of(start + core * half, half), half), :]
+        twins[step] = values[pl.ds(pl.multiple_of(start + (1 - core) * half, half), half), :]
+
+
+def flat(values):
+    return values.reshape(values.shape[0] * values.shape[1], values.shape[2])
+
+
+def branch_kernel(place, joined, weights, kept, other, mine, twins):
+    gather_halves(place, joined, mine, twins)
+    kept[...] = dot(flat(mine[...]), weights[...], (1, 1)).reshape(kept.shape)
+    partial = dot(flat(twins[...]), weights[...], (1, 1))
+    other[...] = partial.astype(jnp.bfloat16).reshape(other.shape)
 
 
 def gradient_kernel(members, quarters, place, own, *refs):
     got, refs = refs[: members - 1], refs[members - 1 :]
     other, refs = refs[: members - 1], refs[members - 1 :]
-    hat, joined, slope, weights = refs[:4]
-    messages, (grad_heads, grad_up, grad) = refs[4 : 4 + quarters], refs[4 + quarters :]
+    hat_turned, joined, slope, weights = refs[:4]
+    messages, refs = refs[4 : 4 + quarters], refs[4 + quarters :]
+    grad_heads, grad_up, grad, partial = refs
     assemble_rows(place, grad, own, got, other)
-    seq_len, depth = grad.shape
+    depth = grad.shape[1]
     width = grad_heads.shape[1]
     units = grad_up.shape[1]
-    block = own.shape[0]
-    biases = jnp.zeros((1, units), jnp.float32)
-    for start in range(0, seq_len, block):
-        rows = slice(start, start + block)
-        back = dot(grad[rows, :], weights[...])
-        grad_heads[rows, :] = back[:, :width].astype(jnp.bfloat16)
-        low = (back[:, width:] * slope[rows, :]).astype(jnp.bfloat16)
-        grad_up[rows, :] = low
-        biases = biases + jnp.sum(low.astype(jnp.float32), axis=0, keepdims=True)
+    grad_heads[...] = dot(grad[...], weights[:, :width]).astype(jnp.bfloat16)
+    grad_up[...] = (dot(grad[...], weights[:, width:]) * slope[...]).astype(jnp.bfloat16)
+    partial[:, :units] = dot(hat_turned[...], grad_up[...]).astype(jnp.bfloat16)
+    partial[:, units:] = dot(grad[...], joined[...], (0, 0)).astype(jnp.bfloat16)
+    biases = column_sums(grad_up[...])
     part = depth // quarters
     for step in range(quarters):
-        columns = span(place[0] ^ step, part)
+        quarter = span(place[0] ^ step, part)
         message = messages[step]
-        message[:part, :units] = dot(hat[:, columns], grad_up[...], (0, 0)).astype(jnp.bfloat16)
-        values = grad[:, columns]
-        message[:part, units:] = dot(values, joined[...], (0, 0)).astype(jnp.bfloat16)
-        sums = jnp.sum(values.astype(jnp.float32), axis=0, keepdims=True)
+        message[:part, :] = partial[quarter, :]
+        sums = column_sums(grad[:, quarter])
         message[part:, :] = small_rows([biases, sums], message.shape[1])
 
 
-def backward_kernel(members, quarters, place, *refs):
-    qkv, mixed, log_total, grad_heads, grad_up, hat, weights, table, gain_one, gain_two = refs[:10]
-    kept, other = refs[10:12]
-    messages, (grad_proj, sum_key, sum_value) = refs[12 : 12 + quarters], refs[12 + quarters :]
-    here, core = place[1], place[2]
+def backward_kernel(block, place, *refs):
+    qkv, mixed, log_total, grad_heads, table, grad_proj, sum_key, sum_value = refs
     seq_len, width = mixed.shape
-    half = kept.shape[1]
-    block = 2 * half
     scale = 1.0 / math.sqrt(HEAD)
     sum_key[...] = jnp.zeros_like(sum_key)
     sum_value[...] = jnp.zeros_like(sum_value)
     for start in range(0, seq_len, block):
         rows = slice(start, start + block)
         keys = start + block
-        visible = causal(block, keys)
+        visible = causal(block, start, keys)
         key, value = qkv[:keys, width : 2 * width], qkv[:keys, 2 * width :]
         grad_query = jnp.zeros((block, width), jnp.float32)
         grad_key = jnp.zeros((keys, width), jnp.float32)
@@ -516,61 +557,74 @@
         grad_proj[rows, :width] = turn(grad_query, turning, -1.0).astype(jnp.bfloat16)
         sum_key[:keys, :] += grad_key
         sum_value[:keys, :] += grad_value
-    for start in range(0, seq_len, block):
-        rows = slice(start, start + block)
-        turning = [table[part, rows, :] for part in range(3)]
-        grad_proj[rows, width : 2 * width] = turn(sum_key[rows, :], turning, -1.0).astype(
-            jnp.bfloat16
-        )
-        grad_proj[rows, 2 * width :] = sum_value[rows, :].astype(jnp.bfloat16)
-
-    def norm_gradient(rows):
-        return (
-            dot(grad_proj[rows, :], weights[:, : 3 * width], (1, 1)) * gain_one[...]
-            + dot(grad_up[rows, :], weights[:, 3 * width :], (1, 1)) * gain_two[...]
-        )
-
-    for step in range(members):
-        start = (here ^ step) * block
-        kept[step] = norm_gradient(pl.ds(pl.multiple_of(start + core * half, half), half))
-        twin = norm_gradient(pl.ds(pl.multiple_of(start + (1 - core) * half, half), half))
-        other[step] = twin.astype(jnp.bfloat16)
-    depth = hat.shape[1]
-    part = depth // quarters
-    biases = jnp.sum(grad_proj[...].astype(jnp.float32), axis=0, keepdims=True)
+    turning = [table[part] for part in range(3)]
+    grad_proj[:, width : 2 * width] = turn(sum_key[...], turning, -1.0).astype(jnp.bfloat16)
+    grad_proj[:, 2 * width :] = sum_value[...].astype(jnp.bfloat16)
+
+
+def norm_gradient_kernel(quarters, place, *refs):
+    grad_proj, grad_up, hat_turned, weights, gain_one, gain_two, kept, other = refs[:8]
+    messages, refs = refs[8 : 8 + quarters], refs[8 + quarters :]
+    mine_proj, twins_proj, mine_up, twins_up, weight_sum = refs
+    cut = grad_proj.shape[1]
+    gather_halves(place, grad_proj, mine_proj, twins_proj)
+    gather_halves(place, grad_up, mine_up, twins_up)
+
+    def gradient(proj, up):
+        first = dot(flat(proj[...]), weights[:, :cut], (1, 1)) * gain_one[...]
+        return first + dot(flat(up[...]), weights[:, cut:], (1, 1)) * gain_two[...]
+
+    other[...] = gradient(twins_proj, twins_up).astype(jnp.bfloat16).reshape(other.shape)
+    kept[...] = gradient(mine_proj, mine_up).reshape(kept.shape)
+    weight_sum[...] = dot(hat_turned[...], grad_proj[...]).astype(jnp.bfloat16)
+    part = hat_turned.shape[0] // quarters
+    biases = column_sums(grad_proj[...])
     for step in range(quarters):
         message = messages[step]
-        message[:part, :] = dot(
-            hat[:, span(place[0] ^ step, part)], grad_proj[...], (0, 0)
-        ).astype(jnp.bfloat16)
+        message[:part, :] = weight_sum[span(place[0] ^ step, part), :]
         message[part:, :] = small_rows([biases], message.shape[1])
 
 
-def share_kernel(members, quarters, place, *refs):
-    parts, messages, line = refs[:quarters], refs[quarters : quarters + members], refs[-1]
-    rows = messages[0].shape[0] - 16
-    whole = rows * members
+def add_parts(parts, chosen):
+    total = parts[0][chosen, :].astype(jnp.float32)
+    for part in parts[1:]:
+        total = total + part[chosen, :].astype(jnp.float32)
+    return total
+
+
+def share_early_kernel(members, quarters, place, *refs):
+    parts, pieces, line = refs[:quarters], refs[quarters:-1], refs[-1]
+    rows = pieces[0].shape[0] - 16
     for step in range(members):
         chosen = span(place[1] ^ step, rows)
-        total = parts[0][chosen, :].astype(jnp.float32)
-        for part in parts[1:]:
-            total = total + part[chosen, :].astype(jnp.float32)
-        messages[step][:rows, :] = total.astype(jnp.bfloat16)
-    total = parts[0][whole:, :].astype(jnp.float32)
-    for part in parts[1:]:
-        total = total + part[whole:, :].astype(jnp.float32)
-    lines = [total[2 * index : 2 * index + 1] + total[2 * index + 1 : 2 * index + 2] for index in (0, 1)]
-    line[...] = lines[1]
-    small = small_rows(lines[:1], total.shape[1])
+        pieces[step][:rows, :] = add_parts(parts, chosen).astype(jnp.bfloat16)
+    total = add_parts(parts, slice(rows * members, rows * members + 16))
+    line[...] = total[2:3] + total[3:4]
+    small = small_rows([total[0:1] + total[1:2]], total.shape[1])
     for step in range(members):
-        messages[step][rows:, :] = small
+        pieces[step][rows:, :] = small
+
+
+def share_late_kernel(members, quarters, place, *refs):
+    parts, refs = refs[:quarters], refs[quarters:]
+    early, pieces = refs[:members], refs[members:]
+    rows = pieces[0].shape[0] - 16
+    width = early[0].shape[1]
+    for step in range(members):
+        chosen = span(place[1] ^ step, rows)
+        pieces[step][:, :width] = early[step][...]
+        pieces[step][:rows, width:] = add_parts(parts, chosen).astype(jnp.bfloat16)
+    total = add_parts(parts, slice(rows * members, rows * members + 16))
+    small = small_rows([total[0:1] + total[1:2]], total.shape[1])
+    for step in range(members):
+        pieces[step][rows:, width:] = small
 
 
 def owner_kernel(members, place, *refs):
-    first, refs = refs[:members], refs[members:]
-    second, refs = refs[:members], refs[members:]
-    w_qkv, w_up, gain_one, shift_one, gain_two, shift_two = refs[:6]
-    grad_qkv, bias_qkv, grad_out, grad_up, bias_up, grad_down, norms = refs[6:]
+    pieces, refs = refs[:members], refs[members:]
+    w_qkv, w_up, lines = refs[:3]
+    grad_qkv, bias_qkv, grad_out, grad_up, bias_up, grad_down, norms = refs[3:]
+    gain_one, shift_one, gain_two, shift_two = [lines[:, i : i + 1] for i in range(4)]
     here = place[1]
     rows = grad_up.shape[0]
     width = grad_out.shape[1] // members
@@ -578,12 +632,12 @@
     sums = [jnp.zeros((rows, 1), jnp.float32)] * 4
     for step in range(members):
         place_of = here ^ step
-        message = first[step]
+        message = pieces[step]
         line = message[rows : rows + 16, :].astype(jnp.float32)
         line = line[0:1, :units] + line[1:2, :units]
         values = message[:rows, :units].astype(jnp.float32)
         there = span(place_of, units)
-        grad_up[:, there] = values * gain_two[...] + shift_two[...] * line
+        grad_up[:, there] = values * gain_two + shift_two * line
         bias_up[:, there] = line
         weight = w_up[:, there].astype(jnp.float32)
         sums[2] = sums[2] + jnp.sum(weight * values, axis=1, keepdims=True)
@@ -591,17 +645,17 @@
         grad_out[:, span(place_of, width)] = message[:rows, units : units + width].astype(
             jnp.float32
         )
-        grad_down[:, there] = message[:rows, units + width :].astype(jnp.float32)
-        message = second[step]
+        begin = 2 * units + width
+        grad_down[:, there] = message[:rows, units + width : begin].astype(jnp.float32)
         whole_line = message[rows : rows + 16, :].astype(jnp.float32)
         for index in range(3):
-            cut = slice(index * width, (index + 1) * width)
+            cut = slice(begin + index * width, begin + (index + 1) * width)
             line = whole_line[0:1, cut] + whole_line[1:2, cut]
             values = message[:rows, cut].astype(jnp.float32)
             there = span(place_of, width)
-            grad_qkv[index, :, there] = values * gain_one[...] + shift_one[...] * line
+            grad_qkv[index, :, there] = values * gain_one + shift_one * line
             bias_qkv[index : index + 1, there] = line
-            weight = w_qkv[:, index, there].astype(jnp.float32)
+            weight = w_qkv[index, :, there].astype(jnp.float32)
             sums[0] = sums[0] + jnp.sum(weight * values, axis=1, keepdims=True)
             sums[1] = sums[1] + jnp.sum(weight * line, axis=1, keepdims=True)
     lane = lax.broadcasted_iota(jnp.int32, (rows, 128), 1)
@@ -611,13 +665,51 @@
     norms[...] = result
 
 
-def sum_rows(kept, other):
-    got = send(other, "tensor", 1)
-    total = kept[0] + got[0].astype(jnp.float32)
-    for step in range(1, kept.shape[0]):
-        piece = (kept[step] + got[step].astype(jnp.float32)).astype(jnp.bfloat16)
-        total = total + send(piece, "context", step).astype(jnp.float32)
-    return total
+def halve_kernel(place, kept, got, stay, leave):
+    for index in range(stay.shape[0]):
+        stay[index] = kept[2 * index] + got[2 * index].astype(jnp.float32)
+        odd = kept[2 * index + 1] + got[2 * index + 1].astype(jnp.float32)
+        leave[index] = odd.astype(jnp.bfloat16)
+
+
+def first_halving(place, kept, other, after=()):
+    members, half, depth = kept.shape
+    return call(
+        halve_kernel,
+        [((members // 2, half, depth), jnp.float32), ((members // 2, half, depth), jnp.bfloat16)],
+        place,
+        kept,
+        send(other, "tensor", 1),
+        after=after,
+        flops=1,
+    )
+
+
+def last_halvings(total):
+    step = 1
+    while total.shape[0] > 1:
+        step = 2 * step
+        leave = send(total[1::2].astype(jnp.bfloat16), "context", step)
+        total = total[0::2] + leave.astype(jnp.float32)
+    return total[0]
+
+
+def gather(values, axis):
+    parts = [values]
+    for step in range(1, lax.axis_size(axis)):
+        top = 1 << (step.bit_length() - 1)
+        low = step ^ top
+        parts.append(send(values, axis, step) if not low else send(parts[top], axis, low))
+    return parts
+
+
+def gather_halves_apart(values):
+    if lax.axis_size("fsdp") != 4:
+        return gather(values, "fsdp")
+    half = values.shape[0] // 2
+    one, two = send(values, "fsdp", 1), send(values, "fsdp", 2)
+    three = [send(one[:half], "fsdp", 2), send(two[half:], "fsdp", 1)]
+    return [values, one, two, jnp.concatenate(three)]
 
 
 def whole_sequences(
@@ -641,54 +733,62 @@
     rows, depth = tokens.shape
     half = rows // 2
     part = depth // quarters
+    lines = part // members
     width = w_qkv.shape[2] // members
     units = w_up.shape[1] // members
     seq_len = rows * members
     low, wide = jnp.bfloat16, jnp.float32
     place = jnp.stack([lax.axis_index("fsdp"), here, core]).astype(jnp.int32)
     others = range(1, members)
-
-    half_tokens, half_grad, own_first, own_second = call(
+    parted_qkv = w_qkv.transpose(1, 0, 2)
+
+    cuts = 4 * width + 2 * units
+    half_tokens, half_grad, own_weights, qkv_rows, up_rows = cut_call(
         pack_kernel,
         [
             ((half, depth), low),
             ((half, depth), low),
-            ((part, 3 * width + units), low),
-            ((part, width + units), low),
+            ((part, cuts), low),
+            ((3, lines, members * width), low),
+            ((lines, members * units), low),
         ],
         place,
-        tokens,
-        cotangent,
-        w_qkv,
-        w_out,
-        w_up,
-        w_down,
-    )
-    seq_got = [send(half_tokens, "context", step) for step in others]
+        [
+            (tokens, (half, depth), lambda at: (at[2], 0)),
+            (cotangent, (half, depth), lambda at: (at[2], 0)),
+            (parted_qkv, (3, part, width), lambda at: (0, 0, at[1])),
+            (w_up, (part, units), lambda at: (0, at[1])),
+            (w_out, (part, width), lambda at: (0, at[1])),
+            (w_down, (part, units), lambda at: (0, at[1])),
+            (parted_qkv, (3, lines, members * width), lambda at: (0, at[1], 0)),
+            (w_up, (lines, members * units), lambda at: (at[1], 0)),
+        ],
+    )
+    seq_got = gather(half_tokens, "context")[1:]
     seq_other = [send(values, "tensor", 1) for values in seq_got]
-    first = [own_first] + [send(own_first, "fsdp", step) for step in range(1, quarters)]
-    second = [own_second] + [send(own_second, "fsdp", step) for step in range(1, quarters)]
-    grad_got = [send(half_grad, "context", step) for step in others]
+    grad_got = gather(half_grad, "context")[1:]
     grad_other = [send(values, "tensor", 1) for values in grad_got]
+    parts = gather_halves_apart(own_weights)
 
     table = turn_tables(seq_len, width)
     line = lambda values: values.reshape(1, -1)
-    hat, qkv, mixed, log_total, joined, slope, weights_one = call(
+    hat_turned, qkv, mixed, log_total, joined, slope, weights_one, weights_two = call(
         lambda *refs: forward_kernel(members, quarters, *refs),
         [
-            ((seq_len, depth), low),
+            ((depth, seq_len), low),
             ((seq_len, 3 * width), low),
             ((seq_len, width), wide),
             ((seq_len, width), wide),
             ((seq_len, width + units), low),
             ((seq_len, units), wide),
             ((depth, 3 * width + units), low),
+            ((depth, width + units), low),
         ],
         place,
         tokens,
         *seq_got,
         *seq_other,
-        *first,
+        *parts,
         line(ln1_gain),
         line(ln1_bias),
         line(ln2_gain),
@@ -696,23 +796,20 @@
         line(take(b_qkv, here * width, width, 1)),
         line(take(b_up, here * units, units)),
         table,
-        scratch=[((seq_len, depth), low)],
-    )
-    weights_two, kept, other = call(
-        lambda *refs: branch_kernel(members, *refs),
-        [
-            ((depth, width + units), low),
-            ((members, half, depth), wide),
-            ((members, half, depth), low),
-        ],
+        scratch=[((seq_len, depth), low)] * 3,
+        flops=12 * 10**9,
+        memory=60,
+    )
+    kept, other = call(
+        branch_kernel,
+        [((members, half, depth), wide), ((members, half, depth), low)],
         place,
         joined,
-        *second,
-    )
-    branches = sum_rows(kept, other)
-    own = take(tokens, core * half, half).astype(wide)
-    result = both_halves((own + branches + b_out + b_down).astype(low))
-
+        weights_two,
+        scratch=[((members, half, width + units), low)] * 2,
+        flops=4 * 10**9,
+        memory=60,
+    )
     *messages, grad_heads, grad_up = call(
         lambda *refs: gradient_kernel(members, quarters, *refs),
         [((part + 16, width + 2 * units), low)] * quarters
@@ -721,52 +818,80 @@
         cotangent,
         *grad_got,
         *grad_other,
-        hat,
+        hat_turned,
         joined,
         slope,
         weights_two,
-        scratch=[((seq_len, depth), low)],
+        scratch=[
+            ((seq_len, depth), low),
+            ((depth, width + 2 * units), low),
+        ],
+        after=[other],
+        flops=11 * 10**9,
+        memory=60,
     )
     early = messages[:1] + [send(messages[step], "fsdp", step) for step in range(1, quarters)]
-    kept, other, *messages = call(
-        lambda *refs: backward_kernel(members, quarters, *refs),
-        [((members, half, depth), wide), ((members, half, depth), low)]
-        + [((part + 16, 3 * width), low)] * quarters,
+    stay, leave = first_halving(place, kept, other, after=[grad_heads])
+    leave = send(leave, "context", 1)
+    (grad_proj,) = call(
+        lambda *refs: backward_kernel(rows, *refs),
+        [((seq_len, 3 * width), low)],
         place,
         qkv,
         mixed,
         log_total,
         grad_heads,
+        table,
+        scratch=[((seq_len, width), wide)] * 2,
+        after=[stay],
+        flops=1,
+        memory=60,
+    )
+    total = stay + leave.astype(wide)
+    kept, other, *messages = call(
+        lambda *refs: norm_gradient_kernel(quarters, *refs),
+        [((members, half, depth), wide), ((members, half, depth), low)]
+        + [((part + 16, 3 * width), low)] * quarters,
+        place,
+        grad_proj,
         grad_up,
-        hat,
+        hat_turned,
         weights_one,
-        table,
         line(ln1_gain),
         line(ln2_gain),
-        scratch=[
-            ((seq_len, 3 * width), low),
-            ((seq_len, width), wide),
-            ((seq_len, width), wide),
-        ],
+        scratch=[((members, half, 3 * width), low)] * 2
+        + [((members, half, units), low)] * 2
+        + [((depth, 3 * width), low)],
+        after=[total],
+        flops=1,
+        memory=60,
     )
     late = messages[:1] + [send(messages[step], "fsdp", step) for step in range(1, quarters)]
-    grad_norm = sum_rows(kept, other)
-
-    lines = part // members
-
-    def share(parts):
-        total = parts[0].shape[1]
-        *pieces, sums = call(
-            lambda *refs: share_kernel(members, quarters, *refs),
-            [((lines + 16, total), low)] * members + [((1, total), wide)],
-            place,
-            *parts,
-        )
-        return pieces[:1] + [send(pieces[step], "context", step) for step in others], sums
-
-    early, sums = share(early)
-    late, _ = share(late)
-
+
+    branches = last_halvings(total)
+    *early, sums = call(
+        lambda *refs: share_early_kernel(members, quarters, *refs),
+        [((lines + 16, width + 2 * units), low)] * members + [((1, width + 2 * units), wide)],
+        place,
+        *early,
+        flops=20 * 10**9,
+    )
+    stay, leave = first_halving(place, kept, other, after=[sums, branches, *late[1:]])
+    leave = send(leave, "context", 1)
+    pieces = call(
+        lambda *refs: share_late_kernel(members, quarters, *refs),
+        [((lines + 16, 4 * width + 2 * units), low)] * members,
+        place,
+        *late,
+        *early,
+        after=[stay],
+        flops=3 * 10**9,
+    )
+    pieces = [pieces[0]] + [send(pieces[step], "context", step) for step in others]
+
+    own = take(tokens, core * half, half).astype(wide)
+    result = both_halves((own + branches + b_out + b_down).astype(low))
+    grad_norm = last_halvings(stay + leave.astype(wide))
     center = own - jnp.mean(own, axis=-1, keepdims=True)
     factor = lax.rsqrt(jnp.mean(center * center, axis=-1, keepdims=True) + EPSILON)
     normed = center * factor
@@ -776,10 +901,11 @@
         - normed * jnp.mean(grad_norm * normed, axis=-1, keepdims=True)
     )
     own_grad = take(cotangent, core * half, half).astype(wide)
-    grad_tokens = both_halves(own_grad + grad_input)
+    grad_half = own_grad + grad_input
+    grad_tokens = both_halves(grad_half)
 
     begin = lax.axis_index("fsdp") * part + here * lines
-    column = lambda values: take(values, begin, lines).reshape(-1, 1)
+    columns = jnp.stack([ln1_gain, ln1_bias, ln2_gain, ln2_bias])
     grad_w_qkv, bias_qkv, grad_w_out, grad_w_up, bias_up, grad_w_down, norms = call(
         lambda *refs: owner_kernel(members, *refs),
         [
@@ -792,14 +918,11 @@
             ((lines, 128), wide),
         ],
         place,
-        *early,
-        *late,
-        take(w_qkv, here * lines, lines),
-        take(w_up, here * lines, lines),
-        column(ln1_gain),
-        column(ln1_bias),
-        column(ln2_gain),
-        column(ln2_bias),
+        *pieces,
+        qkv_rows,
+        up_rows,
+        take(columns, begin, lines, 1).T,
+        after=[leave],
     )
     norms = norms[:, :4].T
     norms = norms + send(norms, "tensor", 1)
@@ -831,7 +954,8 @@
     local_heads = arrays[6].shape[2] // HEAD
     units = arrays[10].shape[1]
     fits = (
-        local_heads % members == 0
+        members > 1
+        and local_heads % members == 0
         and units % members == 0
         and lax.axis_size("tensor") == 2
         and power_of_two(members)

time: 251 us -> 174 us (0.69)
  waiting for transfers between devices: 114 us -> 63.1 us
  starting transfers between devices: 52.8 us -> 37 us
  local copies, waits for them, and re-layouts: 17.7 us -> 10.2 us
    ppermute x41 -> x34, waiting for transfers between devices: 114 us -> 63.1 us  [send(): lax.ppermute(values, axis, [(index, index ^ step) for index in range(size)])]
    ppermute x41 -> x34, starting transfers between devices: 52.8 us -> 37 us  [send(): lax.ppermute(values, axis, [(index, index ^ step) for index in range(size)])]
    reshape x6 -> x0, local copies, waits for them, and re-layouts: 4.41 us -> none  [whole_sequences(): column = lambda values: take(values, begin, lines).reshape(-1, 1)]
    dynamic_slice x4 -> x2, local copies, waits for them, and re-layouts: 5.49 us -> 1.41 us  [take(): return lax.dynamic_slice_in_dim(values, start, size, axis)]
    convert_element_type x2 -> x1, other arithmetic: 2.79 us -> 0.27 us  [whole_sequences(): result = both_halves((own + branches + b_out + b_down).astype(low))]
    pallas_call x8 -> x11, Pallas kernels: 54.7 us -> 52.4 us  [the longest x10 49.1 us: call(): pl.pallas_call(kernel, out_shape=[jax.ShapeDtypeStruct(shape, kind) for s...]
    unnamed x64 -> x78, local copies, waits for them, and re-layouts: 5.33 us -> 6.07 us
  transfers between devices with their start and end apart: 41 -> 34, of which waited for: 16 -> 11; matrix products, arithmetic and copies ran while one was open for 8% -> 7% of each run, Pallas kernels for 11% -> 27%
where the time goes in v2:
time: 174 us
  waiting for transfers between devices  63.1 us (36%)
  Pallas kernels  52.4 us (30%)
  starting transfers between devices  37 us (21%)
  local copies, waits for them, and re-layouts  10.2 us (6%)
  other arithmetic  9.66 us (6%)
    ppermute x34, waiting for transfers between devices, send(): lax.ppermute(values, axis, [(index, index ^ step) for index in range(size)])  63.1 us
    pallas_call x10, Pallas kernels, call(): pl.pallas_call(kernel, out_shape=[jax.ShapeDtypeStruct(shape, kind) for s...  49.1 us
    ppermute x34, starting transfers between devices, send(): lax.ppermute(values, axis, [(index, index ^ step) for index in range(size)])  37 us
    unnamed x78, local copies, waits for them, and re-layouts  6.07 us
  transfers between devices with their start and end apart: 34, of which 11 were waited for; matrix products, arithmetic and copies ran while one was open for 7% of the time, Pallas kernels for 27%

profile of v2, /device:TPU:0, one launch (start us, length us, event | category | flops | bytes accessed | tf_op | source)
XLA Modules:
  0.0 173.5 jit_solution(13698044518136263845)
XLA Ops:
  1.3 3.3 %shard_map.245 = (bf16[128,1024]{1,0:T(8,128)(2,1)}, bf16[128,1024]{1,0:T(8,128)(2,1)}, bf16[256,1536]{1,0:T(8,128)(2,1)}, bf16[3,64,512]{2,1,0:T(8,128)(2,1)}, bf16[64,2048]{1,0:T(8,128)(2,1)}) custom-call(s32[3]{0:T(128)} %pad_add_fusion.place_ref, bf16[256,1024]{1,0:T(8,128)(2,1)} %refs_0_.3, bf16[256,1024]{1,0:T(8,128)(2,1)} %refs_1_.3, ...), custom_call_target="tpu_custom_call" | custom-call | tf_op jit(solution)/shard_map/pallas_call | solution.py:312
  4.6 2.9 %collective-permute-start.6 = (bf16[256,1536]{1,0:T(8,128)(2,1)}, bf16[256,1536]{1,0:T(8,128)(2,1)S(1)}, u32[]{:S(2)}, u32[]{:S(2)}) collective-permute-start(bf16[256,1536]{1,0:T(8,128)(2,1)} %get-tuple-element.62.refs_7_), channel_id=1, source_target_pairs={{0,8},{8,0},{16,24},{24,16},{1,9},{9,1},{17,25},{25,17},{2,10},{10... | collective-permute-start | bytes 2359304 | tf_op jit(solution)/shard_map/ppermute | solution.py:269
  7.5 1.5 collective-permute-start.7
  9.0 2.6 %collective-permute-start.1 = (bf16[128,1024]{1,0:T(8,128)(2,1)}, bf16[128,1024]{1,0:T(8,128)(2,1)}, u32[]{:S(2)}, u32[]{:S(2)}) collective-permute-start(bf16[128,1024]{1,0:T(8,128)(2,1)} %get-tuple-element.61), channel_id=1, source_target_pairs={{0,4},{2,6},{4,0},{6,2},{1,5},{3,7},{5,1},{7,3},{8,12},{10,14},{12... | collective-permute-start | bytes 786440 | tf_op jit(solution)/shard_map/ppermute | solution.py:269
  11.6 1.6 collective-permute-start
  13.9 16.0 %collective-permute-done.1.refs_2_ = bf16[128,1024]{1,0:T(8,128)(2,1)} collective-permute-done((bf16[128,1024]{1,0:T(8,128)(2,1)}, bf16[128,1024]{1,0:T(8,128)(2,1)}, u32[]{:S(2)}, u32[]{:S(2)}) %collective-permute-start.1) | collective-permute-done | bytes 262176 | tf_op jit(solution)/shard_map/ppermute | solution.py:269
  32.2 1.3 pad_maximum_fusion.refs_17_.refs_5_
  33.4 2.0 %collective-permute-start.10 = (bf16[128,1024]{1,0:T(8,128)(2,1)S(1)}, bf16[128,1024]{1,0:T(8,128)(2,1)S(1)}, u32[]{:S(2)}, u32[]{:S(2)}) collective-permute-start(bf16[128,1024]{1,0:T(8,128)(2,1)S(1)} %copy-done.24), channel_id=1, source_target_pairs={{0,2},{2,0},{4,6},{6,4},{1,3},{3,1},{5,7},{7,5},{8,10},{10,8},{12,... | collective-permute-start | bytes 786440 | tf_op jit(solution)/shard_map/ppermute | solution.py:269
  35.5 4.8 %collective-permute-done.2.refs_3_ = bf16[128,1024]{1,0:T(8,128)(2,1)} collective-permute-done((bf16[128,1024]{1,0:T(8,128)(2,1)}, bf16[128,1024]{1,0:T(8,128)(2,1)}, u32[]{:S(2)}, u32[]{:S(2)}) %collective-permute-start.2) | collective-permute-done | bytes 262176 | tf_op jit(solution)/shard_map/ppermute | solution.py:269
  41.4 1.3 dynamic_slice.22
  42.7 1.9 %pad_maximum_fusion.2.refs_10_ = bf16[256,1536]{1,0:T(8,128)(2,1)} fusion(bf16[128,1536]{1,0:T(8,128)(2,1)} %collective-permute-done.9, bf16[128,1536]{1,0:T(8,128)(2,1)S(1)} %collective-permute-done.8), kind=kLoop, calls=%fused_computation.4 | loop fusion | flops 1572864 | bytes 1572864 | tf_op jit(solution)/shard_map/concatenate | solution.py:712
  45.2 3.8 %collective-permute-done.12.refs_4_ = bf16[128,1024]{1,0:T(8,128)(2,1)S(1)} collective-permute-done((bf16[128,1024]{1,0:T(8,128)(2,1)S(1)}, bf16[128,1024]{1,0:T(8,128)(2,1)S(1)}, u32[]{:S(2)}, u32[]{:S(2)}) %collective-permute-start.12) | collective-permute-done | bytes 262176 | tf_op jit(solution)/shard_map/ppermute | solution.py:269
  49.0 0.7 copy-done.28
  49.8 13.1 %shard_map.246 = (bf16[1024,1024]{1,0:T(8,128)(2,1)}, bf16[1024,384]{1,0:T(8,128)(2,1)}, f32[1024,128]{1,0:T(8,128)}, f32[1024,128]{1,0:T(8,128)}, bf16[1024,640...) custom-call(s32[3]{0:T(128)} %pad_add_fusion.place_ref, ...), custom_call_target="tpu_custom_call" | custom-call | flops 12000000000 | tf_op jit(solution)/shard_map/pallas_call | solution.py:290
  62.9 4.5 %shard_map.247 = (f32[4,128,1024]{2,1,0:T(8,128)}, bf16[4,128,1024]{2,1,0:T(8,128)(2,1)}) custom-call(s32[3]{0:T(128)} %pad_add_fusion.place_ref, bf16[1024,640]{1,0:T(8,128)(2,1)} %get-tuple-element.63.refs_0_.refs_9_, bf16[1024,640]{1,0:T(8,128)(2,1)} %get-tuple-element.64.refs_1_.refs_11_), custom_call_target="tpu_custom_call" | custom-call | flops 4000000000 | tf_op jit(solution)/shard_map/pallas_call | solution.py:290
  67.9 0.8 copy-done.32
  68.8 10.8 %shard_map.248 = (bf16[272,1152]{1,0:T(8,128)(2,1)}, bf16[272,1152]{1,0:T(8,128)(2,1)}, bf16[272,1152]{1,0:T(8,128)(2,1)}, bf16[272,1152]{1,0:T(8,128)(2,1)}, bf...) custom-call(s32[3]{0:T(128)} %pad_add_fusion.place_ref, bf16[4,128,1024]{2,1,0:T(8,128)(2,1)} %get-tuple-element.65.refs_0_, ...), custom_call_target="tpu_custom_call" | custom-call | flops 11000000512 | tf_op jit(solution)/shard_map/pallas_call | solution.py:290
  79.6 0.9 copy-done.5
  80.5 1.5 shard_map.249
  82.0 1.0 copy-done.1
  83.8 0.6 collective-permute-start.21
  84.4 2.3 %collective-permute-start.22 = (bf16[272,1152]{1,0:T(8,128)(2,1)}, bf16[272,1152]{1,0:T(8,128)(2,1)S(1)}, u32[]{:S(2)}, u32[]{:S(2)}) collective-permute-start(bf16[272,1152]{1,0:T(8,128)(2,1)} %get-tuple-element.76), channel_id=1, source_target_pairs={{0,24},{8,16},{16,8},{24,0},{1,25},{9,17},{17,9},{25,1},{2,26},{10... | collective-permute-start | bytes 1880072 | tf_op jit(solution)/shard_map/ppermute | solution.py:269
  87.1 7.7 %shard_map.251.refs_1_ = bf16[1024,384]{1,0:T(8,128)(2,1)} custom-call(s32[3]{0:T(128)} %pad_add_fusion.place_ref, f32[2,128,1024]{2,1,0:T(8,128)} %copy-done.1, bf16[1024,384]{1,0:T(8,128)(2,1)} %get-tuple-element.78.refs_1_, f32[1024,128]{1,0:T(8,128)} %get-tuple-element.79.refs_2_, f32[1024,128]{1,0:T(8,128)} %get-tuple-element.80.refs_3_, ...), custom_call_target="tpu_custom_call" | custom-call | flops 1 | tf_op jit(solution)/shard_map/pallas_call | solution.py:290
  94.8 2.4 %collective-permute-done.17 = bf16[2,128,1024]{2,1,0:T(8,128)(2,1)} collective-permute-done((bf16[2,128,1024]{2,1,0:T(8,128)(2,1)}, bf16[2,128,1024]{2,1,0:T(8,128)(2,1)}, u32[]{:S(2)}, u32[]{:S(2)}) %collective-permute-start.17) | collective-permute-done | bytes 524320 | tf_op jit(solution)/shard_map/ppermute | solution.py:269
  97.2 2.2 %convert_add_fusion.1.refs_0_ = f32[2,128,1024]{2,1,0:T(8,128)} fusion(f32[2,128,1024]{2,1,0:T(8,128)S(1)} %copy-done.2, bf16[2,128,1024]{2,1,0:T(8,128)(2,1)} %collective-permute-done.17), kind=kLoop, calls=%fused_computation.3 | loop fusion | flops 524288 | bytes 2621440 | tf_op jit(solution)/shard_map/add | solution.py:850
  99.4 7.2 %shard_map.252 = (f32[4,128,1024]{2,1,0:T(8,128)}, bf16[4,128,1024]{2,1,0:T(8,128)(2,1)}, bf16[272,384]{1,0:T(8,128)(2,1)}, bf16[272,384]{1,0:T(8,128)(2,1)}, bf...) custom-call(s32[3]{0:T(128)} %pad_add_fusion.place_ref, f32[2,128,1024]{2,1,0:T(8,128)} %convert_add_fusion.1.refs_0_, ...), custom_call_target="tpu_custom_call" | custom-call | flops 1 | tf_op jit(solution)/shard_map/pallas_call | solution.py:290
  106.5 1.1 slice.80
  107.7 3.3 %collective-permute-start.18 = (bf16[1,128,1024]{2,1,0:T(8,128)(2,1)S(1)}, bf16[1,128,1024]{2,1,0:T(8,128)(2,1)S(1)}, u32[]{:S(2)}, u32[]{:S(2)}) collective-permute-start(bf16[1,128,1024]{2,1,0:T(8,128)(2,1)S(1)} %slice.80), channel_id=1, source_target_pairs={{0,4},{2,6},{4,0},{6,2},{1,5},{3,7},{5,1},{7,3},{8,12},{10,14},{12... | collective-permute-start | bytes 786440 | tf_op jit(solution)/shard_map/ppermute | solution.py:269
  111.0 2.0 %collective-permute-done.21.refs_2_ = bf16[272,1152]{1,0:T(8,128)(2,1)S(1)} collective-permute-done((bf16[272,1152]{1,0:T(8,128)(2,1)}, bf16[272,1152]{1,0:T(8,128)(2,1)S(1)}, u32[]{:S(2)}, u32[]{:S(2)}) %collective-permute-start.21) | collective-permute-done | bytes 626720 | tf_op jit(solution)/shard_map/ppermute | solution.py:269
  113.0 1.1 copy-done.11
  114.1 0.9 shard_map.250
  115.0 1.6 collective-permute-start.23
  117.1 1.5 collective-permute-start.25
  118.5 5.0 %collective-permute-done.18 = bf16[1,128,1024]{2,1,0:T(8,128)(2,1)S(1)} collective-permute-done((bf16[1,128,1024]{2,1,0:T(8,128)(2,1)S(1)}, bf16[1,128,1024]{2,1,0:T(8,128)(2,1)S(1)}, u32[]{:S(2)}, u32[]{:S(2)}) %collective-permute-start.18) | collective-permute-done | bytes 262176 | tf_op jit(solution)/shard_map/ppermute | solution.py:269
  123.8 2.8 %collective-permute-done.24.refs_3_ = bf16[272,384]{1,0:T(8,128)(2,1)S(1)} collective-permute-done((bf16[272,384]{1,0:T(8,128)(2,1)S(1)}, bf16[272,384]{1,0:T(8,128)(2,1)S(1)}, u32[]{:S(2)}, u32[]{:S(2)}) %collective-permute-start.24) | collective-permute-done | bytes 208928 | tf_op jit(solution)/shard_map/ppermute | solution.py:269
  126.6 0.7 shard_map.253
  127.3 1.8 %collective-permute-start.27 = (bf16[2,128,1024]{2,1,0:T(8,128)(2,1)S(1)}, bf16[2,128,1024]{2,1,0:T(8,128)(2,1)S(1)}, u32[]{:S(2)}, u32[]{:S(2)}) collective-permute-start(bf16[2,128,1024]{2,1,0:T(8,128)(2,1)S(1)} %get-tuple-element.89), channel_id=1, source_target_pairs={{0,2},{2,0},{4,6},{6,4},{1,3},{3,1},{5,7},{7,5},{8,10},{10,8},{12,... | collective-permute-start | bytes 1572872 | tf_op jit(solution)/shard_map/ppermute | solution.py:269
  129.2 0.7 shard_map.254
  130.3 4.7 %collective-permute-start.31 = (bf16[80,1536]{1,0:T(8,128)(2,1)S(1)}, bf16[80,1536]{1,0:T(8,128)(2,1)S(1)}, u32[]{:S(2)}, u32[]{:S(2)}) collective-permute-start(bf16[80,1536]{1,0:T(8,128)(2,1)S(1)} %get-tuple-element.97), channel_id=1, source_target_pairs={{0,4},{2,6},{4,0},{6,2},{1,5},{3,7},{5,1},{7,3},{8,12},{10,14},{12... | collective-permute-start | bytes 737288 | tf_op jit(solution)/shard_map/ppermute | solution.py:269
  134.9 11.7 %collective-permute-done.27.refs_0_ = bf16[2,128,1024]{2,1,0:T(8,128)(2,1)S(1)} collective-permute-done((bf16[2,128,1024]{2,1,0:T(8,128)(2,1)S(1)}, bf16[2,128,1024]{2,1,0:T(8,128)(2,1)S(1)}, u32[]{:S(2)}, u32[]{:S(2)}) %collective-permute-start.27) | collective-permute-done | bytes 524320 | tf_op jit(solution)/shard_map/ppermute | solution.py:269
  146.8 5.2 %collective-permute-start.28 = (bf16[1,128,1024]{2,1,0:T(8,128)(2,1)S(1)}, bf16[1,128,1024]{2,1,0:T(8,128)(2,1)S(1)}, u32[]{:S(2)}, u32[]{:S(2)}) collective-permute-start(bf16[1,128,1024]{2,1,0:T(8,128)(2,1)S(1)} %slice.79), channel_id=1, source_target_pairs={{0,4},{2,6},{4,0},{6,2},{1,5},{3,7},{5,1},{7,3},{8,12},{10,14},{12... | collective-permute-start | bytes 786440 | tf_op jit(solution)/shard_map/ppermute | solution.py:269
  152.2 9.3 %collective-permute-done.32.refs_4_ = bf16[80,1536]{1,0:T(8,128)(2,1)S(1)} collective-permute-done((bf16[80,1536]{1,0:T(8,128)(2,1)S(1)}, bf16[80,1536]{1,0:T(8,128)(2,1)S(1)}, u32[]{:S(2)}, u32[]{:S(2)}) %collective-permute-start.32) | collective-permute-done | bytes 245792 | tf_op jit(solution)/shard_map/ppermute | solution.py:269
  161.5 2.1 %shard_map.255 = (f32[3,64,512]{2,1,0:T(8,128)}, f32[3,512]{1,0:T(4,128)}, f32[64,512]{1,0:T(8,128)}, f32[64,2048]{1,0:T(8,128)}, f32[1,2048]{1,0:T(1,128)}, /*index=5*/f32[64,2048]{1,0:T(8,128)}, f32[64,128]{1,0:T(8,128)S(1)}) custom-call(s32[3]{0:T(128)S(1)} %copy-done.7, bf16[2,128,1024]{2,1,0:T(8,128)(2,1)S(1)} %collective-permute-done.27.refs_0_, ...), custom_call_target="tpu_custom_call" | custom-call | flops 1000000000 | tf_op jit(solution)/shard_map/pallas_call | solution.py:290
  163.6 4.8 %collective-permute-done.28 = bf16[1,128,1024]{2,1,0:T(8,128)(2,1)S(1)} collective-permute-done((bf16[1,128,1024]{2,1,0:T(8,128)(2,1)S(1)}, bf16[1,128,1024]{2,1,0:T(8,128)(2,1)S(1)}, u32[]{:S(2)}, u32[]{:S(2)}) %collective-permute-start.28) | collective-permute-done | bytes 262176 | tf_op jit(solution)/shard_map/ppermute | solution.py:269
  169.7 0.8 pad_maximum_fusion.3
  170.5 0.6 collective-permute-done.33
  171.1 0.7 slice_reduce_fusion
  172.0 1.0 pad_maximum_fusion.1
  (152 shorter events, 10.4 us)
Async XLA Ops:
  0.6 40.2 %copy-start = (f32[3,512]{1,0:T(4,128)S(1)}, f32[3,512]{1,0:T(4,128)}, u32[]{:S(2)}) copy-start(f32[3,512]{1,0:T(4,128)} %param.21) | copy-start | bytes 18436
  4.6 25.4 %collective-permute-start.6 = (bf16[256,1536]{1,0:T(8,128)(2,1)}, bf16[256,1536]{1,0:T(8,128)(2,1)S(1)}, u32[]{:S(2)}, u32[]{:S(2)}) collective-permute-start(bf16[256,1536]{1,0:T(8,128)(2,1)} %get-tuple-element.62.refs_7_), channel_id=1, source_target_pairs={{0,8},{8,0},{16,24},{24,16},{1,9},{9,1},{17,25},{25,17},{2,10},{10... | collective-permute-start | bytes 2359304 | tf_op jit(solution)/shard_map/ppermute | solution.py:269
  7.5 23.0 %collective-permute-start.7 = (bf16[256,1536]{1,0:T(8,128)(2,1)}, bf16[256,1536]{1,0:T(8,128)(2,1)S(1)}, u32[]{:S(2)}, u32[]{:S(2)}) collective-permute-start(bf16[256,1536]{1,0:T(8,128)(2,1)} %get-tuple-element.62.refs_7_), channel_id=1, source_target_pairs={{0,16},{8,24},{16,0},{24,8},{1,17},{9,25},{17,1},{25,9},{2,18},{10... | collective-permute-start | bytes 2359304 | tf_op jit(solution)/shard_map/ppermute | solution.py:269
  9.0 20.9 %collective-permute-start.1 = (bf16[128,1024]{1,0:T(8,128)(2,1)}, bf16[128,1024]{1,0:T(8,128)(2,1)}, u32[]{:S(2)}, u32[]{:S(2)}) collective-permute-start(bf16[128,1024]{1,0:T(8,128)(2,1)} %get-tuple-element.61), channel_id=1, source_target_pairs={{0,4},{2,6},{4,0},{6,2},{1,5},{3,7},{5,1},{7,3},{8,12},{10,14},{12... | collective-permute-start | bytes 786440 | tf_op jit(solution)/shard_map/ppermute | solution.py:269
  11.6 21.8 %collective-permute-start = (bf16[128,1024]{1,0:T(8,128)(2,1)}, bf16[128,1024]{1,0:T(8,128)(2,1)}, u32[]{:S(2)}, u32[]{:S(2)}) collective-permute-start(bf16[128,1024]{1,0:T(8,128)(2,1)} %get-tuple-element.61), channel_id=1, source_target_pairs={{0,2},{2,0},{4,6},{6,4},{1,3},{3,1},{5,7},{7,5},{8,10},{10,8},{12,... | collective-permute-start | bytes 786440 | tf_op jit(solution)/shard_map/ppermute | solution.py:269
  13.2 22.3 %collective-permute-start.11 = (bf16[128,1024]{1,0:T(8,128)(2,1)}, bf16[128,1024]{1,0:T(8,128)(2,1)S(1)}, u32[]{:S(2)}, u32[]{:S(2)}) collective-permute-start(bf16[128,1024]{1,0:T(8,128)(2,1)} %get-tuple-element.66), channel_id=1, source_target_pairs={{0,4},{2,6},{4,0},{6,2},{1,5},{3,7},{5,1},{7,3},{8,12},{10,14},{12... | collective-permute-start | bytes 786440 | tf_op jit(solution)/shard_map/ppermute | solution.py:269
  29.9 10.3 %collective-permute-start.2 = (bf16[128,1024]{1,0:T(8,128)(2,1)}, bf16[128,1024]{1,0:T(8,128)(2,1)}, u32[]{:S(2)}, u32[]{:S(2)}) collective-permute-start(bf16[128,1024]{1,0:T(8,128)(2,1)} %collective-permute-done.1.refs_2_), channel_id=1, source_target_pairs={{0,2},{2,0},{4,6},{6,4},{1,3},{3,1},{5,7},{7,5},{8,10},{10,8},{12,... | collective-permute-start | bytes 786440 | tf_op jit(solution)/shard_map/ppermute | solution.py:269
  30.0 10.3 %collective-permute-start.8 = (bf16[128,1536]{1,0:T(8,128)(2,1)S(1)}, bf16[128,1536]{1,0:T(8,128)(2,1)S(1)}, u32[]{:S(2)}, u32[]{:S(2)}) collective-permute-start(bf16[128,1536]{1,0:T(8,128)(2,1)S(1)} %slice.50), channel_id=1, source_target_pairs={{0,16},{8,24},{16,0},{24,8},{1,17},{9,25},{17,1},{25,9},{2,18},{10... | collective-permute-start | bytes 1179656 | tf_op jit(solution)/shard_map/ppermute | solution.py:269
  30.6 9.7 %collective-permute-start.9 = (bf16[128,1536]{1,0:T(8,128)(2,1)S(1)}, bf16[128,1536]{1,0:T(8,128)(2,1)}, u32[]{:S(2)}, u32[]{:S(2)}) collective-permute-start(bf16[128,1536]{1,0:T(8,128)(2,1)S(1)} %slice.51), channel_id=1, source_target_pairs={{0,8},{8,0},{16,24},{24,16},{1,9},{9,1},{17,25},{25,17},{2,10},{10... | collective-permute-start | bytes 1179656 | tf_op jit(solution)/shard_map/ppermute | solution.py:269
  33.4 11.2 %collective-permute-start.10 = (bf16[128,1024]{1,0:T(8,128)(2,1)S(1)}, bf16[128,1024]{1,0:T(8,128)(2,1)S(1)}, u32[]{:S(2)}, u32[]{:S(2)}) collective-permute-start(bf16[128,1024]{1,0:T(8,128)(2,1)S(1)} %copy-done.24), channel_id=1, source_target_pairs={{0,2},{2,0},{4,6},{6,4},{1,3},{3,1},{5,7},{7,5},{8,10},{10,8},{12,... | collective-permute-start | bytes 786440 | tf_op jit(solution)/shard_map/ppermute | solution.py:269
  35.5 27.4 %copy-start.23 = (bf16[128,1024]{1,0:T(8,128)(2,1)}, bf16[128,1024]{1,0:T(8,128)(2,1)S(1)}, u32[]{:S(2)}) copy-start(bf16[128,1024]{1,0:T(8,128)(2,1)S(1)} %collective-permute-done.11.refs_3_) | copy-start | bytes 786436
  35.5 9.3 %collective-permute-start.4 = (bf16[128,1024]{1,0:T(8,128)(2,1)}, bf16[128,1024]{1,0:T(8,128)(2,1)S(1)}, u32[]{:S(2)}, u32[]{:S(2)}) collective-permute-start(bf16[128,1024]{1,0:T(8,128)(2,1)} %collective-permute-done.1.refs_2_), channel_id=1, source_target_pairs={{0,1},{1,0},{2,3},{3,2},{4,5},{5,4},{6,7},{7,6},{8,9},{9,8},{10,11... | collective-permute-start | bytes 786440 | tf_op jit(solution)/shard_map/ppermute | solution.py:269
  40.2 8.7 %collective-permute-start.3 = (bf16[128,1024]{1,0:T(8,128)(2,1)}, bf16[128,1024]{1,0:T(8,128)(2,1)S(1)}, u32[]{:S(2)}, u32[]{:S(2)}) collective-permute-start(bf16[128,1024]{1,0:T(8,128)(2,1)} %collective-permute-done.refs_1_), channel_id=1, source_target_pairs={{0,1},{1,0},{2,3},{3,2},{4,5},{5,4},{6,7},{7,6},{8,9},{9,8},{10,11... | collective-permute-start | bytes 786440 | tf_op jit(solution)/shard_map/ppermute | solution.py:269
  40.2 8.7 %collective-permute-start.12 = (bf16[128,1024]{1,0:T(8,128)(2,1)S(1)}, bf16[128,1024]{1,0:T(8,128)(2,1)S(1)}, u32[]{:S(2)}, u32[]{:S(2)}) collective-permute-start(bf16[128,1024]{1,0:T(8,128)(2,1)S(1)} %collective-permute-done.11.refs_3_), channel_id=1, source_target_pairs={{0,2},{2,0},{4,6},{6,4},{1,3},{3,1},{5,7},{7,5},{8,10},{10,8},{12,... | collective-permute-start | bytes 786440 | tf_op jit(solution)/shard_map/ppermute | solution.py:269
  40.3 8.7 %collective-permute-start.5 = (bf16[128,1024]{1,0:T(8,128)(2,1)}, bf16[128,1024]{1,0:T(8,128)(2,1)S(1)}, u32[]{:S(2)}, u32[]{:S(2)}) collective-permute-start(bf16[128,1024]{1,0:T(8,128)(2,1)} %collective-permute-done.2.refs_3_), channel_id=1, source_target_pairs={{0,1},{1,0},{2,3},{3,2},{4,5},{5,4},{6,7},{7,6},{8,9},{9,8},{10,11... | collective-permute-start | bytes 786440 | tf_op jit(solution)/shard_map/ppermute | solution.py:269
  44.7 18.2 %copy-start.25 = (bf16[128,1024]{1,0:T(8,128)(2,1)}, bf16[128,1024]{1,0:T(8,128)(2,1)S(1)}, u32[]{:S(2)}) copy-start(bf16[128,1024]{1,0:T(8,128)(2,1)S(1)} %collective-permute-done.10.refs_2_) | copy-start | bytes 786436
  44.7 23.2 %collective-permute-start.14 = (bf16[128,1024]{1,0:T(8,128)(2,1)S(1)}, bf16[128,1024]{1,0:T(8,128)(2,1)S(1)}, u32[]{:S(2)}, u32[]{:S(2)}) collective-permute-start(bf16[128,1024]{1,0:T(8,128)(2,1)S(1)} %collective-permute-done.11.refs_3_), channel_id=1, source_target_pairs={{0,1},{1,0},{2,3},{3,2},{4,5},{5,4},{6,7},{7,6},{8,9},{9,8},{10,11... | collective-permute-start | bytes 786440 | tf_op jit(solution)/shard_map/ppermute | solution.py:269
  44.7 23.2 %collective-permute-start.13 = (bf16[128,1024]{1,0:T(8,128)(2,1)S(1)}, bf16[128,1024]{1,0:T(8,128)(2,1)S(1)}, u32[]{:S(2)}, u32[]{:S(2)}) collective-permute-start(bf16[128,1024]{1,0:T(8,128)(2,1)S(1)} %collective-permute-done.10.refs_2_), channel_id=1, source_target_pairs={{0,1},{1,0},{2,3},{3,2},{4,5},{5,4},{6,7},{7,6},{8,9},{9,8},{10,11... | collective-permute-start | bytes 786440 | tf_op jit(solution)/shard_map/ppermute | solution.py:269
  49.0 13.9 %copy-start.26 = (bf16[128,1024]{1,0:T(8,128)(2,1)}, bf16[128,1024]{1,0:T(8,128)(2,1)S(1)}, u32[]{:S(2)}) copy-start(bf16[128,1024]{1,0:T(8,128)(2,1)S(1)} %collective-permute-done.12.refs_4_) | copy-start | bytes 786436
  49.0 18.9 %collective-permute-start.15 = (bf16[128,1024]{1,0:T(8,128)(2,1)S(1)}, bf16[128,1024]{1,0:T(8,128)(2,1)S(1)}, u32[]{:S(2)}, u32[]{:S(2)}) collective-permute-start(bf16[128,1024]{1,0:T(8,128)(2,1)S(1)} %collective-permute-done.12.refs_4_), channel_id=1, source_target_pairs={{0,1},{1,0},{2,3},{3,2},{4,5},{5,4},{6,7},{7,6},{8,9},{9,8},{10,11... | collective-permute-start | bytes 786440 | tf_op jit(solution)/shard_map/ppermute | solution.py:269
  67.4 12.1 %collective-permute-start.16 = (bf16[4,128,1024]{2,1,0:T(8,128)(2,1)}, bf16[4,128,1024]{2,1,0:T(8,128)(2,1)S(1)}, u32[]{:S(2)}, u32[]{:S(2)}) collective-permute-start(bf16[4,128,1024]{2,1,0:T(8,128)(2,1)} %get-tuple-element.65.refs_0_), channel_id=1, source_target_pairs={{0,1},{1,0},{2,3},{3,2},{4,5},{5,4},{6,7},{7,6},{8,9},{9,8},{10,11... | collective-permute-start | bytes 3145736 | tf_op jit(solution)/shard_map/ppermute | solution.py:269
  68.8 10.8 %copy-start.4 = (f32[4,128,1024]{2,1,0:T(8,128)S(1)}, f32[4,128,1024]{2,1,0:T(8,128)}, u32[]{:S(2)}) copy-start(f32[4,128,1024]{2,1,0:T(8,128)} %get-tuple-element.70.refs_1_) | copy-start | bytes 6291460
  68.8 10.8 %copy-start.6 = (s32[3]{0:T(128)S(1)}, s32[3]{0:T(128)}, u32[]{:S(2)}) copy-start(s32[3]{0:T(128)} %pad_add_fusion.place_ref) | copy-start | bytes 40
  83.0 14.2 %collective-permute-start.17 = (bf16[2,128,1024]{2,1,0:T(8,128)(2,1)}, bf16[2,128,1024]{2,1,0:T(8,128)(2,1)}, u32[]{:S(2)}, u32[]{:S(2)}) collective-permute-start(bf16[2,128,1024]{2,1,0:T(8,128)(2,1)} %get-tuple-element.72), channel_id=1, source_target_pairs={{0,2},{2,0},{4,6},{6,4},{1,3},{3,1},{5,7},{7,5},{8,10},{10,8},{12,... | collective-permute-start | bytes 1572872 | tf_op jit(solution)/shard_map/ppermute | solution.py:269
  83.3 27.7 %collective-permute-start.20 = (bf16[272,1152]{1,0:T(8,128)(2,1)}, bf16[272,1152]{1,0:T(8,128)(2,1)S(1)}, u32[]{:S(2)}, u32[]{:S(2)}) collective-permute-start(bf16[272,1152]{1,0:T(8,128)(2,1)} %get-tuple-element.74), channel_id=1, source_target_pairs={{0,8},{8,0},{16,24},{24,16},{1,9},{9,1},{17,25},{25,17},{2,10},{10... | collective-permute-start | bytes 1880072 | tf_op jit(solution)/shard_map/ppermute | solution.py:269
  83.8 29.2 %collective-permute-start.21 = (bf16[272,1152]{1,0:T(8,128)(2,1)}, bf16[272,1152]{1,0:T(8,128)(2,1)S(1)}, u32[]{:S(2)}, u32[]{:S(2)}) collective-permute-start(bf16[272,1152]{1,0:T(8,128)(2,1)} %get-tuple-element.75), channel_id=1, source_target_pairs={{0,16},{8,24},{16,0},{24,8},{1,17},{9,25},{17,1},{25,9},{2,18},{10... | collective-permute-start | bytes 1880072 | tf_op jit(solution)/shard_map/ppermute | solution.py:269
  84.4 28.5 %collective-permute-start.22 = (bf16[272,1152]{1,0:T(8,128)(2,1)}, bf16[272,1152]{1,0:T(8,128)(2,1)S(1)}, u32[]{:S(2)}, u32[]{:S(2)}) collective-permute-start(bf16[272,1152]{1,0:T(8,128)(2,1)} %get-tuple-element.76), channel_id=1, source_target_pairs={{0,24},{8,16},{16,8},{24,0},{1,25},{9,17},{17,9},{25,1},{2,26},{10... | collective-permute-start | bytes 1880072 | tf_op jit(solution)/shard_map/ppermute | solution.py:269
  87.1 10.1 %copy-start.2 = (f32[2,128,1024]{2,1,0:T(8,128)S(1)}, f32[2,128,1024]{2,1,0:T(8,128)}, u32[]{:S(2)}) copy-start(f32[2,128,1024]{2,1,0:T(8,128)} %copy-done.1) | copy-start | bytes 3145732
  99.4 13.6 %copy-start.7 = (s32[3]{0:T(128)S(1)}, s32[3]{0:T(128)}, u32[]{:S(2)}) copy-start(s32[3]{0:T(128)} %pad_add_fusion.place_ref) | copy-start | bytes 40
  107.6 18.9 %collective-permute-start.26 = (bf16[4,128,1024]{2,1,0:T(8,128)(2,1)}, bf16[4,128,1024]{2,1,0:T(8,128)(2,1)S(1)}, u32[]{:S(2)}, u32[]{:S(2)}) collective-permute-start(bf16[4,128,1024]{2,1,0:T(8,128)(2,1)} %get-tuple-element.87), channel_id=1, source_target_pairs={{0,1},{1,0},{2,3},{3,2},{4,5},{5,4},{6,7},{7,6},{8,9},{9,8},{10,11... | collective-permute-start | bytes 3145736 | tf_op jit(solution)/shard_map/ppermute | solution.py:269
  107.7 15.8 %collective-permute-start.18 = (bf16[1,128,1024]{2,1,0:T(8,128)(2,1)S(1)}, bf16[1,128,1024]{2,1,0:T(8,128)(2,1)S(1)}, u32[]{:S(2)}, u32[]{:S(2)}) collective-permute-start(bf16[1,128,1024]{2,1,0:T(8,128)(2,1)S(1)} %slice.80), channel_id=1, source_target_pairs={{0,4},{2,6},{4,0},{6,2},{1,5},{3,7},{5,1},{7,3},{8,12},{10,14},{12... | collective-permute-start | bytes 786440 | tf_op jit(solution)/shard_map/ppermute | solution.py:269
  114.0 9.4 %copy-start.12 = (f32[2,128,1024]{2,1,0:T(8,128)S(1)}, f32[2,128,1024]{2,1,0:T(8,128)}, u32[]{:S(2)}) copy-start(f32[2,128,1024]{2,1,0:T(8,128)} %convert_add_fusion.1.refs_0_) | copy-start | bytes 3145732
  114.1 9.4 %copy-start.19 = (f32[1024]{0:T(1024)S(1)}, f32[1024]{0:T(1024)}, u32[]{:S(2)}) copy-start(f32[1024]{0:T(1024)} %param.27) | copy-start | bytes 12292
  114.1 12.5 %copy-start.3 = (f32[4,128,1024]{2,1,0:T(8,128)S(1)}, f32[4,128,1024]{2,1,0:T(8,128)}, u32[]{:S(2)}) copy-start(f32[4,128,1024]{2,1,0:T(8,128)} %get-tuple-element.86.refs_5_) | copy-start | bytes 6291460
  115.0 8.8 %collective-permute-start.23 = (bf16[272,384]{1,0:T(8,128)(2,1)S(1)}, bf16[272,384]{1,0:T(8,128)(2,1)S(1)}, u32[]{:S(2)}, u32[]{:S(2)}) collective-permute-start(bf16[272,384]{1,0:T(8,128)(2,1)S(1)} %copy-done.35), channel_id=1, source_target_pairs={{0,8},{8,0},{16,24},{24,16},{1,9},{9,1},{17,25},{25,17},{2,10},{10... | collective-permute-start | bytes 626696 | tf_op jit(solution)/shard_map/ppermute | solution.py:269
  116.5 10.0 %collective-permute-start.24 = (bf16[272,384]{1,0:T(8,128)(2,1)S(1)}, bf16[272,384]{1,0:T(8,128)(2,1)S(1)}, u32[]{:S(2)}, u32[]{:S(2)}) collective-permute-start(bf16[272,384]{1,0:T(8,128)(2,1)S(1)} %copy-done.34), channel_id=1, source_target_pairs={{0,16},{8,24},{16,0},{24,8},{1,17},{9,25},{17,1},{25,9},{2,18},{10... | collective-permute-start | bytes 626696 | tf_op jit(solution)/shard_map/ppermute | solution.py:269
  117.1 9.5 %collective-permute-start.25 = (bf16[272,384]{1,0:T(8,128)(2,1)S(1)}, bf16[272,384]{1,0:T(8,128)(2,1)S(1)}, u32[]{:S(2)}, u32[]{:S(2)}) collective-permute-start(bf16[272,384]{1,0:T(8,128)(2,1)S(1)} %copy-done.33), channel_id=1, source_target_pairs={{0,24},{8,16},{16,8},{24,0},{1,25},{9,17},{17,9},{25,1},{2,26},{10... | collective-permute-start | bytes 626696 | tf_op jit(solution)/shard_map/ppermute | solution.py:269
  127.3 19.4 %collective-permute-start.27 = (bf16[2,128,1024]{2,1,0:T(8,128)(2,1)S(1)}, bf16[2,128,1024]{2,1,0:T(8,128)(2,1)S(1)}, u32[]{:S(2)}, u32[]{:S(2)}) collective-permute-start(bf16[2,128,1024]{2,1,0:T(8,128)(2,1)S(1)} %get-tuple-element.89), channel_id=1, source_target_pairs={{0,2},{2,0},{4,6},{6,4},{1,3},{3,1},{5,7},{7,5},{8,10},{10,8},{12,... | collective-permute-start | bytes 1572872 | tf_op jit(solution)/shard_map/ppermute | solution.py:269
  129.2 43.8 %copy-start.36 = (f32[64]{0:T(128)}, f32[64]{0:T(128)S(1)}, u32[]{:S(2)}) copy-start(f32[64]{0:T(128)S(1)} %fusion.18) | copy-start | bytes 772
  129.2 22.9 %collective-permute-start.19 = (bf16[128,1024]{1,0:T(8,128)(2,1)S(1)}, bf16[128,1024]{1,0:T(8,128)(2,1)S(1)}, u32[]{:S(2)}, u32[]{:S(2)}) collective-permute-start(bf16[128,1024]{1,0:T(8,128)(2,1)S(1)} %get-tuple-element.112), channel_id=1, source_target_pairs={{0,1},{1,0},{2,3},{3,2},{4,5},{5,4},{6,7},{7,6},{8,9},{9,8},{10,11... | collective-permute-start | bytes 786440 | tf_op jit(solution)/shard_map/ppermute | solution.py:269
  129.9 22.3 %collective-permute-start.30 = (bf16[80,1536]{1,0:T(8,128)(2,1)S(1)}, bf16[80,1536]{1,0:T(8,128)(2,1)S(1)}, u32[]{:S(2)}, u32[]{:S(2)}) collective-permute-start(bf16[80,1536]{1,0:T(8,128)(2,1)S(1)} %get-tuple-element.96), channel_id=1, source_target_pairs={{0,2},{2,0},{4,6},{6,4},{1,3},{3,1},{5,7},{7,5},{8,10},{10,8},{12,... | collective-permute-start | bytes 737288 | tf_op jit(solution)/shard_map/ppermute | solution.py:269
  130.3 21.9 %collective-permute-start.31 = (bf16[80,1536]{1,0:T(8,128)(2,1)S(1)}, bf16[80,1536]{1,0:T(8,128)(2,1)S(1)}, u32[]{:S(2)}, u32[]{:S(2)}) collective-permute-start(bf16[80,1536]{1,0:T(8,128)(2,1)S(1)} %get-tuple-element.97), channel_id=1, source_target_pairs={{0,4},{2,6},{4,0},{6,2},{1,5},{3,7},{5,1},{7,3},{8,12},{10,14},{12... | collective-permute-start | bytes 737288 | tf_op jit(solution)/shard_map/ppermute | solution.py:269
  134.9 26.6 %copy-start.8 = (bf16[64,2048]{1,0:T(8,128)(2,1)S(1)}, bf16[64,2048]{1,0:T(8,128)(2,1)}, u32[]{:S(2)}) copy-start(bf16[64,2048]{1,0:T(8,128)(2,1)} %get-tuple-element.100.refs_6_) | copy-start | bytes 786436
  134.9 26.6 %copy-start.10 = (bf16[3,64,512]{2,1,0:T(8,128)(2,1)S(1)}, bf16[3,64,512]{2,1,0:T(8,128)(2,1)}, u32[]{:S(2)}) copy-start(bf16[3,64,512]{2,1,0:T(8,128)(2,1)} %get-tuple-element.99.refs_5_) | copy-start | bytes 589828
  134.9 26.6 %collective-permute-start.32 = (bf16[80,1536]{1,0:T(8,128)(2,1)S(1)}, bf16[80,1536]{1,0:T(8,128)(2,1)S(1)}, u32[]{:S(2)}, u32[]{:S(2)}) collective-permute-start(bf16[80,1536]{1,0:T(8,128)(2,1)S(1)} %get-tuple-element.98), channel_id=1, source_target_pairs={{0,6},{2,4},{4,2},{6,0},{1,7},{3,5},{5,3},{7,1},{8,14},{10,12},{12... | collective-permute-start | bytes 737288 | tf_op jit(solution)/shard_map/ppermute | solution.py:269
  146.8 21.5 %collective-permute-start.28 = (bf16[1,128,1024]{2,1,0:T(8,128)(2,1)S(1)}, bf16[1,128,1024]{2,1,0:T(8,128)(2,1)S(1)}, u32[]{:S(2)}, u32[]{:S(2)}) collective-permute-start(bf16[1,128,1024]{2,1,0:T(8,128)(2,1)S(1)} %slice.79), channel_id=1, source_target_pairs={{0,4},{2,6},{4,0},{6,2},{1,5},{3,7},{5,1},{7,3},{8,12},{10,14},{12... | collective-permute-start | bytes 786440 | tf_op jit(solution)/shard_map/ppermute | solution.py:269
  169.1 2.8 %collective-permute-start.29 = (f32[128,1024]{1,0:T(8,128)S(1)}, f32[128,1024]{1,0:T(8,128)S(1)}, u32[]{:S(2)}, u32[]{:S(2)}) collective-permute-start(f32[128,1024]{1,0:T(8,128)S(1)} %fusion.7), channel_id=1, source_target_pairs={{0,1},{1,0},{2,3},{3,2},{4,5},{5,4},{6,7},{7,6},{8,9},{9,8},{10,11... | collective-permute-start | bytes 1572872 | tf_op jit(solution)/shard_map/ppermute | solution.py:269
  169.2 1.9 %collective-permute-start.33 = (f32[4,64]{0,1:T(8,128)S(1)}, f32[4,64]{0,1:T(8,128)S(1)}, u32[]{:S(2)}, u32[]{:S(2)}) collective-permute-start(f32[4,64]{0,1:T(8,128)S(1)} %slice_bitcast_fusion), channel_id=1, source_target_pairs={{0,1},{1,0},{2,3},{3,2},{4,5},{5,4},{6,7},{7,6},{8,9},{9,8},{10,11... | collective-permute-start | bytes 3080 | tf_op jit(solution)/shard_map/ppermute | solution.py:269
  (23 other events, 70.0 us)

commit v3 on v2

--- a/solution.py
+++ b/solution.py
@@ -281,23 +281,44 @@
     )
 
 
-def call(body, outs, place, *arrays, scratch=(), after=(), flops=10**9, memory=16):
+def call(body, outs, place, *arrays, scratch=(), after=(), far=(), copies=0, flops=10**9, memory=16):
     skipped = len(after)
+    anywhere = pl.BlockSpec(memory_space=pl.ANY)
+    near = pl.BlockSpec(memory_space=pltpu.VMEM)
 
     def kernel(place_ref, *refs):
         body(place_ref, *refs[skipped:])
 
+    scratch_shapes = [pltpu.VMEM(shape, kind) for shape, kind in scratch]
+    if copies:
+        scratch_shapes.append(pltpu.SemaphoreType.DMA((copies,)))
     return pl.pallas_call(
         kernel,
         out_shape=[jax.ShapeDtypeStruct(shape, kind) for shape, kind in outs],
         in_specs=[pl.BlockSpec(memory_space=pltpu.SMEM)]
-        + [pl.BlockSpec(memory_space=pl.ANY)] * skipped
-        + [pl.BlockSpec(memory_space=pltpu.VMEM)] * len(arrays),
-        out_specs=[pl.BlockSpec(memory_space=pltpu.VMEM)] * len(outs),
-        scratch_shapes=[pltpu.VMEM(shape, kind) for shape, kind in scratch],
+        + [anywhere] * (skipped + len(far))
+        + [near] * len(arrays),
+        out_specs=[anywhere if copies else near] * len(outs),
+        scratch_shapes=scratch_shapes,
         cost_estimate=pl.CostEstimate(flops=flops, bytes_accessed=0, transcendentals=0),
         compiler_params=pltpu.CompilerParams(vmem_limit_bytes=memory * MEBIBYTE),
-    )(place, *after, *arrays)
+    )(place, *after, *far, *arrays)
+
+
+class Copies:
+    def __init__(self, semaphores):
+        self.semaphores, self.all = semaphores, []
+
+    def start(self, source, target):
+        copy = pltpu.make_async_copy(source, target, self.semaphores.at[len(self.all)])
+        copy.start()
+        self.all.append(copy)
+        return copy
+
+
+def wait(copies):
+    for copy in copies:
+        copy.wait()
 
 
 def cut_call(body, outs, place, blocks, after=()):
@@ -387,22 +408,25 @@
     own_up[...] = up_rows[...]
 
 
-def assemble_rows(place, whole, own, got, other):
+def assemble_rows(place, copies, whole, own, got, other):
     here, core = place[1], place[2]
     rows, half = own.shape[0], own.shape[0] // 2
-    whole[span(here, rows), :] = own[...]
+    started = [copies.start(own, whole.at[span(here, rows)])]
     for step in range(1, len(got) + 1):
         start = (here ^ step) * rows
         mine = pl.ds(pl.multiple_of(start + core * half, half), half)
-        whole[mine, :] = got[step - 1][...]
         twins = pl.ds(pl.multiple_of(start + (1 - core) * half, half), half)
-        whole[twins, :] = other[step - 1][...]
-
-
-def assemble_width(place, whole, parts, columns):
-    rows = parts[0].shape[0]
-    for step, part in enumerate(parts):
-        whole[span(place[0] ^ step, rows), :] = part[:, columns]
+        started.append(copies.start(got[step - 1], whole.at[mine]))
+        started.append(copies.start(other[step - 1], whole.at[twins]))
+    return started
+
+
+def assemble_width(place, copies, whole, parts):
+    rows, columns = parts[0].shape[0], whole.shape[1]
+    return [
+        copies.start(part.at[:, pl.ds(0, columns)], whole.at[span(place[0] ^ step, rows)])
+        for step, part in enumerate(parts)
+    ]
 
 
 def column_sums(values):
@@ -423,30 +447,67 @@
     return lax.broadcasted_iota(jnp.int32, (rows, keys), 1) <= row
 
 
-def forward_kernel(members, quarters, place, *refs):
-    own, refs = refs[0], refs[1:]
-    got, refs = refs[: members - 1], refs[members - 1 :]
-    other, refs = refs[: members - 1], refs[members - 1 :]
-    parts, refs = refs[:quarters], refs[quarters:]
-    gain_one, shift_one, gain_two, shift_two, bias_qkv, bias_up, table = refs[:7]
-    hat_turned, qkv, mixed, log_total, joined, slope, weights, weights_two = refs[7:15]
-    seq, low_one, low_two = refs[15:]
-    assemble_rows(place, seq, own, got, other)
-    cut = weights.shape[1]
-    assemble_width(place, weights, parts, slice(0, cut))
-    assemble_width(place, weights_two, parts, slice(cut, cut + weights_two.shape[1]))
+def gather_halves(place, values, mine, twins):
+    here, core = place[1], place[2]
+    members, half = mine.shape[:2]
+    for step in range(members):
+        start = (here ^ step) * (2 * half)
+        mine[step] = values[pl.ds(pl.multiple_of(start + core * half, half), half), :]
+        twins[step] = values[pl.ds(pl.multiple_of(start + (1 - core) * half, half), half), :]
+
+
+def flat(values):
+    return values.reshape(values.shape[0] * values.shape[1], values.shape[2])
+
+
+def send_parts(place, copies, sums, small, messages):
+    part = sums.shape[0] // len(messages)
+    started = []
+    for step, message in enumerate(messages):
+        chosen = sums.at[span(place[0] ^ step, part)]
+        started.append(copies.start(chosen, message.at[pl.ds(0, part)]))
+        rows = pl.ds(part, small.shape[1])
+        started.append(copies.start(small.at[step], message.at[rows]))
+    return started
+
+
+def first_kernel(members, quarters, place, *refs):
+    refs = list(refs)
+
+    def some(count):
+        taken = refs[:count]
+        del refs[:count]
+        return taken
+
+    rows_of = [some(1) + [some(members - 1), some(members - 1)] for _ in range(2)]
+    parts = some(quarters)
+    (table_far,) = some(1)
+    gain_one, shift_one, gain_two, shift_two, bias_qkv, bias_up = some(6)
+    hat_out, qkv_out, mixed_out, log_out, heads_out, up_out, kept_out, other_out = some(8)
+    messages = some(quarters)
+    seq, grad, weights, table, low_one, low_two, hat, qkv, mixed, log_total = some(10)
+    joined, slope, grad_heads, grad_up, kept, other, mine, twins, sums_w, small = some(10)
+    copies = Copies(refs[0])
+    row_copies = assemble_rows(place, copies, seq, *rows_of[0])
+    weight_copies = assemble_width(place, copies, weights, parts)
+    weight_copies.append(copies.start(table_far, table))
+    grad_copies = assemble_rows(place, copies, grad, *rows_of[1])
+    block = seq.shape[0] // members
     seq_len = seq.shape[0]
     width = mixed.shape[1]
-    block = own.shape[0]
+    cut = 3 * width + slope.shape[1]
+    wait(row_copies)
     for start in range(0, seq_len, block):
         rows = slice(start, start + block)
         values = seq[rows, :].astype(jnp.float32)
         center = values - jnp.mean(values, axis=-1, keepdims=True)
         spread = jnp.mean(center * center, axis=-1, keepdims=True)
         normed = center * lax.rsqrt(spread + EPSILON)
-        hat_turned[:, rows] = normed.astype(jnp.bfloat16).T
+        hat[:, rows] = normed.astype(jnp.bfloat16).T
         low_one[rows, :] = (normed * gain_one[...] + shift_one[...]).astype(jnp.bfloat16)
         low_two[rows, :] = (normed * gain_two[...] + shift_two[...]).astype(jnp.bfloat16)
+    leaving = [copies.start(hat, hat_out)]
+    wait(weight_copies)
     turning = [table[part] for part in range(3)]
     query = dot(low_one[...], weights[:, :width]) + bias_qkv[:, :width]
     query = turn(query, turning, 1.0).astype(jnp.bfloat16)
@@ -455,7 +516,8 @@
     qkv[:, width : 2 * width] = turn(key, turning, 1.0).astype(jnp.bfloat16)
     value = dot(low_one[...], weights[:, 2 * width : 3 * width]) + bias_qkv[:, 2 * width :]
     qkv[:, 2 * width :] = value.astype(jnp.bfloat16)
-    pre = dot(low_two[...], weights[:, 3 * width :]) + bias_up[...]
+    leaving.append(copies.start(qkv, qkv_out))
+    pre = dot(low_two[...], weights[:, 3 * width : cut]) + bias_up[...]
     phi = 0.5 * (1.0 + lax.erf(pre * (1.0 / math.sqrt(2.0))))
     density = jnp.exp(-0.5 * pre * pre) * (1.0 / math.sqrt(2.0 * math.pi))
     joined[:, width:] = (pre * phi).astype(jnp.bfloat16)
@@ -479,56 +541,60 @@
         mixed[rows, :] = result
         log_total[rows, :] = logs
         joined[rows, :width] = result.astype(jnp.bfloat16)
-
-
-def gather_halves(place, values, mine, twins):
-    here, core = place[1], place[2]
-    members, half = mine.shape[:2]
-    for step in range(members):
-        start = (here ^ step) * (2 * half)
-        mine[step] = values[pl.ds(pl.multiple_of(start + core * half, half), half), :]
-        twins[step] = values[pl.ds(pl.multiple_of(start + (1 - core) * half, half), half), :]
-
-
-def flat(values):
-    return values.reshape(values.shape[0] * values.shape[1], values.shape[2])
-
-
-def branch_kernel(place, joined, weights, kept, other, mine, twins):
+    leaving += [copies.start(mixed, mixed_out), copies.start(log_total, log_out)]
     gather_halves(place, joined, mine, twins)
-    kept[...] = dot(flat(mine[...]), weights[...], (1, 1)).reshape(kept.shape)
-    partial = dot(flat(twins[...]), weights[...], (1, 1))
+    partial = dot(flat(twins[...]), weights[:, cut:], (1, 1))
     other[...] = partial.astype(jnp.bfloat16).reshape(other.shape)
-
-
-def gradient_kernel(members, quarters, place, own, *refs):
-    got, refs = refs[: members - 1], refs[members - 1 :]
-    other, refs = refs[: members - 1], refs[members - 1 :]
-    hat_turned, joined, slope, weights = refs[:4]
+    leaving.append(copies.start(other, other_out))
+    kept[...] = dot(flat(mine[...]), weights[:, cut:], (1, 1)).reshape(kept.shape)
+    leaving.append(copies.start(kept, kept_out))
+    wait(grad_copies)
+    back = cut + width
+    grad_heads[...] = dot(grad[...], weights[:, cut:back]).astype(jnp.bfloat16)
+    leaving.append(copies.start(grad_heads, heads_out))
+    grad_up[...] = (dot(grad[...], weights[:, back:]) * slope[...]).astype(jnp.bfloat16)
+    leaving.append(copies.start(grad_up, up_out))
+    units = grad_up.shape[1]
+    sums_w[:, :units] = dot(hat[...], grad_up[...]).astype(jnp.bfloat16)
+    sums_w[:, units:] = dot(grad[...], joined[...], (0, 0)).astype(jnp.bfloat16)
+    biases = column_sums(grad_up[...])
+    part = grad.shape[1] // quarters
+    for step in range(quarters):
+        sums = column_sums(grad[:, span(place[0] ^ step, part)])
+        small[step] = small_rows([biases, sums], small.shape[2])
+    wait(leaving + send_parts(place, copies, sums_w, small, messages))
+
+
+def pair_kernel(place, kept, got, own, *pieces):
+    own[...] = kept[0] + got[0].astype(jnp.float32)
+    for step, piece in enumerate(pieces, 1):
+        piece[...] = (kept[step] + got[step].astype(jnp.float32)).astype(jnp.bfloat16)
+
+
+def halve_kernel(place, kept, got, stay, leave):
+    for index in range(stay.shape[0]):
+        stay[index] = kept[2 * index] + got[2 * index].astype(jnp.float32)
+        odd = kept[2 * index + 1] + got[2 * index + 1].astype(jnp.float32)
+        leave[index] = odd.astype(jnp.bfloat16)
+
+
+def second_kernel(block, quarters, place, *refs):
+    qkv_far, mixed_far, log_far, heads_far, table_far, up_far, hat_far = refs[:7]
+    parts, refs = refs[7 : 7 + quarters], refs[7 + quarters :]
+    gain_one, gain_two, kept_out, other_out = refs[:4]
     messages, refs = refs[4 : 4 + quarters], refs[4 + quarters :]
-    grad_heads, grad_up, grad, partial = refs
-    assemble_rows(place, grad, own, got, other)
-    depth = grad.shape[1]
-    width = grad_heads.shape[1]
-    units = grad_up.shape[1]
-    grad_heads[...] = dot(grad[...], weights[:, :width]).astype(jnp.bfloat16)
-    grad_up[...] = (dot(grad[...], weights[:, width:]) * slope[...]).astype(jnp.bfloat16)
-    partial[:, :units] = dot(hat_turned[...], grad_up[...]).astype(jnp.bfloat16)
-    partial[:, units:] = dot(grad[...], joined[...], (0, 0)).astype(jnp.bfloat16)
-    biases = column_sums(grad_up[...])
-    part = depth // quarters
-    for step in range(quarters):
-        quarter = span(place[0] ^ step, part)
-        message = messages[step]
-        message[:part, :] = partial[quarter, :]
-        sums = column_sums(grad[:, quarter])
-        message[part:, :] = small_rows([biases, sums], message.shape[1])
-
-
-def backward_kernel(block, place, *refs):
-    qkv, mixed, log_total, grad_heads, table, grad_proj, sum_key, sum_value = refs
+    qkv, mixed, log_total, grad_heads, table, grad_up, hat, weights = refs[:8]
+    grad_proj, sum_key, sum_value, kept, other = refs[8:13]
+    mine_proj, twins_proj, mine_up, twins_up, sums_w, small, semaphores = refs[13:]
+    copies = Copies(semaphores)
+    far = (qkv_far, mixed_far, log_far, heads_far, table_far)
+    near = (qkv, mixed, log_total, grad_heads, table)
+    first_copies = [copies.start(source, target) for source, target in zip(far, near)]
+    later_copies = [copies.start(up_far, grad_up), copies.start(hat_far, hat)]
+    later_copies += assemble_width(place, copies, weights, parts)
     seq_len, width = mixed.shape
     scale = 1.0 / math.sqrt(HEAD)
+    wait(first_copies)
     sum_key[...] = jnp.zeros_like(sum_key)
     sum_value[...] = jnp.zeros_like(sum_value)
     for start in range(0, seq_len, block):
@@ -560,12 +626,7 @@
     turning = [table[part] for part in range(3)]
     grad_proj[:, width : 2 * width] = turn(sum_key[...], turning, -1.0).astype(jnp.bfloat16)
     grad_proj[:, 2 * width :] = sum_value[...].astype(jnp.bfloat16)
-
-
-def norm_gradient_kernel(quarters, place, *refs):
-    grad_proj, grad_up, hat_turned, weights, gain_one, gain_two, kept, other = refs[:8]
-    messages, refs = refs[8 : 8 + quarters], refs[8 + quarters :]
-    mine_proj, twins_proj, mine_up, twins_up, weight_sum = refs
+    wait(later_copies)
     cut = grad_proj.shape[1]
     gather_halves(place, grad_proj, mine_proj, twins_proj)
     gather_halves(place, grad_up, mine_up, twins_up)
@@ -575,14 +636,14 @@
         return first + dot(flat(up[...]), weights[:, cut:], (1, 1)) * gain_two[...]
 
     other[...] = gradient(twins_proj, twins_up).astype(jnp.bfloat16).reshape(other.shape)
+    leaving = [copies.start(other, other_out)]
     kept[...] = gradient(mine_proj, mine_up).reshape(kept.shape)
-    weight_sum[...] = dot(hat_turned[...], grad_proj[...]).astype(jnp.bfloat16)
-    part = hat_turned.shape[0] // quarters
-    biases = column_sums(grad_proj[...])
+    leaving.append(copies.start(kept, kept_out))
+    sums_w[...] = dot(hat[...], grad_proj[...]).astype(jnp.bfloat16)
+    lines = small_rows([column_sums(grad_proj[...])], small.shape[2])
     for step in range(quarters):
-        message = messages[step]
-        message[:part, :] = weight_sum[span(place[0] ^ step, part), :]
-        message[part:, :] = small_rows([biases], message.shape[1])
+        small[step] = lines
+    wait(leaving + send_parts(place, copies, sums_w, small, messages))
 
 
 def add_parts(parts, chosen):
@@ -665,6 +726,12 @@
     norms[...] = result
 
 
+def pair_kernel(place, kept, got, own, *pieces):
+    own[...] = kept[0] + got[0].astype(jnp.float32)
+    for step, piece in enumerate(pieces, 1):
+        piece[...] = (kept[step] + got[step].astype(jnp.float32)).astype(jnp.bfloat16)
+
+
 def halve_kernel(place, kept, got, stay, leave):
     for index in range(stay.shape[0]):
         stay[index] = kept[2 * index] + got[2 * index].astype(jnp.float32)
@@ -772,111 +839,110 @@
 
     table = turn_tables(seq_len, width)
     line = lambda values: values.reshape(1, -1)
-    hat_turned, qkv, mixed, log_total, joined, slope, weights_one, weights_two = call(
-        lambda *refs: forward_kernel(members, quarters, *refs),
+    hat, qkv, mixed, log_total, grad_heads, grad_up, kept, other, *messages = call(
+        lambda *refs: first_kernel(members, quarters, *refs),
         [
+            ((depth, seq_len), low),
+            ((seq_len, 3 * width), low),
+            ((seq_len, width), wide),
+            ((seq_len, width), wide),
+            ((seq_len, width), low),
+            ((seq_len, units), low),
+            ((members, half, depth), wide),
+            ((members, half, depth), low),
+        ]
+        + [((part + 16, width + 2 * units), low)] * quarters,
+        place,
+        line(ln1_gain),
+        line(ln1_bias),
+        line(ln2_gain),
+        line(ln2_bias),
+        line(take(b_qkv, here * width, width, 1)),
+        line(take(b_up, here * units, units)),
+        far=[tokens, *seq_got, *seq_other, cotangent, *grad_got, *grad_other, *parts, table],
+        scratch=[
+            ((seq_len, depth), low),
+            ((seq_len, depth), low),
+            ((depth, cuts), low),
+            ((3, seq_len, width), wide),
+            ((seq_len, depth), low),
+            ((seq_len, depth), low),
             ((depth, seq_len), low),
             ((seq_len, 3 * width), low),
             ((seq_len, width), wide),
             ((seq_len, width), wide),
             ((seq_len, width + units), low),
             ((seq_len, units), wide),
-            ((depth, 3 * width + units), low),
-            ((depth, width + units), low),
+            ((seq_len, width), low),
+            ((seq_len, units), low),
+            ((members, half, depth), wide),
+            ((members, half, depth), low),
+            ((members, half, width + units), low),
+            ((members, half, width + units), low),
+            ((depth, width + 2 * units), low),
+            ((quarters, 16, width + 2 * units), low),
         ],
+        copies=2 * (2 * members - 1) + quarters + 1 + 8 + 2 * quarters,
+        flops=25 * 10**9,
+        memory=60,
+    )
+    early = messages[:1] + [send(messages[step], "fsdp", step) for step in range(1, quarters)]
+    branches, *pieces = call(
+        pair_kernel,
+        [((half, depth), wide)] + [((half, depth), low)] * (members - 1),
         place,
-        tokens,
-        *seq_got,
-        *seq_other,
-        *parts,
-        line(ln1_gain),
-        line(ln1_bias),
-        line(ln2_gain),
-        line(ln2_bias),
-        line(take(b_qkv, here * width, width, 1)),
-        line(take(b_up, here * units, units)),
-        table,
-        scratch=[((seq_len, depth), low)] * 3,
-        flops=12 * 10**9,
-        memory=60,
-    )
-    kept, other = call(
-        branch_kernel,
-        [((members, half, depth), wide), ((members, half, depth), low)],
-        place,
-        joined,
-        weights_two,
-        scratch=[((members, half, width + units), low)] * 2,
-        flops=4 * 10**9,
-        memory=60,
-    )
-    *messages, grad_heads, grad_up = call(
-        lambda *refs: gradient_kernel(members, quarters, *refs),
-        [((part + 16, width + 2 * units), low)] * quarters
-        + [((seq_len, width), low), ((seq_len, units), low)],
-        place,
-        cotangent,
-        *grad_got,
-        *grad_other,
-        hat_turned,
-        joined,
-        slope,
-        weights_two,
-        scratch=[
-            ((seq_len, depth), low),
-            ((depth, width + 2 * units), low),
-        ],
-        after=[other],
-        flops=11 * 10**9,
-        memory=60,
-    )
-    early = messages[:1] + [send(messages[step], "fsdp", step) for step in range(1, quarters)]
-    stay, leave = first_halving(place, kept, other, after=[grad_heads])
-    leave = send(leave, "context", 1)
-    (grad_proj,) = call(
-        lambda *refs: backward_kernel(rows, *refs),
-        [((seq_len, 3 * width), low)],
-        place,
-        qkv,
-        mixed,
-        log_total,
-        grad_heads,
-        table,
-        scratch=[((seq_len, width), wide)] * 2,
-        after=[stay],
+        kept,
+        send(other, "tensor", 1),
         flops=1,
-        memory=60,
-    )
-    total = stay + leave.astype(wide)
+    )
+    branch_pieces = [send(pieces[step - 1], "context", step) for step in others]
     kept, other, *messages = call(
-        lambda *refs: norm_gradient_kernel(quarters, *refs),
+        lambda *refs: second_kernel(rows, quarters, *refs),
         [((members, half, depth), wide), ((members, half, depth), low)]
         + [((part + 16, 3 * width), low)] * quarters,
         place,
-        grad_proj,
-        grad_up,
-        hat_turned,
-        weights_one,
         line(ln1_gain),
         line(ln2_gain),
-        scratch=[((members, half, 3 * width), low)] * 2
-        + [((members, half, units), low)] * 2
-        + [((depth, 3 * width), low)],
-        after=[total],
+        far=[qkv, mixed, log_total, grad_heads, table, grad_up, hat, *parts],
+        scratch=[
+            ((seq_len, 3 * width), low),
+            ((seq_len, width), wide),
+            ((seq_len, width), wide),
+            ((seq_len, width), low),
+            ((3, seq_len, width), wide),
+            ((seq_len, units), low),
+            ((depth, seq_len), low),
+            ((depth, 3 * width + units), low),
+            ((seq_len, 3 * width), low),
+            ((seq_len, width), wide),
+            ((seq_len, width), wide),
+            ((members, half, depth), wide),
+            ((members, half, depth), low),
+            ((members, half, 3 * width), low),
+            ((members, half, 3 * width), low),
+            ((members, half, units), low),
+            ((members, half, units), low),
+            ((depth, 3 * width), low),
+            ((quarters, 16, 3 * width), low),
+        ],
+        copies=7 + quarters + 2 + 2 * quarters,
+        after=[branches],
         flops=1,
         memory=60,
     )
     late = messages[:1] + [send(messages[step], "fsdp", step) for step in range(1, quarters)]
 
-    branches = last_halvings(total)
+    for piece in branch_pieces:
+        branches = branches + piece.astype(wide)
     *early, sums = call(
         lambda *refs: share_early_kernel(members, quarters, *refs),
         [((lines + 16, width + 2 * units), low)] * members + [((1, width + 2 * units), wide)],
         place,
         *early,
+        after=branch_pieces[:2],
         flops=20 * 10**9,
     )
-    stay, leave = first_halving(place, kept, other, after=[sums, branches, *late[1:]])
+    stay, leave = first_halving(place, kept, other, after=[sums])
     leave = send(leave, "context", 1)
     pieces = call(
         lambda *refs: share_late_kernel(members, quarters, *refs),
@@ -922,7 +988,7 @@
         qkv_rows,
         up_rows,
         take(columns, begin, lines, 1).T,
-        after=[leave],
+        after=[leave, branches],
     )
     norms = norms[:, :4].T
     norms = norms + send(norms, "tensor", 1)

time: 174 us -> 167 us (0.960); the launches traced: 174 us -> 163 us
  Pallas kernels: 52.4 us -> 39.6 us
  starting transfers between devices: 37 us -> 46.3 us
  waiting for transfers between devices: 63.1 us -> 56.4 us
  local copies, waits for them, and re-layouts: 10.2 us -> 13.3 us
  other arithmetic: 9.66 us -> 6.58 us
    pallas_call x10 -> x7, Pallas kernels: 49.1 us -> 36.3 us  [call(): pl.pallas_call(kernel, out_shape=[jax.ShapeDtypeStruct(shape, kind) for s...]
    ppermute x34 -> x35, starting transfers between devices: 37 us -> 46.3 us  [send(): lax.ppermute(values, axis, [(index, index ^ step) for index in range(size)])]
    ppermute x34 -> x35, waiting for transfers between devices: 63.1 us -> 56.4 us  [send(): lax.ppermute(values, axis, [(index, index ^ step) for index in range(size)])]
    add x2 -> x0, other arithmetic: 2.46 us -> none  [the longest x1 2.18 us: whole_sequences(): total = stay + leave.astype(wide)]
    concatenate x1 -> x0, other arithmetic: 1.94 us -> none  [gather_halves_apart(): return [values, one, two, jnp.concatenate(three)]]
    unnamed x78 -> x79, local copies, waits for them, and re-layouts: 6.07 us -> 7.63 us
  transfers between devices with their start and end apart: 34 -> 35, of which waited for: 11 -> 11; matrix products, arithmetic and copies ran while one was open for 7% -> 7% of each run, Pallas kernels for 27% -> 9%
where the time goes in v3:
time: 167 us; the launch traced here: 163 us
  waiting for transfers between devices  56.4 us (34%)
  starting transfers between devices  46.3 us (28%)
  Pallas kernels  39.6 us (24%)
  local copies, waits for them, and re-layouts  13.3 us (8%)
  other arithmetic  6.58 us (4%)
    ppermute x35, waiting for transfers between devices, send(): lax.ppermute(values, axis, [(index, index ^ step) for index in range(size)])  56.4 us
    ppermute x35, starting transfers between devices, send(): lax.ppermute(values, axis, [(index, index ^ step) for index in range(size)])  46.3 us
    pallas_call x7, Pallas kernels, call(): pl.pallas_call(kernel, out_shape=[jax.ShapeDtypeStruct(shape, kind) for s...  36.3 us
    unnamed x79, local copies, waits for them, and re-layouts  7.63 us
  transfers between devices with their start and end apart: 35, of which 11 were waited for; matrix products, arithmetic and copies ran while one was open for 7% of the time, Pallas kernels for 9%

profile of v3, /device:TPU:0, one launch (start us, length us, event | category | flops | bytes accessed | tf_op | source)
XLA Modules:
  0.0 163.3 jit_solution(16467795747462759782)
XLA Ops:
  1.3 3.3 %shard_map.245 = (bf16[128,1024]{1,0:T(8,128)(2,1)}, bf16[128,1024]{1,0:T(8,128)(2,1)}, bf16[256,1536]{1,0:T(8,128)(2,1)}, bf16[3,64,512]{2,1,0:T(8,128)(2,1)}, bf16[64,2048]{1,0:T(8,128)(2,1)}) custom-call(s32[3]{0:T(128)} %pad_add_fusion.place_ref, bf16[256,1024]{1,0:T(8,128)(2,1)} %refs_0_.3, bf16[256,1024]{1,0:T(8,128)(2,1)} %refs_7_.3, ...), custom_call_target="tpu_custom_call" | custom-call | tf_op jit(solution)/shard_map/pallas_call | solution.py:333
  4.6 2.9 %collective-permute-start.12 = (bf16[256,1536]{1,0:T(8,128)(2,1)}, bf16[256,1536]{1,0:T(8,128)(2,1)S(1)}, u32[]{:S(2)}, u32[]{:S(2)}) collective-permute-start(bf16[256,1536]{1,0:T(8,128)(2,1)} %get-tuple-element.61.refs_14_.refs_8_), channel_id=1, source_target_pairs={{0,8},{8,0},{16,24},{24,16},{1,9},{9,1},{17,25},{25,17},{2,10},{10... | collective-permute-start | bytes 2359304 | tf_op jit(solution)/shard_map/ppermute | solution.py:269
  7.5 1.5 collective-permute-start.13
  9.0 2.6 %collective-permute-start.1 = (bf16[128,1024]{1,0:T(8,128)(2,1)}, bf16[128,1024]{1,0:T(8,128)(2,1)S(1)}, u32[]{:S(2)}, u32[]{:S(2)}) collective-permute-start(bf16[128,1024]{1,0:T(8,128)(2,1)} %get-tuple-element.59), channel_id=1, source_target_pairs={{0,4},{2,6},{4,0},{6,2},{1,5},{3,7},{5,1},{7,3},{8,12},{10,14},{12... | collective-permute-start | bytes 786440 | tf_op jit(solution)/shard_map/ppermute | solution.py:269
  11.6 1.6 collective-permute-start
  13.5 11.7 %collective-permute-done.12.refs_15_.refs_9_ = bf16[256,1536]{1,0:T(8,128)(2,1)S(1)} collective-permute-done((bf16[256,1536]{1,0:T(8,128)(2,1)}, bf16[256,1536]{1,0:T(8,128)(2,1)S(1)}, u32[]{:S(2)}, u32[]{:S(2)}) %collective-permute-start.12) | collective-permute-done | bytes 786464 | tf_op jit(solution)/shard_map/ppermute | solution.py:269
  25.2 1.8 %collective-permute-start.6 = (bf16[128,1024]{1,0:T(8,128)(2,1)}, bf16[128,1024]{1,0:T(8,128)(2,1)S(1)}, u32[]{:S(2)}, u32[]{:S(2)}) collective-permute-start(bf16[128,1024]{1,0:T(8,128)(2,1)} %get-tuple-element.60), channel_id=1, source_target_pairs={{0,2},{2,0},{4,6},{6,4},{1,3},{3,1},{5,7},{7,5},{8,10},{10,8},{12,... | collective-permute-start | bytes 786440 | tf_op jit(solution)/shard_map/ppermute | solution.py:269
  27.4 0.8 slice.39
  28.2 1.5 collective-permute-start.14
  29.7 0.8 slice.40
  30.5 4.1 %collective-permute-done.7.refs_9_ = bf16[128,1024]{1,0:T(8,128)(2,1)S(1)} collective-permute-done((bf16[128,1024]{1,0:T(8,128)(2,1)}, bf16[128,1024]{1,0:T(8,128)(2,1)S(1)}, u32[]{:S(2)}, u32[]{:S(2)}) %collective-permute-start.7) | collective-permute-done | bytes 262176 | tf_op jit(solution)/shard_map/ppermute | solution.py:269
  36.1 0.8 collective-permute-start.8
  37.5 0.9 collective-permute-start.2
  38.9 1.3 dynamic_slice.22
  40.3 1.3 pad_maximum_fusion.refs_18_.refs_5_
  41.6 3.8 %collective-permute-done.8.refs_10_ = bf16[128,1024]{1,0:T(8,128)(2,1)S(1)} collective-permute-done((bf16[128,1024]{1,0:T(8,128)(2,1)S(1)}, bf16[128,1024]{1,0:T(8,128)(2,1)S(1)}, u32[]{:S(2)}, u32[]{:S(2)}) %collective-permute-start.8) | collective-permute-done | bytes 262176 | tf_op jit(solution)/shard_map/ppermute | solution.py:269
  45.4 3.4 %collective-permute-done.2.refs_3_ = bf16[128,1024]{1,0:T(8,128)(2,1)} collective-permute-done((bf16[128,1024]{1,0:T(8,128)(2,1)S(1)}, bf16[128,1024]{1,0:T(8,128)(2,1)}, u32[]{:S(2)}, u32[]{:S(2)}) %collective-permute-start.2) | collective-permute-done | bytes 262176 | tf_op jit(solution)/shard_map/ppermute | solution.py:269
  49.9 1.0 constant_dynamic-update-slice_fusion.1
  50.9 1.0 constant_dynamic-update-slice_fusion.refs_17_.refs_11_
  52.1 0.8 copy-done.14
  53.3 19.1 %shard_map.246 = (bf16[1024,1024]{1,0:T(8,128)(2,1)}, bf16[1024,384]{1,0:T(8,128)(2,1)}, f32[1024,128]{1,0:T(8,128)}, f32[1024,128]{1,0:T(8,128)}, bf16[1024,128...) custom-call(s32[3]{0:T(128)} %pad_add_fusion.place_ref, ...), custom_call_target="tpu_custom_call" | custom-call | flops 24999999488 | tf_op jit(solution)/shard_map/pallas_call | solution.py:295
  72.5 1.5 collective-permute-start.21
  74.0 1.4 collective-permute-start.22
  76.0 1.6 copy-done.2
  77.6 0.7 shard_map.247
  78.3 0.8 copy-done.3
  79.1 1.7 %collective-permute-start.17 = (bf16[128,1024]{1,0:T(8,128)(2,1)S(1)}, bf16[128,1024]{1,0:T(8,128)(2,1)S(1)}, u32[]{:S(2)}, u32[]{:S(2)}) collective-permute-start(bf16[128,1024]{1,0:T(8,128)(2,1)S(1)} %get-tuple-element.65), channel_id=1, source_target_pairs={{0,2},{2,0},{4,6},{6,4},{1,3},{3,1},{5,7},{7,5},{8,10},{10,8},{12,... | collective-permute-start | bytes 786440 | tf_op jit(solution)/shard_map/ppermute | solution.py:269
  80.8 3.3 %collective-permute-start.18 = (bf16[128,1024]{1,0:T(8,128)(2,1)S(1)}, bf16[128,1024]{1,0:T(8,128)(2,1)S(1)}, u32[]{:S(2)}, u32[]{:S(2)}) collective-permute-start(bf16[128,1024]{1,0:T(8,128)(2,1)S(1)} %get-tuple-element.66), channel_id=1, source_target_pairs={{0,4},{2,6},{4,0},{6,2},{1,5},{3,7},{5,1},{7,3},{8,12},{10,14},{12... | collective-permute-start | bytes 786440 | tf_op jit(solution)/shard_map/ppermute | solution.py:269
  84.4 1.1 convert_reduce_fusion
  85.4 12.1 %shard_map.249 = (f32[4,128,1024]{2,1,0:T(8,128)}, bf16[4,128,1024]{2,1,0:T(8,128)(2,1)}, bf16[272,384]{1,0:T(8,128)(2,1)}, bf16[272,384]{1,0:T(8,128)(2,1)}, bf...) custom-call(s32[3]{0:T(128)} %pad_add_fusion.place_ref, f32[128,1024]{1,0:T(8,128)} %copy-done.3, ...), custom_call_target="tpu_custom_call" | custom-call | flops 1 | tf_op jit(solution)/shard_map/pallas_call | solution.py:295
  97.6 6.2 %collective-permute-done.22.refs_4_ = bf16[272,1152]{1,0:T(8,128)(2,1)S(1)} collective-permute-done((bf16[272,1152]{1,0:T(8,128)(2,1)}, bf16[272,1152]{1,0:T(8,128)(2,1)S(1)}, u32[]{:S(2)}, u32[]{:S(2)}) %collective-permute-start.22) | collective-permute-done | bytes 626720 | tf_op jit(solution)/shard_map/ppermute | solution.py:269
  103.8 1.1 copy-done.10
  104.9 0.9 shard_map.248
  107.2 1.8 %collective-permute-start.25 = (bf16[2,128,1024]{2,1,0:T(8,128)(2,1)S(1)}, bf16[2,128,1024]{2,1,0:T(8,128)(2,1)S(1)}, u32[]{:S(2)}, u32[]{:S(2)}) collective-permute-start(bf16[2,128,1024]{2,1,0:T(8,128)(2,1)S(1)} %get-tuple-element.82), channel_id=1, source_target_pairs={{0,2},{2,0},{4,6},{6,4},{1,3},{3,1},{5,7},{7,5},{8,10},{10,8},{12,... | collective-permute-start | bytes 1572872 | tf_op jit(solution)/shard_map/ppermute | solution.py:269
  109.3 0.8 collective-permute-start.28
  110.1 1.2 collective-permute-start.29
  111.3 1.8 %collective-permute-start.30 = (bf16[272,384]{1,0:T(8,128)(2,1)S(1)}, bf16[272,384]{1,0:T(8,128)(2,1)S(1)}, u32[]{:S(2)}, u32[]{:S(2)}) collective-permute-start(bf16[272,384]{1,0:T(8,128)(2,1)S(1)} %copy-done.33), channel_id=1, source_target_pairs={{0,24},{8,16},{16,8},{24,0},{1,25},{9,17},{17,9},{25,1},{2,26},{10... | collective-permute-start | bytes 626696 | tf_op jit(solution)/shard_map/ppermute | solution.py:269
  113.0 3.0 %collective-permute-start.19 = (bf16[128,1024]{1,0:T(8,128)(2,1)S(1)}, bf16[128,1024]{1,0:T(8,128)(2,1)S(1)}, u32[]{:S(2)}, u32[]{:S(2)}) collective-permute-start(bf16[128,1024]{1,0:T(8,128)(2,1)S(1)} %get-tuple-element.67), channel_id=1, source_target_pairs={{0,6},{2,4},{4,2},{6,0},{1,7},{3,5},{5,3},{7,1},{8,14},{10,12},{12... | collective-permute-start | bytes 786440 | tf_op jit(solution)/shard_map/ppermute | solution.py:269
  116.0 5.4 %collective-permute-done.25.refs_0_ = bf16[2,128,1024]{2,1,0:T(8,128)(2,1)S(1)} collective-permute-done((bf16[2,128,1024]{2,1,0:T(8,128)(2,1)S(1)}, bf16[2,128,1024]{2,1,0:T(8,128)(2,1)S(1)}, u32[]{:S(2)}, u32[]{:S(2)}) %collective-permute-start.25) | collective-permute-done | bytes 524320 | tf_op jit(solution)/shard_map/ppermute | solution.py:269
  121.6 7.2 %collective-permute-start.26 = (bf16[1,128,1024]{2,1,0:T(8,128)(2,1)S(1)}, bf16[1,128,1024]{2,1,0:T(8,128)(2,1)S(1)}, u32[]{:S(2)}, u32[]{:S(2)}) collective-permute-start(bf16[1,128,1024]{2,1,0:T(8,128)(2,1)S(1)} %slice.62), channel_id=1, source_target_pairs={{0,4},{2,6},{4,0},{6,2},{1,5},{3,7},{5,1},{7,3},{8,12},{10,14},{12... | collective-permute-start | bytes 786440 | tf_op jit(solution)/shard_map/ppermute | solution.py:269
  129.6 3.0 %collective-permute-start.31 = (bf16[80,1536]{1,0:T(8,128)(2,1)S(1)}, bf16[80,1536]{1,0:T(8,128)(2,1)S(1)}, u32[]{:S(2)}, u32[]{:S(2)}) collective-permute-start(bf16[80,1536]{1,0:T(8,128)(2,1)S(1)} %get-tuple-element.92), channel_id=1, source_target_pairs={{0,2},{2,0},{4,6},{6,4},{1,3},{3,1},{5,7},{7,5},{8,10},{10,8},{12,... | collective-permute-start | bytes 737288 | tf_op jit(solution)/shard_map/ppermute | solution.py:269
  133.3 1.8 %collective-permute-start.33 = (bf16[80,1536]{1,0:T(8,128)(2,1)S(1)}, bf16[80,1536]{1,0:T(8,128)(2,1)S(1)}, u32[]{:S(2)}, u32[]{:S(2)}) collective-permute-start(bf16[80,1536]{1,0:T(8,128)(2,1)S(1)} %get-tuple-element.94), channel_id=1, source_target_pairs={{0,6},{2,4},{4,2},{6,0},{1,7},{3,5},{5,3},{7,1},{8,14},{10,12},{12... | collective-permute-start | bytes 737288 | tf_op jit(solution)/shard_map/ppermute | solution.py:269
  135.1 15.8 %collective-permute-done.26 = bf16[1,128,1024]{2,1,0:T(8,128)(2,1)S(1)} collective-permute-done((bf16[1,128,1024]{2,1,0:T(8,128)(2,1)S(1)}, bf16[1,128,1024]{2,1,0:T(8,128)(2,1)S(1)}, u32[]{:S(2)}, u32[]{:S(2)}) %collective-permute-start.26) | collective-permute-done | bytes 262176 | tf_op jit(solution)/shard_map/ppermute | solution.py:269
  151.7 4.3 %collective-permute-done.32.refs_4_ = bf16[80,1536]{1,0:T(8,128)(2,1)S(1)} collective-permute-done((bf16[80,1536]{1,0:T(8,128)(2,1)S(1)}, bf16[80,1536]{1,0:T(8,128)(2,1)S(1)}, u32[]{:S(2)}, u32[]{:S(2)}) %collective-permute-start.32) | collective-permute-done | bytes 245792 | tf_op jit(solution)/shard_map/ppermute | solution.py:269
  156.1 2.1 %shard_map.252 = (f32[3,64,512]{2,1,0:T(8,128)}, f32[3,512]{1,0:T(4,128)}, f32[64,512]{1,0:T(8,128)}, f32[64,2048]{1,0:T(8,128)}, f32[1,2048]{1,0:T(1,128)}, /*index=5*/f32[64,2048]{1,0:T(8,128)}, f32[64,128]{1,0:T(8,128)S(1)}) custom-call(s32[3]{0:T(128)S(1)} %copy-done.6, bf16[2,128,1024]{2,1,0:T(8,128)(2,1)S(1)} %collective-permute-done.25.refs_0_, ...), custom_call_target="tpu_custom_call" | custom-call | flops 1000000000 | tf_op jit(solution)/shard_map/pallas_call | solution.py:295
  159.4 0.7 slice_reduce_fusion
  160.8 0.8 pad_maximum_fusion.2
  161.7 1.0 pad_maximum_fusion.1
  (150 shorter events, 12.8 us)
Async XLA Ops:
  0.6 37.7 %copy-start = (f32[3,512]{1,0:T(4,128)S(1)}, f32[3,512]{1,0:T(4,128)}, u32[]{:S(2)}) copy-start(f32[3,512]{1,0:T(4,128)} %param.21) | copy-start | bytes 18436
  4.6 20.7 %collective-permute-start.12 = (bf16[256,1536]{1,0:T(8,128)(2,1)}, bf16[256,1536]{1,0:T(8,128)(2,1)S(1)}, u32[]{:S(2)}, u32[]{:S(2)}) collective-permute-start(bf16[256,1536]{1,0:T(8,128)(2,1)} %get-tuple-element.61.refs_14_.refs_8_), channel_id=1, source_target_pairs={{0,8},{8,0},{16,24},{24,16},{1,9},{9,1},{17,25},{25,17},{2,10},{10... | collective-permute-start | bytes 2359304 | tf_op jit(solution)/shard_map/ppermute | solution.py:269
  7.5 20.7 %collective-permute-start.13 = (bf16[256,1536]{1,0:T(8,128)(2,1)}, bf16[256,1536]{1,0:T(8,128)(2,1)S(1)}, u32[]{:S(2)}, u32[]{:S(2)}) collective-permute-start(bf16[256,1536]{1,0:T(8,128)(2,1)} %get-tuple-element.61.refs_14_.refs_8_), channel_id=1, source_target_pairs={{0,16},{8,24},{16,0},{24,8},{1,17},{9,25},{17,1},{25,9},{2,18},{10... | collective-permute-start | bytes 2359304 | tf_op jit(solution)/shard_map/ppermute | solution.py:269
  9.0 27.1 %collective-permute-start.1 = (bf16[128,1024]{1,0:T(8,128)(2,1)}, bf16[128,1024]{1,0:T(8,128)(2,1)S(1)}, u32[]{:S(2)}, u32[]{:S(2)}) collective-permute-start(bf16[128,1024]{1,0:T(8,128)(2,1)} %get-tuple-element.59), channel_id=1, source_target_pairs={{0,4},{2,6},{4,0},{6,2},{1,5},{3,7},{5,1},{7,3},{8,12},{10,14},{12... | collective-permute-start | bytes 786440 | tf_op jit(solution)/shard_map/ppermute | solution.py:269
  11.6 25.3 %collective-permute-start = (bf16[128,1024]{1,0:T(8,128)(2,1)}, bf16[128,1024]{1,0:T(8,128)(2,1)S(1)}, u32[]{:S(2)}, u32[]{:S(2)}) collective-permute-start(bf16[128,1024]{1,0:T(8,128)(2,1)} %get-tuple-element.59), channel_id=1, source_target_pairs={{0,2},{2,0},{4,6},{6,4},{1,3},{3,1},{5,7},{7,5},{8,10},{10,8},{12,... | collective-permute-start | bytes 786440 | tf_op jit(solution)/shard_map/ppermute | solution.py:269
  13.2 21.4 %collective-permute-start.7 = (bf16[128,1024]{1,0:T(8,128)(2,1)}, bf16[128,1024]{1,0:T(8,128)(2,1)S(1)}, u32[]{:S(2)}, u32[]{:S(2)}) collective-permute-start(bf16[128,1024]{1,0:T(8,128)(2,1)} %get-tuple-element.60), channel_id=1, source_target_pairs={{0,4},{2,6},{4,0},{6,2},{1,5},{3,7},{5,1},{7,3},{8,12},{10,14},{12... | collective-permute-start | bytes 786440 | tf_op jit(solution)/shard_map/ppermute | solution.py:269
  25.2 10.1 %copy-start.12 = (bf16[256,1536]{1,0:T(8,128)(2,1)}, bf16[256,1536]{1,0:T(8,128)(2,1)S(1)}, u32[]{:S(2)}) copy-start(bf16[256,1536]{1,0:T(8,128)(2,1)S(1)} %collective-permute-done.12.refs_15_.refs_9_) | copy-start | bytes 2359300
  25.2 12.2 %collective-permute-start.6 = (bf16[128,1024]{1,0:T(8,128)(2,1)}, bf16[128,1024]{1,0:T(8,128)(2,1)S(1)}, u32[]{:S(2)}, u32[]{:S(2)}) collective-permute-start(bf16[128,1024]{1,0:T(8,128)(2,1)} %get-tuple-element.60), channel_id=1, source_target_pairs={{0,2},{2,0},{4,6},{6,4},{1,3},{3,1},{5,7},{7,5},{8,10},{10,8},{12,... | collective-permute-start | bytes 786440 | tf_op jit(solution)/shard_map/ppermute | solution.py:269
  28.2 7.1 %copy-start.13 = (bf16[256,1536]{1,0:T(8,128)(2,1)}, bf16[256,1536]{1,0:T(8,128)(2,1)S(1)}, u32[]{:S(2)}) copy-start(bf16[256,1536]{1,0:T(8,128)(2,1)S(1)} %collective-permute-done.13.refs_16_.refs_10_) | copy-start | bytes 2359300
  28.2 21.2 %collective-permute-start.14 = (bf16[128,1536]{1,0:T(8,128)(2,1)}, bf16[128,1536]{1,0:T(8,128)(2,1)}, u32[]{:S(2)}, u32[]{:S(2)}) collective-permute-start(bf16[128,1536]{1,0:T(8,128)(2,1)} %slice.39), channel_id=1, source_target_pairs={{0,16},{8,24},{16,0},{24,8},{1,17},{9,25},{17,1},{25,9},{2,18},{10... | collective-permute-start | bytes 1179656 | tf_op jit(solution)/shard_map/ppermute | solution.py:269
  34.6 14.9 %collective-permute-start.15 = (bf16[128,1536]{1,0:T(8,128)(2,1)}, bf16[128,1536]{1,0:T(8,128)(2,1)}, u32[]{:S(2)}, u32[]{:S(2)}) collective-permute-start(bf16[128,1536]{1,0:T(8,128)(2,1)} %slice.40), channel_id=1, source_target_pairs={{0,8},{8,0},{16,24},{24,16},{1,9},{9,1},{17,25},{25,17},{2,10},{10... | collective-permute-start | bytes 1179656 | tf_op jit(solution)/shard_map/ppermute | solution.py:269
  36.1 9.3 %copy-start.22 = (bf16[128,1024]{1,0:T(8,128)(2,1)}, bf16[128,1024]{1,0:T(8,128)(2,1)S(1)}, u32[]{:S(2)}) copy-start(bf16[128,1024]{1,0:T(8,128)(2,1)S(1)} %collective-permute-done.1.refs_2_) | copy-start | bytes 786436
  36.1 9.3 %collective-permute-start.8 = (bf16[128,1024]{1,0:T(8,128)(2,1)S(1)}, bf16[128,1024]{1,0:T(8,128)(2,1)S(1)}, u32[]{:S(2)}, u32[]{:S(2)}) collective-permute-start(bf16[128,1024]{1,0:T(8,128)(2,1)S(1)} %collective-permute-done.7.refs_9_), channel_id=1, source_target_pairs={{0,2},{2,0},{4,6},{6,4},{1,3},{3,1},{5,7},{7,5},{8,10},{10,8},{12,... | collective-permute-start | bytes 786440 | tf_op jit(solution)/shard_map/ppermute | solution.py:269
  36.9 11.9 %copy-start.23 = (bf16[128,1024]{1,0:T(8,128)(2,1)}, bf16[128,1024]{1,0:T(8,128)(2,1)S(1)}, u32[]{:S(2)}) copy-start(bf16[128,1024]{1,0:T(8,128)(2,1)S(1)} %collective-permute-done.refs_1_) | copy-start | bytes 786436
  36.9 11.9 %collective-permute-start.10 = (bf16[128,1024]{1,0:T(8,128)(2,1)S(1)}, bf16[128,1024]{1,0:T(8,128)(2,1)S(1)}, u32[]{:S(2)}, u32[]{:S(2)}) collective-permute-start(bf16[128,1024]{1,0:T(8,128)(2,1)S(1)} %collective-permute-done.7.refs_9_), channel_id=1, source_target_pairs={{0,1},{1,0},{2,3},{3,2},{4,5},{5,4},{6,7},{7,6},{8,9},{9,8},{10,11... | collective-permute-start | bytes 786440 | tf_op jit(solution)/shard_map/ppermute | solution.py:269
  37.5 11.4 %copy-start.25 = (bf16[128,1024]{1,0:T(8,128)(2,1)}, bf16[128,1024]{1,0:T(8,128)(2,1)S(1)}, u32[]{:S(2)}) copy-start(bf16[128,1024]{1,0:T(8,128)(2,1)S(1)} %collective-permute-done.6.refs_8_) | copy-start | bytes 786436
  37.5 11.3 %collective-permute-start.2 = (bf16[128,1024]{1,0:T(8,128)(2,1)S(1)}, bf16[128,1024]{1,0:T(8,128)(2,1)}, u32[]{:S(2)}, u32[]{:S(2)}) collective-permute-start(bf16[128,1024]{1,0:T(8,128)(2,1)S(1)} %collective-permute-done.1.refs_2_), channel_id=1, source_target_pairs={{0,2},{2,0},{4,6},{6,4},{1,3},{3,1},{5,7},{7,5},{8,10},{10,8},{12,... | collective-permute-start | bytes 786440 | tf_op jit(solution)/shard_map/ppermute | solution.py:269
  45.4 6.6 %collective-permute-start.4 = (bf16[128,1024]{1,0:T(8,128)(2,1)S(1)}, bf16[128,1024]{1,0:T(8,128)(2,1)S(1)}, u32[]{:S(2)}, u32[]{:S(2)}) collective-permute-start(bf16[128,1024]{1,0:T(8,128)(2,1)S(1)} %collective-permute-done.1.refs_2_), channel_id=1, source_target_pairs={{0,1},{1,0},{2,3},{3,2},{4,5},{5,4},{6,7},{7,6},{8,9},{9,8},{10,11... | collective-permute-start | bytes 786440 | tf_op jit(solution)/shard_map/ppermute | solution.py:269
  48.8 3.2 %collective-permute-start.3 = (bf16[128,1024]{1,0:T(8,128)(2,1)S(1)}, bf16[128,1024]{1,0:T(8,128)(2,1)S(1)}, u32[]{:S(2)}, u32[]{:S(2)}) collective-permute-start(bf16[128,1024]{1,0:T(8,128)(2,1)S(1)} %collective-permute-done.refs_1_), channel_id=1, source_target_pairs={{0,1},{1,0},{2,3},{3,2},{4,5},{5,4},{6,7},{7,6},{8,9},{9,8},{10,11... | collective-permute-start | bytes 786440 | tf_op jit(solution)/shard_map/ppermute | solution.py:269
  48.8 3.2 %collective-permute-start.9 = (bf16[128,1024]{1,0:T(8,128)(2,1)S(1)}, bf16[128,1024]{1,0:T(8,128)(2,1)S(1)}, u32[]{:S(2)}, u32[]{:S(2)}) collective-permute-start(bf16[128,1024]{1,0:T(8,128)(2,1)S(1)} %collective-permute-done.6.refs_8_), channel_id=1, source_target_pairs={{0,1},{1,0},{2,3},{3,2},{4,5},{5,4},{6,7},{7,6},{8,9},{9,8},{10,11... | collective-permute-start | bytes 786440 | tf_op jit(solution)/shard_map/ppermute | solution.py:269
  49.4 2.6 %collective-permute-start.11 = (bf16[128,1024]{1,0:T(8,128)(2,1)S(1)}, bf16[128,1024]{1,0:T(8,128)(2,1)S(1)}, u32[]{:S(2)}, u32[]{:S(2)}) collective-permute-start(bf16[128,1024]{1,0:T(8,128)(2,1)S(1)} %collective-permute-done.8.refs_10_), channel_id=1, source_target_pairs={{0,1},{1,0},{2,3},{3,2},{4,5},{5,4},{6,7},{7,6},{8,9},{9,8},{10,11... | collective-permute-start | bytes 786440 | tf_op jit(solution)/shard_map/ppermute | solution.py:269
  49.5 2.6 %collective-permute-start.5 = (bf16[128,1024]{1,0:T(8,128)(2,1)}, bf16[128,1024]{1,0:T(8,128)(2,1)S(1)}, u32[]{:S(2)}, u32[]{:S(2)}) collective-permute-start(bf16[128,1024]{1,0:T(8,128)(2,1)} %collective-permute-done.2.refs_3_), channel_id=1, source_target_pairs={{0,1},{1,0},{2,3},{3,2},{4,5},{5,4},{6,7},{7,6},{8,9},{9,8},{10,11... | collective-permute-start | bytes 786440 | tf_op jit(solution)/shard_map/ppermute | solution.py:269
  53.3 22.7 %copy-start.5 = (s32[3]{0:T(128)S(1)}, s32[3]{0:T(128)}, u32[]{:S(2)}) copy-start(s32[3]{0:T(128)} %pad_add_fusion.place_ref) | copy-start | bytes 40
  72.3 3.6 %collective-permute-start.16 = (bf16[4,128,1024]{2,1,0:T(8,128)(2,1)}, bf16[4,128,1024]{2,1,0:T(8,128)(2,1)S(1)}, u32[]{:S(2)}, u32[]{:S(2)}) collective-permute-start(bf16[4,128,1024]{2,1,0:T(8,128)(2,1)} %get-tuple-element.63), channel_id=1, source_target_pairs={{0,1},{1,0},{2,3},{3,2},{4,5},{5,4},{6,7},{7,6},{8,9},{9,8},{10,11... | collective-permute-start | bytes 3145736 | tf_op jit(solution)/shard_map/ppermute | solution.py:269
  72.5 25.0 %collective-permute-start.21 = (bf16[272,1152]{1,0:T(8,128)(2,1)}, bf16[272,1152]{1,0:T(8,128)(2,1)S(1)}, u32[]{:S(2)}, u32[]{:S(2)}) collective-permute-start(bf16[272,1152]{1,0:T(8,128)(2,1)} %get-tuple-element.69), channel_id=1, source_target_pairs={{0,8},{8,0},{16,24},{24,16},{1,9},{9,1},{17,25},{25,17},{2,10},{10... | collective-permute-start | bytes 1880072 | tf_op jit(solution)/shard_map/ppermute | solution.py:269
  74.0 29.8 %collective-permute-start.22 = (bf16[272,1152]{1,0:T(8,128)(2,1)}, bf16[272,1152]{1,0:T(8,128)(2,1)S(1)}, u32[]{:S(2)}, u32[]{:S(2)}) collective-permute-start(bf16[272,1152]{1,0:T(8,128)(2,1)} %get-tuple-element.70), channel_id=1, source_target_pairs={{0,16},{8,24},{16,0},{24,8},{1,17},{9,25},{17,1},{25,9},{2,18},{10... | collective-permute-start | bytes 1880072 | tf_op jit(solution)/shard_map/ppermute | solution.py:269
  75.4 28.4 %collective-permute-start.23 = (bf16[272,1152]{1,0:T(8,128)(2,1)}, bf16[272,1152]{1,0:T(8,128)(2,1)S(1)}, u32[]{:S(2)}, u32[]{:S(2)}) collective-permute-start(bf16[272,1152]{1,0:T(8,128)(2,1)} %get-tuple-element.71), channel_id=1, source_target_pairs={{0,24},{8,16},{16,8},{24,0},{1,25},{9,17},{17,9},{25,1},{2,26},{10... | collective-permute-start | bytes 1880072 | tf_op jit(solution)/shard_map/ppermute | solution.py:269
  79.1 24.7 %collective-permute-start.17 = (bf16[128,1024]{1,0:T(8,128)(2,1)S(1)}, bf16[128,1024]{1,0:T(8,128)(2,1)S(1)}, u32[]{:S(2)}, u32[]{:S(2)}) collective-permute-start(bf16[128,1024]{1,0:T(8,128)(2,1)S(1)} %get-tuple-element.65), channel_id=1, source_target_pairs={{0,2},{2,0},{4,6},{6,4},{1,3},{3,1},{5,7},{7,5},{8,10},{10,8},{12,... | collective-permute-start | bytes 786440 | tf_op jit(solution)/shard_map/ppermute | solution.py:269
  80.8 23.0 %collective-permute-start.18 = (bf16[128,1024]{1,0:T(8,128)(2,1)S(1)}, bf16[128,1024]{1,0:T(8,128)(2,1)S(1)}, u32[]{:S(2)}, u32[]{:S(2)}) collective-permute-start(bf16[128,1024]{1,0:T(8,128)(2,1)S(1)} %get-tuple-element.66), channel_id=1, source_target_pairs={{0,4},{2,6},{4,0},{6,2},{1,5},{3,7},{5,1},{7,3},{8,12},{10,14},{12... | collective-permute-start | bytes 786440 | tf_op jit(solution)/shard_map/ppermute | solution.py:269
  85.4 18.4 %copy-start.6 = (s32[3]{0:T(128)S(1)}, s32[3]{0:T(128)}, u32[]{:S(2)}) copy-start(s32[3]{0:T(128)} %pad_add_fusion.place_ref) | copy-start | bytes 40
  97.5 8.3 %collective-permute-start.24 = (bf16[4,128,1024]{2,1,0:T(8,128)(2,1)}, bf16[4,128,1024]{2,1,0:T(8,128)(2,1)S(1)}, u32[]{:S(2)}, u32[]{:S(2)}) collective-permute-start(bf16[4,128,1024]{2,1,0:T(8,128)(2,1)} %get-tuple-element.80), channel_id=1, source_target_pairs={{0,1},{1,0},{2,3},{3,2},{4,5},{5,4},{6,7},{7,6},{8,9},{9,8},{10,11... | collective-permute-start | bytes 3145736 | tf_op jit(solution)/shard_map/ppermute | solution.py:269
  107.2 14.2 %collective-permute-start.25 = (bf16[2,128,1024]{2,1,0:T(8,128)(2,1)S(1)}, bf16[2,128,1024]{2,1,0:T(8,128)(2,1)S(1)}, u32[]{:S(2)}, u32[]{:S(2)}) collective-permute-start(bf16[2,128,1024]{2,1,0:T(8,128)(2,1)S(1)} %get-tuple-element.82), channel_id=1, source_target_pairs={{0,2},{2,0},{4,6},{6,4},{1,3},{3,1},{5,7},{7,5},{8,10},{10,8},{12,... | collective-permute-start | bytes 1572872 | tf_op jit(solution)/shard_map/ppermute | solution.py:269
  109.3 19.6 %collective-permute-start.28 = (bf16[272,384]{1,0:T(8,128)(2,1)S(1)}, bf16[272,384]{1,0:T(8,128)(2,1)S(1)}, u32[]{:S(2)}, u32[]{:S(2)}) collective-permute-start(bf16[272,384]{1,0:T(8,128)(2,1)S(1)} %copy-done.35), channel_id=1, source_target_pairs={{0,8},{8,0},{16,24},{24,16},{1,9},{9,1},{17,25},{25,17},{2,10},{10... | collective-permute-start | bytes 626696 | tf_op jit(solution)/shard_map/ppermute | solution.py:269
  110.1 18.8 %collective-permute-start.29 = (bf16[272,384]{1,0:T(8,128)(2,1)S(1)}, bf16[272,384]{1,0:T(8,128)(2,1)S(1)}, u32[]{:S(2)}, u32[]{:S(2)}) collective-permute-start(bf16[272,384]{1,0:T(8,128)(2,1)S(1)} %copy-done.34), channel_id=1, source_target_pairs={{0,16},{8,24},{16,0},{24,8},{1,17},{9,25},{17,1},{25,9},{2,18},{10... | collective-permute-start | bytes 626696 | tf_op jit(solution)/shard_map/ppermute | solution.py:269
  111.3 17.5 %collective-permute-start.30 = (bf16[272,384]{1,0:T(8,128)(2,1)S(1)}, bf16[272,384]{1,0:T(8,128)(2,1)S(1)}, u32[]{:S(2)}, u32[]{:S(2)}) collective-permute-start(bf16[272,384]{1,0:T(8,128)(2,1)S(1)} %copy-done.33), channel_id=1, source_target_pairs={{0,24},{8,16},{16,8},{24,0},{1,25},{9,17},{17,9},{25,1},{2,26},{10... | collective-permute-start | bytes 626696 | tf_op jit(solution)/shard_map/ppermute | solution.py:269
  113.0 38.2 %collective-permute-start.19 = (bf16[128,1024]{1,0:T(8,128)(2,1)S(1)}, bf16[128,1024]{1,0:T(8,128)(2,1)S(1)}, u32[]{:S(2)}, u32[]{:S(2)}) collective-permute-start(bf16[128,1024]{1,0:T(8,128)(2,1)S(1)} %get-tuple-element.67), channel_id=1, source_target_pairs={{0,6},{2,4},{4,2},{6,0},{1,7},{3,5},{5,3},{7,1},{8,14},{10,12},{12... | collective-permute-start | bytes 786440 | tf_op jit(solution)/shard_map/ppermute | solution.py:269
  121.4 7.4 %copy-start.8 = (bf16[272,384]{1,0:T(8,128)(2,1)S(1)}, bf16[272,384]{1,0:T(8,128)(2,1)}, u32[]{:S(2)}) copy-start(bf16[272,384]{1,0:T(8,128)(2,1)} %get-tuple-element.83.refs_1_) | copy-start | bytes 626692
  121.6 29.2 %collective-permute-start.26 = (bf16[1,128,1024]{2,1,0:T(8,128)(2,1)S(1)}, bf16[1,128,1024]{2,1,0:T(8,128)(2,1)S(1)}, u32[]{:S(2)}, u32[]{:S(2)}) collective-permute-start(bf16[1,128,1024]{2,1,0:T(8,128)(2,1)S(1)} %slice.62), channel_id=1, source_target_pairs={{0,4},{2,6},{4,0},{6,2},{1,5},{3,7},{5,1},{7,3},{8,12},{10,14},{12... | collective-permute-start | bytes 786440 | tf_op jit(solution)/shard_map/ppermute | solution.py:269
  129.5 21.7 %copy-start.4 = (f32[128,1024]{1,0:T(8,128)S(1)}, f32[128,1024]{1,0:T(8,128)}, u32[]{:S(2)}) copy-start(f32[128,1024]{1,0:T(8,128)} %copy-done.3) | copy-start | bytes 1572868
  129.6 21.7 %copy-start.15 = (bf16[256,1024]{1,0:T(8,128)(2,1)S(1)}, bf16[256,1024]{1,0:T(8,128)(2,1)}, u32[]{:S(2)}) copy-start(bf16[256,1024]{1,0:T(8,128)(2,1)} %refs_7_.3) | copy-start | bytes 1572868
  129.6 21.7 %copy-start.20 = (f32[1024]{0:T(1024)S(1)}, f32[1024]{0:T(1024)}, u32[]{:S(2)}) copy-start(f32[1024]{0:T(1024)} %param.27) | copy-start | bytes 12292
  129.6 21.7 %copy-start.21 = (f32[1024]{0:T(1024)S(1)}, f32[1024]{0:T(1024)}, u32[]{:S(2)}) copy-start(f32[1024]{0:T(1024)} %param.23) | copy-start | bytes 12292
  129.6 22.2 %collective-permute-start.31 = (bf16[80,1536]{1,0:T(8,128)(2,1)S(1)}, bf16[80,1536]{1,0:T(8,128)(2,1)S(1)}, u32[]{:S(2)}, u32[]{:S(2)}) collective-permute-start(bf16[80,1536]{1,0:T(8,128)(2,1)S(1)} %get-tuple-element.92), channel_id=1, source_target_pairs={{0,2},{2,0},{4,6},{6,4},{1,3},{3,1},{5,7},{7,5},{8,10},{10,8},{12,... | collective-permute-start | bytes 737288 | tf_op jit(solution)/shard_map/ppermute | solution.py:269
  132.6 23.5 %collective-permute-start.32 = (bf16[80,1536]{1,0:T(8,128)(2,1)S(1)}, bf16[80,1536]{1,0:T(8,128)(2,1)S(1)}, u32[]{:S(2)}, u32[]{:S(2)}) collective-permute-start(bf16[80,1536]{1,0:T(8,128)(2,1)S(1)} %get-tuple-element.93), channel_id=1, source_target_pairs={{0,4},{2,6},{4,0},{6,2},{1,5},{3,7},{5,1},{7,3},{8,12},{10,14},{12... | collective-permute-start | bytes 737288 | tf_op jit(solution)/shard_map/ppermute | solution.py:269
  133.3 22.8 %collective-permute-start.33 = (bf16[80,1536]{1,0:T(8,128)(2,1)S(1)}, bf16[80,1536]{1,0:T(8,128)(2,1)S(1)}, u32[]{:S(2)}, u32[]{:S(2)}) collective-permute-start(bf16[80,1536]{1,0:T(8,128)(2,1)S(1)} %get-tuple-element.94), channel_id=1, source_target_pairs={{0,6},{2,4},{4,2},{6,0},{1,7},{3,5},{5,3},{7,1},{8,14},{10,12},{12... | collective-permute-start | bytes 737288 | tf_op jit(solution)/shard_map/ppermute | solution.py:269
  158.2 1.2 collective-permute-start.34
  158.3 3.3 %collective-permute-start.27 = (f32[128,1024]{1,0:T(8,128)S(1)}, f32[128,1024]{1,0:T(8,128)S(1)}, u32[]{:S(2)}, u32[]{:S(2)}) collective-permute-start(f32[128,1024]{1,0:T(8,128)S(1)} %get-tuple-element.112), channel_id=1, source_target_pairs={{0,1},{1,0},{2,3},{3,2},{4,5},{5,4},{6,7},{7,6},{8,9},{9,8},{10,11... | collective-permute-start | bytes 1572872 | tf_op jit(solution)/shard_map/ppermute | solution.py:269
  158.8 1.9 %collective-permute-start.20 = (bf16[128,1024]{1,0:T(8,128)(2,1)S(1)}, bf16[128,1024]{1,0:T(8,128)(2,1)S(1)}, u32[]{:S(2)}, u32[]{:S(2)}) collective-permute-start(bf16[128,1024]{1,0:T(8,128)(2,1)S(1)} %get-tuple-element.108), channel_id=1, source_target_pairs={{0,1},{1,0},{2,3},{3,2},{4,5},{5,4},{6,7},{7,6},{8,9},{9,8},{10,11... | collective-permute-start | bytes 786440 | tf_op jit(solution)/shard_map/ppermute | solution.py:269
  (24 other events, 77.8 us)
